TPU v7x, 32 devices: a whole 2x2x4 slice. The times are simulated.
32 devices in a mesh: dp: 8 (over y, x, core), fsdp: 4 (over z).
Axes of the slice: x: 2, y: 2, z: 4, core: 2. Of those that a mesh axis runs over, the one named last changes fastest.
Arguments:
- token_ids: int32 [64, 512], P(('dp', 'fsdp')), may hold values from 0 to 50303
- true_mask: int32 [64, 512], P(('dp', 'fsdp')), may hold values from 0 to 1, as said below
- keep_layer: int32 [64], P(('dp', 'fsdp')), may hold values 0 or 1
- picked: int32 [64, 64], P(('dp', 'fsdp')), may hold values from 0 to 511, as said below
- teacher_hidden: bfloat16 [64, 512, 768], P(('dp', 'fsdp')), may hold values from -8 to 8
- teacher_logits: bfloat16 [64, 64, 50304], P(('dp', 'fsdp')), may hold values from -12 to 12
- embed_table: float32 [50304, 768], P(('dp', 'fsdp'))
- pos_table: float32 [512, 768], P(None, ('dp', 'fsdp')), may hold values from -0.21875 to 0.21875
- query_key_value_weight: float32 [768, 2304], P(('dp', 'fsdp')), may hold values from -0.21875 to 0.21875
- output_weight: float32 [768, 768], P(('dp', 'fsdp')), may hold values from -0.875 to 0.875
- up_weight: float32 [768, 3072], P(('dp', 'fsdp')), may hold values from -0.21875 to 0.21875
- down_weight: float32 [3072, 768], P(('dp', 'fsdp')), may hold values from -0.109375 to 0.109375
- gains_biases: float32 [14, 768], P(None, ('dp', 'fsdp'))
- first_embed: float32 [50304, 768], P(('dp', 'fsdp')), may hold values from -4.5776367e-05 to 4.5776367e-05
- first_pos: float32 [512, 768], P(None, ('dp', 'fsdp')), may hold values from -4.5776367e-05 to 4.5776367e-05
- first_qkv: float32 [768, 2304], P(('dp', 'fsdp')), may hold values from -4.5776367e-05 to 4.5776367e-05
- first_out: float32 [768, 768], P(('dp', 'fsdp')), may hold values from -4.5776367e-05 to 4.5776367e-05
- first_up: float32 [768, 3072], P(('dp', 'fsdp')), may hold values from -4.5776367e-05 to 4.5776367e-05
- first_down: float32 [3072, 768], P(('dp', 'fsdp')), may hold values from -4.5776367e-05 to 4.5776367e-05
- first_gains: float32 [14, 768], P(None, ('dp', 'fsdp')), may hold values from -0.00018310547 to 0.00018310547
- second_embed: float32 [50304, 768], P(('dp', 'fsdp')), may hold values from 5.421191e-12 to 2.1684763e-11
- second_pos: float32 [512, 768], P(None, ('dp', 'fsdp')), may hold values from 5.421191e-12 to 2.1684763e-11
- second_qkv: float32 [768, 2304], P(('dp', 'fsdp')), may hold values from 5.421191e-12 to 2.1684763e-11
- second_out: float32 [768, 768], P(('dp', 'fsdp')), may hold values from 5.421191e-12 to 2.1684763e-11
- second_up: float32 [768, 3072], P(('dp', 'fsdp')), may hold values from 5.421191e-12 to 2.1684763e-11
- second_down: float32 [3072, 768], P(('dp', 'fsdp')), may hold values from 5.421191e-12 to 2.1684763e-11
- second_gains: float32 [14, 768], P(None, ('dp', 'fsdp')), may hold values from 8.673905e-11 to 3.469562e-10
Outputs:
- loss_sum: float32 [], replicated
- token_count: float32 [], replicated
- grad_norm: float32 [], replicated
- new_embed: float32 [50304, 768], P(('dp', 'fsdp'))
- new_pos: float32 [512, 768], P(None, ('dp', 'fsdp'))
- new_qkv: float32 [768, 2304], P(('dp', 'fsdp'))
- new_out: float32 [768, 768], P(('dp', 'fsdp'))
- new_up: float32 [768, 3072], P(('dp', 'fsdp'))
- new_down: float32 [3072, 768], P(('dp', 'fsdp'))
- new_gains: float32 [14, 768], P(None, ('dp', 'fsdp'))
- moment_embed: float32 [50304, 768], P(('dp', 'fsdp'))
- moment_pos: float32 [512, 768], P(None, ('dp', 'fsdp'))
- moment_qkv: float32 [768, 2304], P(('dp', 'fsdp'))
- moment_out: float32 [768, 768], P(('dp', 'fsdp'))
- moment_up: float32 [768, 3072], P(('dp', 'fsdp'))
- moment_down: float32 [3072, 768], P(('dp', 'fsdp'))
- moment_gains: float32 [14, 768], P(None, ('dp', 'fsdp'))
- square_embed: float32 [50304, 768], P(('dp', 'fsdp'))
- square_pos: float32 [512, 768], P(None, ('dp', 'fsdp'))
- square_qkv: float32 [768, 2304], P(('dp', 'fsdp'))
- square_out: float32 [768, 768], P(('dp', 'fsdp'))
- square_up: float32 [768, 3072], P(('dp', 'fsdp'))
- square_down: float32 [3072, 768], P(('dp', 'fsdp'))
- square_gains: float32 [14, 768], P(None, ('dp', 'fsdp'))
- matrix_norms: float32 [2, 7], replicated
Inputs may be any that keep to these rules, and one draw needn't show every extreme that they name: `true_mask`: in each sequence the true tokens are the first ones, at least one. `picked`: each entry is a position of a true token of its sequence.
All inputs are finite; a program needn't handle non-finite values. No bound on the sum of `keep_layer` on one device may be relied on, other than what follows from the above.
Results may differ from a plain program's by a relative error of at most 0.0098.
The roundings to bfloat16 on the way count: a program that leaves them out, or rounds other values in their place, can miss the bound.
Values may be sent and summed in bfloat16 or wider, within the bound.
No kernel may reach another device: no remote copies, remote signals or barrier semaphores. Data moves between devices by JAX's collectives and lax.ppermute only.
A program may use at most 832 MiB of HBM per device.

v0:
```python
import functools

import jax
import jax.numpy as jnp
from jax import lax
from jax.experimental import pallas as pl
from jax.experimental.pallas import tpu as pltpu
from jax.sharding import Mesh
from jax.sharding import PartitionSpec as P

H = 12
HD = 64
STEP = 10


NORM_EPS = 1e-05
CLIP_NORM = 0.5
BETA_ONE = 0.9
BETA_TWO = 0.999
ADAM_EPS = 1e-06
DECAY_RATE = 0.01
LEARN_RATE = 0.3
MASKED_SCORE = -1e30

SPLIT = ("plane", "pair")
AXES = ("plane", "pair", "fsdp")
VMEM = 60 * 2**20
NO_COST = pl.CostEstimate(flops=0, bytes_accessed=0, transcendentals=0)


def normal_cdf(values):
    return 0.5 + 0.5 * lax.erf(values * 0.5**0.5)


def dense(left_op, right_op):
    return jnp.dot(left_op, right_op, preferred_element_type=jnp.float32)


def dense_tn(left_op, right_op):
    return lax.dot_general(
        left_op, right_op, (((0,), (0,)), ((), ())), preferred_element_type=jnp.float32
    )


def dense_nt(left_op, right_op):
    return lax.dot_general(
        left_op, right_op, (((1,), (1,)), ((), ())), preferred_element_type=jnp.float32
    )


def pair_lanes(shape, member):
    lane = lax.broadcasted_iota(jnp.int32, shape, 1)
    return (lane >= HD) if member else (lane < HD)


def softmax_rows(query_rows, key_rows, length):
    scores = dense_nt(query_rows, key_rows)
    spot = lax.broadcasted_iota(jnp.int32, (1, scores.shape[1]), 1)
    scores = scores + jnp.where(spot < length, 0.0, MASKED_SCORE)
    exponent = jnp.exp(scores - jnp.max(scores, axis=1, keepdims=True))
    return exponent * (1.0 / jnp.sum(exponent, axis=1, keepdims=True))


def softmax_columns(key_rows, query_rows, length):
    scores = dense_nt(key_rows, query_rows)
    spot = lax.broadcasted_iota(jnp.int32, (scores.shape[0], 1), 0)
    scores = scores + jnp.where(spot < length, 0.0, MASKED_SCORE)
    exponent = jnp.exp(scores - jnp.max(scores, axis=0, keepdims=True))
    return exponent * (1.0 / jnp.sum(exponent, axis=0, keepdims=True))


def row_spans(seq_len):
    half = seq_len // 2
    return ((0, half), (half, seq_len))


def mix_kernel(length_ref, query_ref, key_ref, value_ref, mixed_ref):
    seq_len = query_ref.shape[0]
    length = length_ref[pl.program_id(0)]

    for low, high in row_spans(seq_len):

        @pl.when((length > low) & (length <= high))
        def _():
            step = high
            keys, values = key_ref[0:high, :], value_ref[0:high, :]
            for row in range(0, high, step):
                queries = query_ref[row : row + step, :] * 0.125
                parts = []
                for member in (0, 1):
                    lanes = pair_lanes(queries.shape, member)
                    chance = softmax_rows(
                        jnp.where(lanes, queries, jnp.zeros_like(queries)), keys, length
                    )
                    parts.append(dense(chance.astype(jnp.bfloat16), values))
                mixed_ref[row : row + step, :] = jnp.where(
                    pair_lanes(parts[0].shape, 1), parts[1], parts[0]
                ).astype(jnp.bfloat16)
            if high < seq_len:
                mixed_ref[high:, :] = jnp.zeros((seq_len - high, 2 * HD), jnp.bfloat16)

    @pl.when(length == 0)
    def _():
        mixed_ref[...] = jnp.zeros_like(mixed_ref)


def unmix_kernel(
    length_ref, query_ref, key_ref, value_ref, grad_ref, query_out, key_out, value_out
):
    seq_len = query_ref.shape[0]
    length = length_ref[pl.program_id(0)]
    outs = (query_out, key_out, value_out)

    for low, high in row_spans(seq_len):

        @pl.when((length > low) & (length <= high))
        def _():
            step = high
            keys, values = key_ref[0:high, :], value_ref[0:high, :]
            key_total, value_total = None, None
            for row in range(0, high, step):
                plain = query_ref[row : row + step, :]
                queries = plain * 0.125
                grads = grad_ref[row : row + step, :]
                parts = []
                for member in (0, 1):
                    lanes = pair_lanes(queries.shape, member)
                    zero = jnp.zeros_like(queries)
                    chance = softmax_columns(keys, jnp.where(lanes, queries, zero), length)
                    slope = dense_nt(values, jnp.where(lanes, grads, zero))
                    slope = chance * (slope - jnp.sum(slope * chance, axis=0, keepdims=True))
                    slope = slope.astype(jnp.bfloat16)
                    parts.append(
                        (
                            dense_tn(slope, keys),
                            dense(slope, plain),
                            dense(chance.astype(jnp.bfloat16), grads),
                        )
                    )
                query_part, key_part, value_part = [
                    jnp.where(pair_lanes(first.shape, 1), second, first)
                    for first, second in zip(*parts)
                ]
                query_out[row : row + step, :] = (query_part * 0.125).astype(jnp.bfloat16)
                key_total = key_part if key_total is None else key_total + key_part
                value_total = value_part if value_total is None else value_total + value_part
            key_out[0:high, :] = (key_total * 0.125).astype(jnp.bfloat16)
            value_out[0:high, :] = value_total.astype(jnp.bfloat16)
            if high < seq_len:
                for ref in outs:
                    ref[high:, :] = jnp.zeros((seq_len - high, 2 * HD), jnp.bfloat16)

    @pl.when(length == 0)
    def _():
        for ref in outs:
            ref[...] = jnp.zeros_like(ref)


def attend(lengths, packed, grad_mixed=None):
    seq_count = lengths.shape[0]
    seq_len = packed.shape[0] // seq_count
    pairs = H // 2

    def block(first):
        return pl.BlockSpec((seq_len, 2 * HD), lambda s, h, _: (s, first + h))

    out = jax.ShapeDtypeStruct((packed.shape[0], H * HD), jnp.bfloat16)
    forward = grad_mixed is None
    operands = (packed, packed, packed) + (() if forward else (grad_mixed,))
    return pl.pallas_call(
        mix_kernel if forward else unmix_kernel,
        out_shape=out if forward else (out, out, out),
        grid_spec=pltpu.PrefetchScalarGridSpec(
            num_scalar_prefetch=1,
            grid=(seq_count, pairs),
            in_specs=[block(0), block(pairs), block(2 * pairs)] + ([] if forward else [block(0)]),
            out_specs=block(0) if forward else (block(0),) * 3,
        ),
        compiler_params=pltpu.CompilerParams(vmem_limit_bytes=VMEM),
        cost_estimate=NO_COST,
    )(lengths, *operands)


def norm_parts(values):
    centered = values - jnp.mean(values, axis=1, keepdims=True)
    spread = lax.rsqrt(jnp.mean(centered * centered, axis=1, keepdims=True) + NORM_EPS)
    return centered * spread, spread


def norm_back(grads, unit_rows, spread, gain_row):
    scaled = grads * gain_row
    inner = jnp.mean(scaled * unit_rows, axis=1, keepdims=True)
    rows = spread * (scaled - jnp.mean(scaled, axis=1, keepdims=True) - unit_rows * inner)
    return rows, eight_rows(grads * unit_rows), eight_rows(grads)


def eight_rows(values):
    return jnp.sum(values.reshape(-1, 8, values.shape[1]), axis=0)


def picks_hot(picked_ref, first_row, rows):
    spot = lax.broadcasted_iota(jnp.int32, (picked_ref.shape[0], rows), 1) + first_row
    return (picked_ref[...] == spot).astype(jnp.bfloat16)


def enter_kernel(
    length_ref, token_ref, place_ref, vector_ref, weight_ref, embedded_ref, input_ref, low_ref, packed_ref
):
    block, seq = pl.program_id(0), pl.program_id(1)
    rows = token_ref.shape[0]
    vectors = vector_ref[...].astype(jnp.float32).T
    embedded = token_ref[...] + place_ref[...].astype(jnp.float32).T
    embedded_ref[...] = embedded
    inputs = norm_parts(embedded)[0] * vectors[0:1] + vectors[1:2]
    input_ref[...] = inputs
    low = inputs.astype(jnp.bfloat16)
    low_ref[...] = low

    @pl.when(length_ref[seq] > block * rows)
    def _():
        width = low.shape[1]
        for part, bias in enumerate((vectors[2:3], None, vectors[3:4])):
            columns = slice(part * width, (part + 1) * width)
            values = dense(low, weight_ref[:, columns])
            if bias is not None:
                values = values + bias
            packed_ref[:, columns] = values.astype(jnp.bfloat16)


def feed_kernel(
    length_ref,
    true_ref,
    mixed_ref,
    input_ref,
    teacher_ref,
    picked_ref,
    vector_ref,
    bias_ref,
    out_ref,
    up_ref,
    down_ref,
    joined_one_ref,
    normed_ref,
    slope_ref,
    active_ref,
    joined_two_ref,
    grad_ref,
    chosen_ref,
    loss_ref,
    final_ref,
):
    seq, block = pl.program_id(0), pl.program_id(1)
    rows, width = mixed_ref.shape
    alive = length_ref[seq] > block * rows
    final_ref[...] = input_ref[...]

    @pl.when(alive)
    def _():
        vectors = vector_ref[...].astype(jnp.float32).T
        joined = input_ref[...] + (dense(mixed_ref[...], out_ref[...]) + vectors[4:5])
        joined_one_ref[...] = joined
        normed = norm_parts(joined)[0] * vectors[5:6] + vectors[6:7]
        low = normed.astype(jnp.bfloat16)
        normed_ref[...] = low
        fed = None
        for column in range(0, up_ref.shape[1], width):
            columns = slice(column, column + width)
            hidden = dense(low, up_ref[:, columns]) + bias_ref[:, columns]
            share = normal_cdf(hidden)
            density = jnp.exp(-0.5 * hidden * hidden) * (2.0 * jnp.pi) ** -0.5
            slope_ref[:, columns] = (share + hidden * density).astype(jnp.bfloat16)
            active = (hidden * share).astype(jnp.bfloat16)
            active_ref[:, columns] = active
            part = dense(active, down_ref[:, columns])
            fed = part if fed is None else fed + part
        joined = normed + (fed + vectors[7:8])
        joined_two_ref[...] = joined
        final_ref[...] = norm_parts(joined)[0] * vectors[8:9] + vectors[9:10]

    @pl.when(jnp.logical_not(alive))
    def _():
        normed_ref[...] = jnp.zeros_like(normed_ref)
        active_ref[...] = jnp.zeros_like(active_ref)

    final = final_ref[...]
    row = lax.broadcasted_iota(jnp.int32, final.shape, 0) + block * rows
    gap = jnp.where(row < true_ref[seq], final - teacher_ref[...].astype(jnp.float32), 0.0)
    grad_ref[...] = 2.0 * gap
    hot = picks_hot(picked_ref, block * rows, rows)
    chosen = dense(hot, final.astype(jnp.bfloat16)).astype(jnp.bfloat16)

    @pl.when(block == 0)
    def _():
        chosen_ref[...] = chosen

    @pl.when(block > 0)
    def _():
        chosen_ref[...] += chosen

    @pl.when((block == 0) & (seq == 0))
    def _():
        loss_ref[...] = jnp.zeros_like(loss_ref)

    loss_ref[...] += eight_rows(gap * gap)


def unfeed_kernel(
    length_ref,
    grad_ref,
    head_ref,
    picked_ref,
    joined_one_ref,
    slope_ref,
    joined_two_ref,
    vector_ref,
    out_ref,
    up_ref,
    down_ref,
    final_ref,
    joined_out,
    mixed_out,
    attention_out,
    feed_out,
    hidden_out,
    sums_ref,
    hidden_sum_ref,
):
    seq, block = pl.program_id(0), pl.program_id(1)
    rows, width = grad_ref.shape
    alive = length_ref[seq] > block * rows
    head = jnp.sum(head_ref[...].astype(jnp.float32), axis=0)
    high = head.astype(jnp.bfloat16)
    rest = (head - high.astype(jnp.float32)).astype(jnp.bfloat16)
    hot = picks_hot(picked_ref, block * rows, rows)
    grads = grad_ref[...] + dense_tn(hot, high) + dense_tn(hot, rest)
    final_ref[...] = grads

    @pl.when((block == 0) & (seq == 0))
    def _():
        sums_ref[...] = jnp.zeros_like(sums_ref)
        hidden_sum_ref[...] = jnp.zeros_like(hidden_sum_ref)

    @pl.when(alive)
    def _():
        vectors = vector_ref[...].astype(jnp.float32).T
        unit_rows, spread = norm_parts(joined_two_ref[...])
        grad_two, gain_two, shift_two = norm_back(grads, unit_rows, spread, vectors[8:9])
        feed = grad_two.astype(jnp.bfloat16)
        feed_out[...] = feed
        back = grad_two
        for column in range(0, up_ref.shape[1], width):
            columns = slice(column, column + width)
            hidden = dense_nt(feed, down_ref[:, columns])
            hidden = (hidden * slope_ref[:, columns].astype(jnp.float32)).astype(jnp.bfloat16)
            hidden_out[:, columns] = hidden
            hidden_sum_ref[:, columns] += eight_rows(hidden.astype(jnp.float32))
            back = back + dense_nt(hidden, up_ref[:, columns])
        unit_rows, spread = norm_parts(joined_one_ref[...])
        grad_one, gain_one, shift_one = norm_back(back, unit_rows, spread, vectors[5:6])
        joined_out[...] = grad_one
        attention = grad_one.astype(jnp.bfloat16)
        attention_out[...] = attention
        mixed_out[...] = dense_nt(attention, out_ref[...]).astype(jnp.bfloat16)
        sums_ref[0] += eight_rows(attention.astype(jnp.float32))
        sums_ref[1] += gain_one
        sums_ref[2] += shift_one
        sums_ref[3] += eight_rows(feed.astype(jnp.float32))
        sums_ref[4] += gain_two
        sums_ref[5] += shift_two

    @pl.when(jnp.logical_not(alive))
    def _():
        for ref in (joined_out, mixed_out, attention_out, feed_out, hidden_out):
            ref[...] = jnp.zeros_like(ref)


def leave_kernel(
    length_ref,
    keep_ref,
    query_ref,
    key_ref,
    value_ref,
    joined_ref,
    final_ref,
    embedded_ref,
    vector_ref,
    weight_ref,
    rows_ref,
    place_ref,
    sums_ref,
    place_sum,
):
    block, seq = pl.program_id(0), pl.program_id(1)
    rows, width = joined_ref.shape
    alive = length_ref[seq] > block * rows
    vectors = vector_ref[...].astype(jnp.float32).T
    dropped = (keep_ref[seq] == 0).astype(jnp.float32)

    @pl.when((block == 0) & (seq == 0))
    def _():
        sums_ref[...] = jnp.zeros_like(sums_ref)

    @pl.when(seq == 0)
    def _():
        place_sum[...] = jnp.zeros_like(place_sum)

    def finish(grads):
        unit_rows, spread = norm_parts(embedded_ref[...])
        grads, gain, shift = norm_back(grads, unit_rows, spread, vectors[0:1])
        sums_ref[0] += gain
        sums_ref[1] += shift
        rows_ref[...] = grads.astype(jnp.bfloat16)
        place_sum[...] += grads

    @pl.when(alive)
    def _():
        grads = joined_ref[...]
        for part, ref in enumerate((query_ref, key_ref, value_ref)):
            grads = grads + dense_nt(ref[...], weight_ref[:, part * width : (part + 1) * width])
        sums_ref[2] += eight_rows(query_ref[...].astype(jnp.float32))
        sums_ref[3] += eight_rows(value_ref[...].astype(jnp.float32))
        finish(grads)

    @pl.when(jnp.logical_not(alive))
    def _():
        finish(final_ref[...] * dropped)

    @pl.when(seq == pl.num_programs(1) - 1)
    def _():
        place_ref[...] = place_sum[...].T.astype(jnp.bfloat16)


def deal_out(product, member_ref, kept_ref, given_ref, halves):
    halves[...] = product.reshape(halves.shape).astype(halves.dtype)
    member = member_ref[0]
    kept_ref[0] = halves[:, member]
    given_ref[0] = halves[:, 1 - member]


def early_kernel(
    member_ref,
    mixed_ref,
    attention_ref,
    normed_ref,
    hidden_ref,
    active_ref,
    feed_ref,
    kept_ref,
    given_ref,
    halves,
):
    place, blocks = pl.program_id(0), pl.num_programs(0) // 2
    cases = (
        (place == 0, mixed_ref, attention_ref),
        ((place > 0) & (place <= blocks), normed_ref, hidden_ref),
        (place > blocks, active_ref, feed_ref),
    )
    for wanted, left_ref, right_ref in cases:

        @pl.when(wanted)
        def _():
            product = dense_tn(left_ref[...], right_ref[...])
            deal_out(product, member_ref, kept_ref, given_ref, halves)


def late_kernel(
    member_ref,
    low_ref,
    query_ref,
    key_ref,
    value_ref,
    place_ref,
    sums_one_ref,
    sums_two_ref,
    up_ref,
    kept_ref,
    given_ref,
    halves,
    columns,
    vectors,
):
    for part, ref in enumerate((query_ref, key_ref, value_ref)):

        @pl.when(pl.program_id(0) == part)
        def _():
            product = dense_tn(low_ref[...], ref[...])
            deal_out(product, member_ref, kept_ref, given_ref, halves)

    @pl.when(pl.program_id(0) == 3)
    def _():
        vectors[...] = jnp.zeros_like(vectors)
        for row in range(4):
            vectors[row : row + 1, :] = jnp.sum(sums_two_ref[row], axis=0, keepdims=True)
        for row in range(6):
            vectors[4 + row : 5 + row, :] = jnp.sum(sums_one_ref[row], axis=0, keepdims=True)
        vectors[10:14, :] = up_ref[...]
        columns[...] = jnp.zeros_like(columns)
        width = place_ref.shape[1]
        columns[:, :width] = place_ref[...].astype(jnp.float32)
        columns[:, width : width + vectors.shape[0]] = vectors[...].T
        deal_out(columns[...], member_ref, kept_ref, given_ref, halves)


def head_grad_kernel(slope_ref, last_ref, chosen_ref, *grad_refs):
    count = len(grad_refs)
    for place, grad_ref in enumerate(grad_refs):
        source = last_ref if place == count - 2 else slope_ref

        @pl.when(pl.program_id(0) == place)
        def _():
            grad_ref[...] = dense_tn(source[0], chosen_ref[...]).astype(grad_ref.dtype)


def head_first_kernel(slope_ref, chosen_ref, grad_ref):
    grad_ref[...] = dense_tn(slope_ref[0], chosen_ref[...]).astype(grad_ref.dtype)


def row_kernel(kernel, prefetch, operands, outs, grid, scratch=()):
    return pl.pallas_call(
        kernel,
        out_shape=tuple(jax.ShapeDtypeStruct(shape, kind) for shape, kind, _, _ in outs),
        grid_spec=pltpu.PrefetchScalarGridSpec(
            num_scalar_prefetch=len(prefetch),
            grid=grid,
            in_specs=[pl.BlockSpec(block, where) for _, block, where in operands],
            out_specs=tuple(pl.BlockSpec(block, where) for _, _, block, where in outs),
            scratch_shapes=list(scratch),
        ),
        compiler_params=pltpu.CompilerParams(vmem_limit_bytes=VMEM),
        cost_estimate=NO_COST,
    )(*prefetch, *[array for array, _, _ in operands])


def parcel_kernel(own_rows, tiles, wide, source, parcel_ref, slots, sems):
    part, parts = pl.program_id(0), pl.num_programs(0)

    def first_tile(index):
        return jnp.minimum(own_rows * index // 128, tiles - wide)

    def fetch(index):
        lane = pl.multiple_of(first_tile(index) * 128, 128)
        slot = lax.rem(index, 2)
        return pltpu.make_async_copy(
            source.at[:, pl.ds(lane, wide * 128)],
            slots.at[slot, :, pl.ds(0, wide * 128)],
            sems.at[slot],
        )

    @pl.when(part == 0)
    def _():
        fetch(0).start()

    @pl.when(part + 1 < parts)
    def _():
        fetch(part + 1).start()

    fetch(part).wait()
    shift = own_rows * part - 128 * first_tile(part)
    slot, skip, turn = lax.rem(part, 2), shift // 128, lax.rem(128 - lax.rem(shift, 128), 128)
    n_pick, width = parcel_ref.shape[1:]
    lane = lax.broadcasted_iota(jnp.int32, (n_pick, 128), 1)

    def turned(tile):
        start = pl.multiple_of((tile + skip) * 128, 128)
        values = slots[slot, :, pl.ds(start, 128)].astype(jnp.float32)
        return pltpu.roll(values, turn, axis=1)

    low = turned(0)
    for tile in range(width // 128):
        high = turned(tile + 1)
        values = jnp.where(lane < 128 - lax.rem(shift, 128), low, high)
        values = jnp.where(lane + 128 * tile < own_rows, values, 0.0)
        parcel_ref[0, :, 128 * tile : 128 * (tile + 1)] = values.astype(jnp.bfloat16)
        low = high


def parcels_of(flat_teacher, own_rows, lanes, n_dev):
    n_pick, vocab = flat_teacher.shape
    tiles = vocab // 128
    wide = min(tiles, lanes // 128 + 1)
    return pl.pallas_call(
        functools.partial(parcel_kernel, own_rows, tiles, wide),
        out_shape=jax.ShapeDtypeStruct((n_dev, n_pick, lanes), jnp.bfloat16),
        grid=(n_dev,),
        in_specs=[pl.BlockSpec(memory_space=pl.ANY)],
        out_specs=pl.BlockSpec((1, n_pick, lanes), lambda r: (r, 0, 0)),
        scratch_shapes=[
            pltpu.VMEM((2, n_pick, (wide + 2) * 128), jnp.bfloat16),
            pltpu.SemaphoreType.DMA((2,)),
        ],
        compiler_params=pltpu.CompilerParams(vmem_limit_bytes=VMEM),
        cost_estimate=NO_COST,
    )(flat_teacher)


def head_kernel(steps, place_ref, chosen_ref, target_ref, *refs):
    tables = refs[:steps]
    before = refs[steps:-3]
    slope_ref, part_ref, loss_ref = refs[-3:]
    chosen = chosen_ref[...]
    senders, _, n_pick, _ = target_ref.shape
    total, loss = before[0][...] if before else None, None
    for step in range(steps):
        table = tables[step][...]
        width = table.shape[0]
        target = target_ref[:, place_ref[step]].reshape(senders * n_pick, -1)[:, :width]
        gap = dense_nt(chosen, table) - target.astype(jnp.float32)
        square = jnp.sum((gap * gap).reshape(-1, 8, width), axis=0)
        loss = square if loss is None else loss + square
        slope = (2.0 * gap).astype(jnp.bfloat16)
        slope_ref[step] = slope
        part = dense(slope, table)
        total = part if total is None else total + part
    part_ref[...] = total.astype(part_ref.dtype)

    @pl.when(pl.program_id(0) == 0)
    def _():
        loss_ref[...] = jnp.zeros_like(loss_ref)

    loss_ref[...] += loss


def head_products(places, all_chosen, targets, tables, before, part_type):
    n_dp, n_fs, n_pick, lanes = targets.shape
    row_width = all_chosen.shape[1]
    padded = tables[0].shape[0]
    rows, steps = 2 * n_pick, len(tables)
    whole = pl.BlockSpec((padded, row_width), lambda m, _: (0, 0))
    some = pl.BlockSpec((rows, row_width), lambda m, _: (m, 0))
    return pl.pallas_call(
        functools.partial(head_kernel, steps),
        out_shape=(
            jax.ShapeDtypeStruct((steps, n_dp * n_pick, padded), jnp.bfloat16),
            jax.ShapeDtypeStruct((n_dp * n_pick, row_width), part_type),
            jax.ShapeDtypeStruct((8, padded), jnp.float32),
        ),
        grid_spec=pltpu.PrefetchScalarGridSpec(
            num_scalar_prefetch=1,
            grid=(n_dp // 2,),
            in_specs=[
                some,
                pl.BlockSpec((2, n_fs, n_pick, lanes), lambda m, _: (m, 0, 0, 0)),
            ]
            + [whole] * steps
            + [some] * len(before),
            out_specs=(
                pl.BlockSpec((steps, rows, padded), lambda m, _: (0, m, 0)),
                some,
                pl.BlockSpec((8, padded), lambda m, _: (0, 0)),
            ),
        ),
        compiler_params=pltpu.CompilerParams(vmem_limit_bytes=VMEM),
        cost_estimate=NO_COST,
    )(places, all_chosen, targets, *tables, *before)


def sum_over_peers(part, axis):
    size, me = lax.axis_size(axis), lax.axis_index(axis)
    arrived = [lax.dynamic_index_in_dim(part, me, 1, False).astype(jnp.float32)]
    for apart in range(1, size):
        given = lax.dynamic_index_in_dim(part, me ^ apart, 1, False)
        got = lax.ppermute(given, axis, [(peer, peer ^ apart) for peer in range(size)])
        arrived.append(got.astype(jnp.float32))
    return sum(arrived)


def sum_in_pair(kept, given, pieces=1):
    swap = [(0, 1), (1, 0)]
    size = given.shape[0] // pieces
    got = [
        lax.ppermute(given[p * size : (p + 1) * size], "pair", swap) for p in range(pieces)
    ]
    got = got[0] if pieces == 1 else jnp.concatenate(got)
    return (kept.astype(jnp.float32) + got.astype(jnp.float32)).astype(jnp.bfloat16)


def sum_in_plane(part):
    part = sum_over_peers(part, "plane").astype(jnp.bfloat16)
    return part.reshape(part.shape[0], lax.axis_size("fsdp"), -1, part.shape[-1])


def sum_in_line(part):
    return sum_over_peers(part, "fsdp")


def route_plan(ids, live, own_rows, n_dev):
    place = jnp.arange(ids.shape[0])
    owner = ids // own_rows
    same = (ids[:, None] == ids[None, :]) & live[None, :]
    leader = jnp.min(jnp.where(same, place[None, :], ids.shape[0]), axis=1)
    first = live & (leader == place)
    before = (owner[:, None] == owner[None, :]) & (place[None, :] < leader[:, None])
    rank = jnp.sum(before & first[None, :], axis=1, dtype=jnp.int32)
    room = max(16, 1280 // n_dev)
    rounds = jnp.max(jnp.where(first, rank, 0)) // room + 1
    return ids, live, owner, first, rank, room, rounds, own_rows, n_dev


def slots_of(plan, turn):
    ids, live, owner, first, rank, room, rounds, own_rows, n_dev = plan
    here = live & (rank >= turn * room) & (rank < (turn + 1) * room)
    return jnp.where(here, owner * room + rank - turn * room, -1)


def exchange_wanted(plan, turn, axes):
    ids, live, owner, first, rank, room, rounds, own_rows, n_dev = plan
    slots = slots_of(plan, turn)
    local = jnp.where(first, ids - owner * own_rows + 1, 0)
    hit = jnp.arange(n_dev * room)[:, None] == slots[None, :]
    asked = jnp.max(jnp.where(hit, local[None, :], 0), axis=1) - 1
    message = jnp.concatenate(
        [
            asked.reshape(n_dev, room),
            jnp.broadcast_to(rounds, (n_dev, 128 - room)).astype(jnp.int32),
        ],
        axis=1,
    ).reshape(n_dev, 1, 128)
    heard = lax.all_to_all(message, axes, split_axis=0, concat_axis=0).reshape(n_dev, 128)
    return heard[:, :room].reshape(-1), jnp.max(heard[:, room:])


def ask_rows(plan, wanted, table_low, axes):
    room, own_rows, n_dev = plan[5], plan[7], plan[8]
    one_hot = (wanted[:, None] == jnp.arange(own_rows)[None, :]).astype(jnp.bfloat16)
    rows = dense(one_hot, table_low).astype(jnp.bfloat16)
    return lax.all_to_all(rows.reshape(n_dev, room, -1), axes, split_axis=0, concat_axis=0)


def place_rows(plan, turn, rows):
    room, n_dev = plan[5], plan[8]
    back = (slots_of(plan, turn)[:, None] == jnp.arange(n_dev * room)[None, :]).astype(
        jnp.bfloat16
    )
    return dense(back, rows.reshape(n_dev * room, -1))


def more_rows(plan, rounds, token_rows, table_low, axes):
    def body(state):
        turn, total = state
        wanted, _ = exchange_wanted(plan, turn, axes)
        rows = ask_rows(plan, wanted, table_low, axes)
        return turn + 1, total + place_rows(plan, turn, rows)

    return lax.while_loop(lambda state: state[0] < rounds, body, (jnp.int32(1), token_rows))[1]


def rows_to_give(plan, turn, flat_grad):
    room, n_dev = plan[5], plan[8]
    spread = (jnp.arange(n_dev * room)[:, None] == slots_of(plan, turn)[None, :]).astype(
        jnp.bfloat16
    )
    sums = dense(spread, flat_grad).astype(jnp.bfloat16)
    return sums.reshape(n_dev, room, -1)


def give_rows(sums, axes):
    got = lax.all_to_all(sums, axes, split_axis=0, concat_axis=0)
    return got.reshape(-1, sums.shape[-1])


def more_given(plan, rounds, flat_grad, own_rows, own_part, axes):
    def body(state):
        turn, total = state
        wanted, _ = exchange_wanted(plan, turn, axes)
        one_hot = (jnp.arange(own_part.shape[0])[:, None] == wanted[None, :]).astype(jnp.bfloat16)
        got = give_rows(rows_to_give(plan, turn, flat_grad), axes)
        return turn + 1, (total.astype(jnp.float32) + dense(one_hot, got)).astype(total.dtype)

    return lax.while_loop(lambda state: state[0] < rounds, body, (jnp.int32(1), own_part))[1]


def at_lane(tile, lane, value):
    row = lax.broadcasted_iota(jnp.int32, tile.shape, 0)
    column = lax.broadcasted_iota(jnp.int32, tile.shape, 1)
    return tile + jnp.where((row == 0) & (column == lane), value, 0.0)


def total_sum(values):
    return jnp.sum(jnp.sum(values, axis=0, keepdims=True), axis=1, keepdims=True)


def table_kernel(
    own_rows,
    wanted_ref,
    returned_ref,
    moved_ref,
    part_ref,
    tile_ref,
    hidden_loss_ref,
    head_loss_ref,
    last_loss_ref,
    out_ref,
    up_ref,
    down_ref,
    last_ref,
    grad_ref,
    place_ref,
    qkv_ref,
    vector_ref,
    sum_ref,
):
    rows = grad_ref.shape[0]
    first = pl.program_id(0) * rows
    spot = lax.broadcasted_iota(jnp.int32, (rows, wanted_ref.shape[1]), 0) + first
    hot = (spot == wanted_ref[...]).astype(jnp.bfloat16)
    grads = dense(hot, returned_ref[...])
    grads = grads + (moved_ref[...].astype(jnp.float32) + part_ref[...].astype(jnp.float32))
    row = lax.broadcasted_iota(jnp.int32, grads.shape, 0) + first
    grads = jnp.where(row < own_rows, grads, 0.0)
    grad_ref[...] = grads

    @pl.when(pl.program_id(0) == 0)
    def _():
        sum_ref[...] = tile_ref[...]
        for loss_ref in (hidden_loss_ref, head_loss_ref, last_loss_ref):
            sum_ref[...] = at_lane(sum_ref[...], 1, total_sum(loss_ref[...]))
        width, places = last_ref.shape[2], place_ref.shape[1]
        for part in range(3):
            qkv_ref[:, part * width : (part + 1) * width] = last_ref[part]
        place_ref[...] = last_ref[3][:, :places]
        vectors = last_ref[3][:, places : places + 128].T
        vector_ref[...] = vectors[: vector_ref.shape[0], :]
        for other in (out_ref, up_ref, down_ref, place_ref, qkv_ref, vector_ref):
            sum_ref[...] = at_lane(sum_ref[...], 0, total_sum(other[...] * other[...]))

    sum_ref[...] = at_lane(sum_ref[...], 0, total_sum(grads * grads))


def update_kernel(own_rows, steps, every_ref, *refs):
    weights, grads, firsts, seconds = [refs[7 * k : 7 * k + 7] for k in range(4)]
    moments, squares, updates = [refs[7 * k : 7 * k + 7] for k in range(4, 7)]
    total_ref, sum_ref = refs[49:]
    totals = jnp.sum(every_ref[...], axis=0)
    count = totals[0:1, 2:3]
    norm = jnp.sqrt(totals[0:1, 0:1]) / count
    factor = jnp.minimum(1.0, CLIP_NORM / norm) / count

    def step(place, live=None):
        weight = weights[place][...]
        clipped = grads[place][...] * factor
        moment = BETA_ONE * firsts[place][...] + (1.0 - BETA_ONE) * clipped
        square = BETA_TWO * seconds[place][...] + (1.0 - BETA_TWO) * clipped * clipped
        update = (
            moment
            * (1.0 / (1.0 - BETA_ONE**STEP))
            / (jnp.sqrt(square * (1.0 / (1.0 - BETA_TWO**STEP))) + ADAM_EPS)
            + DECAY_RATE * weight
        )
        moments[place][...] = moment
        squares[place][...] = square
        updates[place][...] = update
        if live is not None:
            update = jnp.where(live, update, 0.0)
        sum_ref[...] = at_lane(sum_ref[...], place, total_sum(update * update))

    @pl.when(pl.program_id(0) == 0)
    def _():
        total_ref[...] = at_lane(totals, 127, norm)
        sum_ref[...] = jnp.zeros_like(sum_ref)

    for place in range(1, 7):

        @pl.when(pl.program_id(0) == place % steps)
        def _():
            step(place)

    row = lax.broadcasted_iota(jnp.int32, weights[0].shape, 0)
    step(0, row + pl.program_id(0) * weights[0].shape[0] < own_rows)


def weight_kernel(steps, every_ref, total_ref, *refs):
    weights, updates, outs = refs[:7], refs[7:14], refs[14:21]
    sum_ref = refs[21]
    update_norms = jnp.sqrt(jnp.sum(every_ref[...], axis=0))

    def step(place):
        norm = jnp.sqrt(total_ref[0:1, 3 + place : 4 + place])
        ratio = LEARN_RATE * (norm / update_norms[0:1, place : place + 1])
        outs[place][...] = weights[place][...] - ratio * updates[place][...]

    @pl.when(pl.program_id(0) == 0)
    def _():
        sum_ref[...] = update_norms

    for place in range(1, 7):

        @pl.when(pl.program_id(0) == place % steps)
        def _():
            step(place)

    step(0)


def hidden_order(values, row_width):
    lead = values.shape[:-1]
    return jnp.swapaxes(values.reshape(lead + (row_width, -1)), -1, -2).reshape(lead + (-1,))


def hidden_back(values, row_width):
    lead = values.shape[:-1]
    return jnp.swapaxes(values.reshape(lead + (-1, row_width)), -1, -2).reshape(lead + (-1,))


def column_blocks(values, row_width):
    return [values[:, c : c + row_width] for c in range(0, values.shape[1], row_width)]


def on_device(
    token_ids,
    true_mask,
    keep_layer,
    picked,
    teacher_hidden,
    teacher_logits,
    embed_table,
    pos_table,
    query_key_value_weight,
    output_weight,
    up_weight,
    down_weight,
    gains_biases,
    first_embed,
    first_pos,
    first_qkv,
    first_out,
    first_up,
    first_down,
    first_gains,
    second_embed,
    second_pos,
    second_qkv,
    second_out,
    second_up,
    second_down,
    second_gains,
):
    axes = AXES
    n_dp, n_fs = lax.axis_size(SPLIT), lax.axis_size("fsdp")
    n_dev = n_dp * n_fs
    i_fs = lax.axis_index("fsdp")
    masters = (
        embed_table,
        pos_table,
        query_key_value_weight,
        output_weight,
        up_weight,
        down_weight,
        gains_biases,
    )
    firsts = (first_embed, first_pos, first_qkv, first_out, first_up, first_down, first_gains)
    seconds = (
        second_embed,
        second_pos,
        second_qkv,
        second_out,
        second_up,
        second_down,
        second_gains,
    )
    seq_count, seq_len = token_ids.shape
    own_rows, row_width = embed_table.shape
    ff = up_weight.shape[1]
    in_rows = query_key_value_weight.shape[0]
    n_tok = seq_count * seq_len
    n_pick = picked.shape[0] * picked.shape[1]
    vocab = own_rows * n_dev
    block_rows = own_rows * n_fs

    table_low = embed_table.astype(jnp.bfloat16)
    pack_width = 3 * row_width + row_width + ff + ff + seq_len
    gain_width = -(-14 // 128) * 128
    packed_low = jnp.concatenate(
        [
            query_key_value_weight,
            output_weight,
            hidden_order(up_weight, row_width),
            down_weight.reshape(in_rows, ff),
            pos_table.T,
            jnp.pad(gains_biases.T, ((0, 0), (0, gain_width - 14))),
        ],
        axis=1,
    ).astype(jnp.bfloat16)
    gathered = lax.all_gather(packed_low, axes, axis=0, tiled=True)
    plan = route_plan(token_ids.reshape(-1), true_mask.reshape(-1) > 0, own_rows, n_dev)
    wanted, rounds = exchange_wanted(plan, 0, axes)
    ring = [(z, (z + 1) % n_fs) for z in range(n_fs)]
    padded = -(-own_rows // 16) * 16
    lanes = -(-own_rows // 128) * 128
    first_table = jnp.pad(table_low, ((0, padded - own_rows), (0, 0)))
    arrived = ask_rows(plan, wanted, table_low, axes)

    targets = parcels_of(teacher_logits.reshape(n_pick, vocab), own_rows, lanes, n_dev)
    arrived, targets = lax.optimization_barrier((arrived, targets))
    targets = lax.all_to_all(
        targets.reshape(n_dp, n_fs, n_pick, lanes), SPLIT, split_axis=0, concat_axis=0
    )
    tile = jnp.zeros((8, 128), jnp.float32)
    scalars = [jnp.sum(true_mask.astype(jnp.float32))]
    scalars += [jnp.sum(member * member) for member in masters]
    for place, value in enumerate(scalars):
        tile = at_lane(tile, place + 2, value)
    arrived, first_table, tile = lax.optimization_barrier((arrived, first_table, tile))
    tables = [first_table, lax.ppermute(first_table, "fsdp", ring)]

    i_dp = lax.axis_index(SPLIT)
    token_rows = place_rows(plan, 0, arrived)
    token_rows = more_rows(plan, rounds, token_rows, table_low, axes)

    def pass_table(*later):
        newest, *later = lax.optimization_barrier((tables[-1], *later))
        if len(tables) < n_fs:
            tables.append(lax.ppermute(newest, "fsdp", ring))
        return later

    places = lax.rem(i_fs - jnp.arange(n_fs, dtype=jnp.int32) + n_fs, n_fs)

    rows = seq_len // 2
    n_block = seq_len // rows
    keeps = (keep_layer > 0).astype(jnp.int32)
    trues = jnp.sum(true_mask, axis=1)
    lengths = trues * keeps
    pick_column = picked.reshape(-1, 1)
    bf16, f32 = jnp.bfloat16, jnp.float32

    def by_seq(width, array=None):
        spec = ((rows, width), lambda s, b, *_: (s * n_block + b, 0))
        return spec if array is None else (array, *spec)

    def by_block(width, array=None):
        spec = ((rows, width), lambda b, s, *_: (s * n_block + b, 0))
        return spec if array is None else (array, *spec)

    def whole(shape):
        return (shape, lambda *_: (0,) * len(shape))

    def weight(width, place):
        return (gathered, (row_width, width), lambda *_: (0, place))

    vectors = weight(gain_width, pack_width // gain_width)
    qkv_weight = weight(3 * row_width, 0)
    out_weight = weight(row_width, 3)
    up_weight_low, down_weight_low = weight(ff, 1), weight(ff, 2)
    first_place = (4 * row_width + 2 * ff) // rows
    embedded, flat_in, flat_low, packed = row_kernel(
        enter_kernel,
        (lengths,),
        [
            by_block(row_width, token_rows),
            (gathered, (row_width, rows), lambda b, s, *_: (0, first_place + b)),
            vectors,
            qkv_weight,
        ],
        [
            ((n_tok, row_width), f32, *by_block(row_width)),
            ((n_tok, row_width), f32, *by_block(row_width)),
            ((n_tok, row_width), bf16, *by_block(row_width)),
            ((n_tok, 3 * row_width), bf16, *by_block(3 * row_width)),
        ],
        (n_block, seq_count),
    )
    mixed_output = attend(lengths, packed)
    (mixed_output,) = pass_table(mixed_output)
    up_bias = hidden_order(
        gathered[:, pack_width + 10 : pack_width + 14].astype(f32).T.reshape(1, -1), row_width
    )
    pick_count = picked.shape[1]
    picks = (pick_column, (pick_count, 1), lambda s, b, *_: (s, 0))
    (
        joined_one,
        normed_low,
        gelu_slopes,
        gelu_activated,
        joined_two,
        grad_start,
        chosen,
        hidden_loss,
    ) = row_kernel(
        feed_kernel,
        (lengths, trues),
        [
            by_seq(row_width, mixed_output),
            by_seq(row_width, flat_in),
            by_seq(row_width, teacher_hidden.reshape(n_tok, row_width)),
            picks,
            vectors,
            (up_bias, *whole((1, ff))),
            out_weight,
            up_weight_low,
            down_weight_low,
        ],
        [
            ((n_tok, row_width), f32, *by_seq(row_width)),
            ((n_tok, row_width), bf16, *by_seq(row_width)),
            ((n_tok, ff), bf16, *by_seq(ff)),
            ((n_tok, ff), bf16, *by_seq(ff)),
            ((n_tok, row_width), f32, *by_seq(row_width)),
            ((n_tok, row_width), f32, *by_seq(row_width)),
            ((n_pick, row_width), bf16, (pick_count, row_width), lambda s, b, *_: (s, 0)),
            ((8, row_width), f32, *whole((8, row_width))),
        ],
        (seq_count, n_block),
        [pltpu.VMEM((rows, row_width), f32)],
    )

    if n_fs > 2:
        (chosen,) = pass_table(chosen)
    by_distance = jnp.stack(
        [chosen]
        + [
            lax.ppermute(chosen, SPLIT, [(p, p ^ apart) for p in range(n_dp)])
            for apart in range(1, n_dp)
        ]
    )
    all_chosen = jnp.concatenate(
        [lax.dynamic_index_in_dim(by_distance, i_dp ^ p, 0, False) for p in range(n_dp)]
    )
    while len(tables) < n_fs:
        (all_chosen,) = pass_table(all_chosen)
    slopes, chosen_part, head_loss = head_products(
        places[:-1], all_chosen, targets, tables[:-1], [], jnp.float32
    )
    last_slopes, chosen_part, last_loss = head_products(
        places[-1:], all_chosen, targets, tables[-1:], [chosen_part], jnp.bfloat16
    )
    many = n_dp * n_pick
    all_picked = (all_chosen, (many, row_width), lambda d: (0, 0))
    (head_part,) = row_kernel(
        head_first_kernel,
        (),
        [(slopes, (1, many, padded), lambda d: (1, 0, 0)), all_picked],
        [((padded, row_width), bf16, (padded, row_width), lambda d: (0, 0))],
        (1,),
    )
    head_sums = [lax.ppermute(head_part, "fsdp", ring)]
    last_slopes, grad_chosen = lax.optimization_barrier((last_slopes, chosen_part))
    grad_chosen = lax.all_to_all(
        grad_chosen.reshape(n_dp, n_pick, row_width), SPLIT, split_axis=0, concat_axis=0
    )
    head_parts = row_kernel(
        head_grad_kernel,
        (),
        [
            (
                slopes,
                (1, many, padded),
                lambda d: (jnp.where(d < n_fs - 3, d + 2, 0), 0, 0),
            ),
            (last_slopes, (1, many, padded), lambda d: (0, 0, 0)),
            all_picked,
        ],
        [((padded, row_width), bf16, (padded, row_width), lambda d: (0, 0))] * (n_fs - 1),
        (n_fs - 1,),
    )

    def pass_sum(*later):
        newest, *later = lax.optimization_barrier((head_sums[-1], *later))
        step = len(head_sums)
        if step + 1 < n_fs:
            total = newest.astype(f32) + head_parts[step - 1].astype(f32)
            head_sums.append(lax.ppermute(total.astype(bf16), "fsdp", ring))
        return later

    grad_chosen, *head_parts = pass_sum(grad_chosen, *head_parts)
    for _ in range(n_fs - 4):
        (grad_chosen,) = pass_sum(grad_chosen)

    (
        grad_final,
        grad_joined_one,
        grad_mixed,
        grad_attention,
        grad_feed,
        grad_hidden,
        sums_one,
        hidden_sums,
    ) = row_kernel(
        unfeed_kernel,
        (lengths,),
        [
            by_seq(row_width, grad_start),
            (grad_chosen, (n_dp, pick_count, row_width), lambda s, b, *_: (0, s, 0)),
            picks,
            by_seq(row_width, joined_one),
            by_seq(ff, gelu_slopes),
            by_seq(row_width, joined_two),
            vectors,
            out_weight,
            up_weight_low,
            down_weight_low,
        ],
        [
            ((n_tok, row_width), f32, *by_seq(row_width)),
            ((n_tok, row_width), f32, *by_seq(row_width)),
            ((n_tok, row_width), bf16, *by_seq(row_width)),
            ((n_tok, row_width), bf16, *by_seq(row_width)),
            ((n_tok, row_width), bf16, *by_seq(row_width)),
            ((n_tok, ff), bf16, *by_seq(ff)),
            ((6, 8, row_width), f32, *whole((6, 8, row_width))),
            ((8, ff), f32, *whole((8, ff))),
        ],
        (seq_count, n_block),
    )
    member = lax.axis_index("pair").reshape(1).astype(jnp.int32)
    n_plane = lax.axis_size("plane")
    share = row_width // (2 * n_plane)
    halves = pltpu.VMEM((n_plane, 2, share, row_width), bf16)

    def dealt(columns):
        out = (
            (columns, n_plane, share, row_width),
            bf16,
            (1, n_plane, share, row_width),
            lambda j, *_: (j, 0, 0, 0),
        )
        return [out, out]

    def full(array):
        return (array, *whole(array.shape))

    blocks = ff // row_width
    early_kept, early_given = row_kernel(
        early_kernel,
        (member,),
        [
            full(mixed_output),
            full(grad_attention),
            full(normed_low),
            (
                grad_hidden,
                (n_tok, row_width),
                lambda j, *_: (0, jnp.clip(j - 1, 0, blocks - 1)),
            ),
            (
                gelu_activated,
                (n_tok, row_width),
                lambda j, *_: (0, jnp.clip(j - 1 - blocks, 0, blocks - 1)),
            ),
            full(grad_feed),
        ],
        dealt(1 + 2 * blocks),
        (1 + 2 * blocks,),
        [halves],
    )
    up_rows = hidden_back(jnp.sum(hidden_sums, axis=0, keepdims=True), row_width)
    early_kept, early_given = pass_sum(early_kept, early_given)
    early = sum_in_pair(early_kept, early_given)
    grad_mixed, early, up_rows = lax.optimization_barrier((grad_mixed, early, up_rows))
    early = sum_in_plane(early)
    *grad_parts, head_sums[-1] = lax.optimization_barrier(
        (*attend(lengths, packed, grad_mixed), head_sums[-1])
    )
    flat_grad, place_grad, sums_two = row_kernel(
        leave_kernel,
        (lengths, keeps),
        [by_block(row_width, part) for part in grad_parts]
        + [
            by_block(row_width, grad_joined_one),
            by_block(row_width, grad_final),
            by_block(row_width, embedded),
            vectors,
            qkv_weight,
        ],
        [
            ((n_tok, row_width), bf16, *by_block(row_width)),
            ((row_width, seq_len), bf16, (row_width, rows), lambda b, s, *_: (0, b)),
            ((4, 8, row_width), f32, *whole((4, 8, row_width))),
        ],
        (n_block, seq_count),
        [pltpu.VMEM((rows, row_width), f32)],
    )
    flat_grad, early = lax.optimization_barrier((flat_grad, early))
    early = lax.psum_scatter(
        early.reshape(early.shape[0], -1, row_width), "fsdp", scatter_dimension=1, tiled=True
    ).astype(f32)
    given_rows = rows_to_give(plan, 0, flat_grad)
    given_rows, *grad_parts = lax.optimization_barrier((given_rows, *grad_parts))
    returned = give_rows(given_rows, axes)
    own_part = more_given(plan, rounds, flat_grad, own_rows, head_parts[n_fs - 2], axes)
    late_kept, late_given = row_kernel(
        late_kernel,
        (member,),
        [full(flat_low)]
        + [full(part) for part in grad_parts]
        + [
            full(place_grad),
            full(sums_one),
            full(sums_two),
            full(up_rows.reshape(4, row_width)),
        ],
        dealt(4),
        (4,),
        [
            halves,
            pltpu.VMEM((row_width, row_width), f32),
            pltpu.VMEM((gain_width, row_width), f32),
        ],
    )
    late_kept, late_given, own_part = lax.optimization_barrier(
        (late_kept, late_given, own_part)
    )
    last = sum_in_plane(sum_in_pair(late_kept, late_given, 4))
    returned, last = lax.optimization_barrier((returned, last))
    last = sum_in_line(last)
    early_grads = (
        early[0],
        jnp.transpose(early[1 : 1 + blocks], (1, 2, 0)).reshape(in_rows, ff),
        jnp.swapaxes(early[1 + blocks :], 0, 1).reshape(-1, row_width),
    )
    rows = 208
    steps = -(-own_rows // rows)

    def by_row(array=None, width=row_width):
        spec = ((rows, width), lambda r, *_: (r, 0))
        return spec if array is None else (array, *spec)

    table_grad, place_sums, qkv_sums, vector_sums, tile = row_kernel(
        functools.partial(table_kernel, own_rows),
        (),
        [
            full(wanted.reshape(1, -1)),
            full(returned),
            by_row(head_sums[-1]),
            by_row(own_part),
            full(tile),
            full(hidden_loss),
            full(head_loss),
            full(last_loss),
        ]
        + [full(grad) for grad in early_grads]
        + [full(last)],
        [
            ((own_rows, row_width), f32, *by_row()),
            ((in_rows, seq_len), f32, *whole((in_rows, seq_len))),
            ((in_rows, 3 * row_width), f32, *whole((in_rows, 3 * row_width))),
            (gains_biases.shape, f32, *whole(gains_biases.shape)),
            ((8, 128), f32, *whole((8, 128))),
        ],
        (steps,),
    )

    def exchange(tile):
        return lax.all_to_all(
            jnp.broadcast_to(tile[None], (n_dev, 8, 128)), axes, split_axis=0, concat_axis=0
        )

    def turned(arrays):
        return [array.T if place == 1 else array for place, array in enumerate(arrays)]

    def specs(arrays):
        return [by_row(arrays[0])] + [full(array) for array in arrays[1:]]

    weights = turned(masters)
    like = [
        (array.shape, f32, *(whole(array.shape) if place else by_row()))
        for place, array in enumerate(weights)
    ]
    tile_out = ((8, 128), f32, *whole((8, 128)))
    *results, totals, tile = row_kernel(
        functools.partial(update_kernel, own_rows, steps),
        (),
        [full(exchange(tile))]
        + specs(weights)
        + specs([table_grad, place_sums, qkv_sums, *early_grads, vector_sums])
        + specs(turned(firsts))
        + specs(turned(seconds)),
        like * 3 + [tile_out, tile_out],
        (steps,),
    )
    new_moments, new_squares = turned(results[:7]), turned(results[7:14])
    *new_weights, update_norms = row_kernel(
        functools.partial(weight_kernel, steps),
        (),
        [full(exchange(tile)), full(totals)] + specs(weights) + specs(results[14:]),
        like + [tile_out],
        (steps,),
    )
    new_weights = turned(new_weights)
    loss_sum, token_count, grad_norm = totals[0, 1], totals[0, 2], totals[0, 127]
    matrix_norms = jnp.stack([jnp.sqrt(totals[0, 3:10]), update_norms[0, :7]])
    return (
        loss_sum,
        token_count,
        grad_norm,
        new_weights[0],
        new_weights[1],
        new_weights[2],
        new_weights[3],
        new_weights[4],
        new_weights[5],
        new_weights[6],
        new_moments[0],
        new_moments[1],
        new_moments[2],
        new_moments[3],
        new_moments[4],
        new_moments[5],
        new_moments[6],
        new_squares[0],
        new_squares[1],
        new_squares[2],
        new_squares[3],
        new_squares[4],
        new_squares[5],
        new_squares[6],
        matrix_norms,
    )


def solution(mesh):
    split = Mesh(
        mesh.devices.reshape(mesh.shape["dp"] // 2, 2, mesh.shape["fsdp"]), AXES
    )
    placed = (
        P(AXES, None),
        P(AXES, None),
        P(AXES),
        P(AXES, None),
        P(AXES, None, None),
        P(AXES, None, None),
        P(AXES, None),
        P(None, AXES),
        P(AXES, None),
        P(AXES, None),
        P(AXES, None),
        P(AXES, None),
        P(None, AXES),
        P(AXES, None),
        P(None, AXES),
        P(AXES, None),
        P(AXES, None),
        P(AXES, None),
        P(AXES, None),
        P(None, AXES),
        P(AXES, None),
        P(None, AXES),
        P(AXES, None),
        P(AXES, None),
        P(AXES, None),
        P(AXES, None),
        P(None, AXES),
    )
    return jax.shard_map(
        on_device,
        mesh=split,
        in_specs=placed,
        out_specs=(
            P(),
            P(),
            P(),
            P(AXES, None),
            P(None, AXES),
            P(AXES, None),
            P(AXES, None),
            P(AXES, None),
            P(AXES, None),
            P(None, AXES),
            P(AXES, None),
            P(None, AXES),
            P(AXES, None),
            P(AXES, None),
            P(AXES, None),
            P(AXES, None),
            P(None, AXES),
            P(AXES, None),
            P(None, AXES),
            P(AXES, None),
            P(AXES, None),
            P(AXES, None),
            P(AXES, None),
            P(None, AXES),
            P(),
        ),
        check_vma=False,
    )
```

profile of v0, /device:TPU:0, one launch (start us, length us, event | category | flops | bytes accessed | tf_op | source)
XLA Modules:
  0.0 721.0 jit_solution(98281848447991414)
XLA Ops:
  21.2 7.3 %all-to-all-start.4 = ((s32[32,1,128]{2,1,0:T(1,128)}), s32[32,1,128]{2,1,0:T(1,128)S(1)}, u32[]{:S(2)}, u32[]{:S(2)}) async-start(s32[32,1,128]{2,1,0:T(1,128)} %bitcast.8), calls=%async_computation.4 | async-start | bytes 32768 | tf_op jit(solution)/shard_map/all_to_all | solution.py:718
  28.5 7.1 multiply_reduce_fusion
  35.9 6.9 fusion.17
  42.8 5.6 all-to-all-start.5
  48.5 24.3 %shard_map.450 = bf16[32,128,1664]{2,1,0:T(8,128)(2,1)} custom-call(bf16[128,50304]{1,0:T(8,128)(2,1)} %bitcast.161), custom_call_target="tpu_custom_call" | custom-call | tf_op jit(solution)/shard_map/pallas_call | solution.py:581
  78.7 5.8 select_add_fusion.tile_ref
  85.3 42.4 %all-to-all-done.5 = bf16[32,40,768]{2,1,0:T(8,128)(2,1)S(1)} async-done(((bf16[32,40,768]{2,1,0:T(8,128)(2,1)}), bf16[32,40,768]{2,1,0:T(8,128)(2,1)S(1)}, u32[]{:S(2)}, u32[]{:S(2)}) %all-to-all-start.5) | async-done | bytes 1966112 | tf_op jit(solution)/shard_map/all_to_all | solution.py:726
  127.7 4.1 fusion.13
  132.6 5.6 all-to-all-start.6
  138.2 6.7 collective-permute-start
  145.6 61.2 %all-gather.2.cloned.1.call-done.place_ref.vector_ref.weight_ref.out_ref.up_ref.down_ref = bf16[768,9856]{1,0:T(8,128)(2,1)} async-done(((bf16[24,9856]{1,0:T(8,128)(2,1)}), bf16[768,9856]{1,0:T(8,128)(2,1)}) %all-gather.2.cloned.1.call-update) | async-done | bytes 15138832 | tf_op jit(solution)/shard_map/all_gather | solution.py:983
  206.8 9.2 %shard_map.451 = (f32[1024,768]{1,0:T(8,128)}, f32[1024,768]{1,0:T(8,128)}, bf16[1024,768]{1,0:T(8,128)(2,1)}, bf16[1024,2304]{1,0:T(8,128)(2,1)}) custom-call(s32[2]{0:T(128)} %compare_select_fusion.2.length_ref, f32[1024,768]{1,0:T(8,128)} %get-tuple-element.394.token_ref, ...), custom_call_target="tpu_custom_call" | custom-call | tf_op jit(solution)/shard_map/pallas_call | solution.py:519
  216.1 8.9 %shard_map.452.mixed_ref = bf16[1024,768]{1,0:T(8,128)(2,1)} custom-call(s32[2]{0:T(128)} %compare_select_fusion.2.length_ref, bf16[1024,2304]{1,0:T(8,128)(2,1)} %get-tuple-element.395.query_ref.key_ref.value_ref, bf16[1024,2304]{1,0:T(8,128)(2,1)} %get-tuple-element.395.query_ref.key_ref.value_ref, ...), custom_call_target="tpu_custom_call" | custom-call | tf_op jit(solution)/shard_map/pallas_call | solution.py:170
  228.9 14.6 %shard_map.453 = (f32[1024,768]{1,0:T(8,128)}, bf16[1024,768]{1,0:T(8,128)(2,1)}, bf16[1024,3072]{1,0:T(8,128)(2,1)}, bf16[1024,3072]{1,0:T(8,128)(2,1)}, f32[10...) custom-call(s32[2]{0:T(128)} %compare_select_fusion.2.length_ref, ...), custom_call_target="tpu_custom_call" | custom-call | tf_op jit(solution)/shard_map/pallas_call | solution.py:519
  243.5 33.4 %collective-permute-done.1.refs_2_ = bf16[1584,768]{1,0:T(8,128)(2,1)} collective-permute-done((bf16[1584,768]{1,0:T(8,128)(2,1)}, bf16[1584,768]{1,0:T(8,128)(2,1)}, u32[]{:S(2)}, u32[]{:S(2)}) %collective-permute-start.1) | collective-permute-done | bytes 2433056 | tf_op jit(solution)/shard_map/ppermute | solution.py:1012
  276.8 6.0 collective-permute-start.2
  284.2 4.7 collective-permute-start.5
  296.5 5.8 collective-permute-start.10
  302.3 4.0 collective-permute-done.6
  307.8 25.6 %shard_map.454 = (bf16[3,1024,1584]{2,1,0:T(8,128)(2,1)}, f32[1024,768]{1,0:T(8,128)}, f32[8,1584]{1,0:T(8,128)}) custom-call(s32[3]{0:T(128)} %bitcast.196, bf16[1024,768]{1,0:T(8,128)(2,1)} %copy-done, bf16[8,4,128,1664]{3,2,1,0:T(8,128)(2,1)} %all-to-all-done.6.target_ref, bf16[1584,768]{1,0:T(8,128)(2,1)} %pad.18.refs_0_, ...), custom_call_target="tpu_custom_call" | custom-call | tf_op jit(solution)/shard_map/pallas_call | solution.py:630
  333.4 6.7 shard_map.455
  340.1 5.0 collective-permute-start.9
  345.7 10.0 %collective-permute-done.10.refs_0_ = bf16[1584,768]{1,0:T(8,128)(2,1)} collective-permute-done((bf16[1584,768]{1,0:T(8,128)(2,1)}, bf16[1584,768]{1,0:T(8,128)(2,1)}, u32[]{:S(2)}, u32[]{:S(2)}) %collective-permute-start.10) | collective-permute-done | bytes 2433056 | tf_op jit(solution)/shard_map/ppermute | solution.py:1012
  355.7 14.0 %shard_map.456 = (bf16[1,1024,1584]{2,1,0:T(8,128)(2,1)}, bf16[1024,768]{1,0:T(8,128)(2,1)}, f32[8,1584]{1,0:T(8,128)}) custom-call(s32[1]{0:T(128)} %slice.67.place_ref, bf16[1024,768]{1,0:T(8,128)(2,1)} %copy-done, bf16[8,4,128,1664]{3,2,1,0:T(8,128)(2,1)} %all-to-all-done.6.target_ref, bf16[1584,768]{1,0:T(8,128)(2,1)} %collective-permute-done.10.refs_0_, ...), custom_call_target="tpu_custom_call" | custom-call | tf_op jit(solution)/shard_map/pallas_call | solution.py:630
  369.8 4.1 all-to-all-start.7
  373.8 14.9 %shard_map.457 = (bf16[1584,768]{1,0:T(8,128)(2,1)}, bf16[1584,768]{1,0:T(8,128)(2,1)}, bf16[1584,768]{1,0:T(8,128)(2,1)}) custom-call(bf16[3,1024,1584]{2,1,0:T(8,128)(2,1)} %get-tuple-element.404.slope_ref, bf16[1,1024,1584]{2,1,0:T(8,128)(2,1)} %get-tuple-element.410.last_ref, bf16[1024,768]{1,0:T(8,128)(2,1)} %copy-done), custom_call_target="tpu_custom_call" | custom-call | tf_op jit(solution)/shard_map/pallas_call | solution.py:519
  388.7 19.2 %collective-permute-done.9 = bf16[1584,768]{1,0:T(8,128)(2,1)} collective-permute-done((bf16[1584,768]{1,0:T(8,128)(2,1)}, bf16[1584,768]{1,0:T(8,128)(2,1)}, u32[]{:S(2)}, u32[]{:S(2)}) %collective-permute-start.9) | collective-permute-done | bytes 2433056 | tf_op jit(solution)/shard_map/ppermute | solution.py:1134
  407.9 5.0 add_convert_fusion.3
  415.6 16.5 %shard_map.458 = (f32[1024,768]{1,0:T(8,128)}, f32[1024,768]{1,0:T(8,128)}, bf16[1024,768]{1,0:T(8,128)(2,1)}, bf16[1024,768]{1,0:T(8,128)(2,1)}, bf16[1024,768]...) custom-call(s32[2]{0:T(128)} %compare_select_fusion.2.length_ref, ...), custom_call_target="tpu_custom_call" | custom-call | tf_op jit(solution)/shard_map/pallas_call | solution.py:519
  432.1 20.0 %shard_map.459 = (bf16[9,4,96,768]{3,2,1,0:T(8,128)(2,1)}, bf16[9,4,96,768]{3,2,1,0:T(8,128)(2,1)}) custom-call(s32[1]{0:T(128)} %bitcast.38.member_ref, bf16[1024,768]{1,0:T(8,128)(2,1)} %shard_map.452.mixed_ref, bf16[1024,768]{1,0:T(8,128)(2,1)} %get-tuple-element.420.attention_ref, bf16[1024,768]{1,0:T(8,128)(2,1)} %get-tuple-element.421.normed_ref, ...), custom_call_target="tpu_custom_call" | custom-call | tf_op jit(solution)/shard_map/pallas_call | solution.py:519
  452.0 18.1 %collective-permute-done.11 = bf16[1584,768]{1,0:T(8,128)(2,1)} collective-permute-done((bf16[1584,768]{1,0:T(8,128)(2,1)}, bf16[1584,768]{1,0:T(8,128)(2,1)}, u32[]{:S(2)}, u32[]{:S(2)}) %collective-permute-start.11) | collective-permute-done | bytes 2433056 | tf_op jit(solution)/shard_map/ppermute | solution.py:1160
  470.2 3.8 add_convert_fusion.2
  475.4 3.8 collective-permute-done.12
  479.3 6.1 add_convert_fusion.1
  492.9 9.9 %shard_map.460 = (bf16[1024,768]{1,0:T(8,128)(2,1)}, bf16[1024,768]{1,0:T(8,128)(2,1)}, bf16[1024,768]{1,0:T(8,128)(2,1)}) custom-call(s32[2]{0:T(128)} %compare_select_fusion.2.length_ref, bf16[1024,2304]{1,0:T(8,128)(2,1)} %get-tuple-element.395.query_ref.key_ref.value_ref, bf16[1024,2304]{1,0:T(8,128)(2,1)} %get-tuple-element.395.query_ref.key_ref.value_ref, ...), custom_call_target="tpu_custom_call" | custom-call | tf_op jit(solution)/shard_map/pallas_call | solution.py:170
  502.8 28.8 %collective-permute-done.13.moved_ref = bf16[1584,768]{1,0:T(8,128)(2,1)S(1)} collective-permute-done((bf16[1584,768]{1,0:T(8,128)(2,1)}, bf16[1584,768]{1,0:T(8,128)(2,1)S(1)}, u32[]{:S(2)}, u32[]{:S(2)}) %collective-permute-start.13) | collective-permute-done | bytes 2433056 | tf_op jit(solution)/shard_map/ppermute | solution.py:1160
  531.6 10.5 %shard_map.461 = (bf16[1024,768]{1,0:T(8,128)(2,1)}, bf16[768,512]{1,0:T(8,128)(2,1)}, f32[4,8,768]{2,1,0:T(8,128)}) custom-call(s32[2]{0:T(128)} %compare_select_fusion.2.length_ref, s32[2]{0:T(128)} %compare_convert_fusion.keep_ref, bf16[1024,768]{1,0:T(8,128)(2,1)} %get-tuple-element.447.query_ref, bf16[1024,768]{1,0:T(8,128)(2,1)} %get-tuple-element.448.key_ref, ...), custom_call_target="tpu_custom_call" | custom-call | tf_op jit(solution)/shard_map/pallas_call | solution.py:519
  542.1 6.1 collective-permute-done.15
  553.0 5.1 fusion.18
  565.5 9.1 %shard_map.462 = (bf16[4,4,96,768]{3,2,1,0:T(8,128)(2,1)}, bf16[4,4,96,768]{3,2,1,0:T(8,128)(2,1)}) custom-call(s32[1]{0:T(128)} %bitcast.38.member_ref, bf16[1024,768]{1,0:T(8,128)(2,1)} %get-tuple-element.446.low_ref, bf16[1024,768]{1,0:T(8,128)(2,1)} %get-tuple-element.447.query_ref, bf16[1024,768]{1,0:T(8,128)(2,1)} %get-tuple-element.448.key_ref, ...), custom_call_target="tpu_custom_call" | custom-call | tf_op jit(solution)/shard_map/pallas_call | solution.py:519
  587.1 15.1 %collective-permute-done.21 = bf16[4,96,768]{2,1,0:T(8,128)(2,1)S(1)} collective-permute-done((bf16[4,96,768]{2,1,0:T(8,128)(2,1)}, bf16[4,96,768]{2,1,0:T(8,128)(2,1)S(1)}, u32[]{:S(2)}, u32[]{:S(2)}) %collective-permute-start.21) | collective-permute-done | bytes 589856 | tf_op jit(solution)/shard_map/ppermute | solution.py:662
  602.2 17.2 %collective-permute-done.23 = bf16[4,96,768]{2,1,0:T(8,128)(2,1)} collective-permute-done((bf16[4,96,768]{2,1,0:T(8,128)(2,1)S(1)}, bf16[4,96,768]{2,1,0:T(8,128)(2,1)}, u32[]{:S(2)}, u32[]{:S(2)}) %collective-permute-start.23) | collective-permute-done | bytes 589856 | tf_op jit(solution)/shard_map/ppermute | solution.py:662
  637.3 7.9 %collective-permute-done.25 = bf16[4,24,768]{2,1,0:T(8,128)(2,1)S(1)} collective-permute-done((bf16[4,24,768]{2,1,0:T(8,128)(2,1)S(1)}, bf16[4,24,768]{2,1,0:T(8,128)(2,1)S(1)}, u32[]{:S(2)}, u32[]{:S(2)}) %collective-permute-start.25) | collective-permute-done | bytes 147488 | tf_op jit(solution)/shard_map/ppermute | solution.py:662
  646.0 10.8 %shard_map.463 = (f32[1572,768]{1,0:T(8,128)}, f32[24,512]{1,0:T(8,128)}, f32[24,2304]{1,0:T(8,128)}, f32[14,24]{1,0:T(8,128)}, f32[8,128]{1,0:T(8,128)}) custom-call(s32[1,1280]{1,0:T(1,128)} %reshape_reshape.7.wanted_ref, bf16[1280,768]{1,0:T(8,128)(2,1)} %bitcast.46.returned_ref, bf16[1584,768]{1,0:T(8,128)(2,1)} %copy-done.5, ...), custom_call_target="tpu_custom_call" | custom-call | tf_op jit(solution)/shard_map/pallas_call | solution.py:519
  657.5 12.2 %all_to_all.71.every_ref = f32[32,8,128]{2,1,0:T(8,128)} all-to-all(f32[32,8,128]{2,1,0:T(8,128)S(1)} %broadcast_in_dim.167), channel_id=1, replica_groups=mesh['plane'=4,'pair'=2,'fsdp'=4] {'plane','pair','fsdp'}, dimensions={0} | all-to-all | bytes 262144 | tf_op jit(solution)/shard_map/all_to_all | solution.py:1342
  669.7 20.0 %shard_map.464 = (f32[1572,768]{1,0:T(8,128)}, f32[24,512]{1,0:T(8,128)}, f32[24,2304]{1,0:T(8,128)}, f32[24,768]{1,0:T(8,128)}, f32[24,3072]{1,0:T(8,128)}, /*i...) custom-call(f32[32,8,128]{2,1,0:T(8,128)} %all_to_all.71.every_ref, ...), custom_call_target="tpu_custom_call" | custom-call | tf_op jit(solution)/shard_map/pallas_call | solution.py:519
  695.7 6.3 all-to-all-done.10.every_ref
  702.7 10.1 %shard_map.465 = (f32[1572,768]{1,0:T(8,128)}, f32[24,512]{1,0:T(8,128)}, f32[24,2304]{1,0:T(8,128)}, f32[24,768]{1,0:T(8,128)}, f32[24,3072]{1,0:T(8,128)}, /*i...) custom-call(f32[32,8,128]{2,1,0:T(8,128)} %copy-done.11, f32[8,128]{1,0:T(8,128)} %get-tuple-element.474.total_ref, ...), custom_call_target="tpu_custom_call" | custom-call | tf_op jit(solution)/shard_map/pallas_call | solution.py:519
  (195 shorter events, 98.5 us)
Async XLA Ops:
  7.2 6.0 copy-start.4
  7.2 6.2 copy-start.8
  7.2 6.2 copy-start.9
  7.2 199.6 %all-gather.2.cloned.1.call-start = ((), (), s32[]{:S(2)}) async-start(), calls=%async_computation.12 | async-start | bytes 15611904 | tf_op jit(solution)/shard_map/all_gather | solution.py:983
  19.8 107.9 %copy-start.16 = (s32[1024]{0:T(1024)}, s32[1024]{0:T(1024)S(1)}, u32[]{:S(2)}) copy-start(s32[1024]{0:T(1024)S(1)} %add_select_fusion.4) | copy-start | bytes 12292
  21.2 14.6 %all-to-all-start.4 = ((s32[32,1,128]{2,1,0:T(1,128)}), s32[32,1,128]{2,1,0:T(1,128)S(1)}, u32[]{:S(2)}, u32[]{:S(2)}) async-start(s32[32,1,128]{2,1,0:T(1,128)} %bitcast.8), calls=%async_computation.4 | async-start | bytes 32768 | tf_op jit(solution)/shard_map/all_to_all | solution.py:718
  35.8 48.8 %copy-start.12 = (s32[32,1,128]{2,1,0:T(1,128)}, s32[32,1,128]{2,1,0:T(1,128)S(1)}, u32[]{:S(2)}) copy-start(s32[32,1,128]{2,1,0:T(1,128)S(1)} %all-to-all-done.4) | copy-start | bytes 49156
  42.8 84.8 %all-to-all-start.5 = ((bf16[32,40,768]{2,1,0:T(8,128)(2,1)}), bf16[32,40,768]{2,1,0:T(8,128)(2,1)S(1)}, u32[]{:S(2)}, u32[]{:S(2)}) async-start(bf16[32,40,768]{2,1,0:T(8,128)(2,1)} %bitcast.171), calls=%async_computation.5 | async-start | bytes 3932160 | tf_op jit(solution)/shard_map/all_to_all | solution.py:726
  132.6 12.5 %copy-start.22 = (s32[2]{0:T(128)S(1)}, s32[2]{0:T(128)}, u32[]{:S(2)}) copy-start(s32[2]{0:T(128)} %param.33) | copy-start | bytes 28
  132.6 174.1 %all-to-all-start.6 = ((bf16[8,4,128,1664]{3,2,1,0:T(8,128)(2,1)}), bf16[8,4,128,1664]{3,2,1,0:T(8,128)(2,1)}, u32[]{:S(2)}, u32[]{:S(2)}) async-start(bf16[8,4,128,1664]{3,2,1,0:T(8,128)(2,1)} %bitcast.157), calls=%async_computation.6 | async-start | bytes 27262976 | tf_op jit(solution)/shard_map/all_to_all | solution.py:994
  138.2 86.8 %collective-permute-start = (bf16[1584,768]{1,0:T(8,128)(2,1)S(1)}, bf16[1584,768]{1,0:T(8,128)(2,1)}, u32[]{:S(2)}, u32[]{:S(2)}) collective-permute-start(bf16[1584,768]{1,0:T(8,128)(2,1)S(1)} %copy-done.2), channel_id=1, source_target_pairs={{0,1},{1,2},{2,3},{3,0},{4,5},{5,6},{6,7},{7,4},{8,9},{9,10},{10,1... | collective-permute-start | bytes 7299080 | tf_op jit(solution)/shard_map/ppermute | solution.py:1003
  145.0 71.0 %copy-start.19 = (s32[2]{0:T(128)}, s32[2]{0:T(128)S(1)}, u32[]{:S(2)}) copy-start(s32[2]{0:T(128)S(1)} %reduce_sum.103.true_ref) | copy-start | bytes 28
  216.1 9.2 %copy-start.20 = (s32[2,64]{1,0:T(2,128)S(1)}, s32[2,64]{1,0:T(2,128)}, u32[]{:S(2)}) copy-start(s32[2,64]{1,0:T(2,128)} %param.34) | copy-start | bytes 1540
  225.0 51.9 %collective-permute-start.1 = (bf16[1584,768]{1,0:T(8,128)(2,1)}, bf16[1584,768]{1,0:T(8,128)(2,1)}, u32[]{:S(2)}, u32[]{:S(2)}) collective-permute-start(bf16[1584,768]{1,0:T(8,128)(2,1)} %collective-permute-done.refs_1_), channel_id=1, source_target_pairs={{0,1},{1,2},{2,3},{3,0},{4,5},{5,6},{6,7},{7,4},{8,9},{9,10},{10,1... | collective-permute-start | bytes 7299080 | tf_op jit(solution)/shard_map/ppermute | solution.py:1012
  276.8 13.1 %collective-permute-start.2 = (bf16[128,768]{1,0:T(8,128)(2,1)}, bf16[128,768]{1,0:T(8,128)(2,1)S(1)}, u32[]{:S(2)}, u32[]{:S(2)}) collective-permute-start(bf16[128,768]{1,0:T(8,128)(2,1)} %get-tuple-element.402), channel_id=1, source_target_pairs={{0,4},{4,0},{8,12},{12,8},{16,20},{20,16},{24,28},{28,24},{1,5},{5... | collective-permute-start | bytes 589832 | tf_op jit(solution)/shard_map/ppermute | solution.py:1110
  282.8 10.1 %collective-permute-start.3 = (bf16[128,768]{1,0:T(8,128)(2,1)}, bf16[128,768]{1,0:T(8,128)(2,1)S(1)}, u32[]{:S(2)}, u32[]{:S(2)}) collective-permute-start(bf16[128,768]{1,0:T(8,128)(2,1)} %get-tuple-element.402), channel_id=1, source_target_pairs={{0,8},{4,12},{8,0},{12,4},{16,24},{20,28},{24,16},{28,20},{1,9},{5... | collective-permute-start | bytes 589832 | tf_op jit(solution)/shard_map/ppermute | solution.py:1110
  283.7 12.8 %collective-permute-start.4 = (bf16[128,768]{1,0:T(8,128)(2,1)}, bf16[128,768]{1,0:T(8,128)(2,1)S(1)}, u32[]{:S(2)}, u32[]{:S(2)}) collective-permute-start(bf16[128,768]{1,0:T(8,128)(2,1)} %get-tuple-element.402), channel_id=1, source_target_pairs={{0,12},{4,8},{8,4},{12,0},{16,28},{20,24},{24,20},{28,16},{1,13},{... | collective-permute-start | bytes 589832 | tf_op jit(solution)/shard_map/ppermute | solution.py:1110
  284.2 18.1 %collective-permute-start.5 = (bf16[128,768]{1,0:T(8,128)(2,1)}, bf16[128,768]{1,0:T(8,128)(2,1)S(1)}, u32[]{:S(2)}, u32[]{:S(2)}) collective-permute-start(bf16[128,768]{1,0:T(8,128)(2,1)} %get-tuple-element.402), channel_id=1, source_target_pairs={{0,16},{4,20},{8,24},{12,28},{16,0},{20,4},{24,8},{28,12},{1,17},{... | collective-permute-start | bytes 589832 | tf_op jit(solution)/shard_map/ppermute | solution.py:1110
  288.9 17.4 %collective-permute-start.6 = (bf16[128,768]{1,0:T(8,128)(2,1)}, bf16[128,768]{1,0:T(8,128)(2,1)S(1)}, u32[]{:S(2)}, u32[]{:S(2)}) collective-permute-start(bf16[128,768]{1,0:T(8,128)(2,1)} %get-tuple-element.402), channel_id=1, source_target_pairs={{0,20},{4,16},{8,28},{12,24},{16,4},{20,0},{24,12},{28,8},{1,21},{... | collective-permute-start | bytes 589832 | tf_op jit(solution)/shard_map/ppermute | solution.py:1110
  289.9 16.4 %collective-permute-start.7 = (bf16[128,768]{1,0:T(8,128)(2,1)}, bf16[128,768]{1,0:T(8,128)(2,1)S(1)}, u32[]{:S(2)}, u32[]{:S(2)}) collective-permute-start(bf16[128,768]{1,0:T(8,128)(2,1)} %get-tuple-element.402), channel_id=1, source_target_pairs={{0,24},{4,28},{8,16},{12,20},{16,8},{20,12},{24,0},{28,4},{1,25},{... | collective-permute-start | bytes 589832 | tf_op jit(solution)/shard_map/ppermute | solution.py:1110
  292.9 13.5 %collective-permute-start.8 = (bf16[128,768]{1,0:T(8,128)(2,1)}, bf16[128,768]{1,0:T(8,128)(2,1)S(1)}, u32[]{:S(2)}, u32[]{:S(2)}) collective-permute-start(bf16[128,768]{1,0:T(8,128)(2,1)} %get-tuple-element.402), channel_id=1, source_target_pairs={{0,28},{4,24},{8,20},{12,16},{16,12},{20,8},{24,4},{28,0},{1,29},{... | collective-permute-start | bytes 589832 | tf_op jit(solution)/shard_map/ppermute | solution.py:1110
  296.5 59.2 %collective-permute-start.10 = (bf16[1584,768]{1,0:T(8,128)(2,1)}, bf16[1584,768]{1,0:T(8,128)(2,1)}, u32[]{:S(2)}, u32[]{:S(2)}) collective-permute-start(bf16[1584,768]{1,0:T(8,128)(2,1)} %collective-permute-done.1.refs_2_), channel_id=1, source_target_pairs={{0,1},{1,2},{2,3},{3,0},{4,5},{5,6},{6,7},{7,4},{8,9},{9,10},{10,1... | collective-permute-start | bytes 7299080 | tf_op jit(solution)/shard_map/ppermute | solution.py:1012
  333.4 11.7 %copy-start.21 = (s32[4]{0:T(128)S(1)}, s32[4]{0:T(128)}, u32[]{:S(2)}) copy-start(s32[4]{0:T(128)} %compare_select_fusion) | copy-start | bytes 52
  340.1 67.8 %collective-permute-start.9 = (bf16[1584,768]{1,0:T(8,128)(2,1)}, bf16[1584,768]{1,0:T(8,128)(2,1)}, u32[]{:S(2)}, u32[]{:S(2)}) collective-permute-start(bf16[1584,768]{1,0:T(8,128)(2,1)} %shard_map.455), channel_id=1, source_target_pairs={{0,1},{1,2},{2,3},{3,0},{4,5},{5,6},{6,7},{7,4},{8,9},{9,10},{10,1... | collective-permute-start | bytes 7299080 | tf_op jit(solution)/shard_map/ppermute | solution.py:1134
  369.8 38.1 %all-to-all-start.7 = ((bf16[8,128,768]{2,1,0:T(8,128)(2,1)}), bf16[8,128,768]{2,1,0:T(8,128)(2,1)S(1)}, u32[]{:S(2)}, u32[]{:S(2)}) async-start(bf16[8,128,768]{2,1,0:T(8,128)(2,1)} %bitcast.175), calls=%async_computation.7 | async-start | bytes 3145728 | tf_op jit(solution)/shard_map/all_to_all | solution.py:1136
  412.9 57.2 %collective-permute-start.11 = (bf16[1584,768]{1,0:T(8,128)(2,1)}, bf16[1584,768]{1,0:T(8,128)(2,1)}, u32[]{:S(2)}, u32[]{:S(2)}) collective-permute-start(bf16[1584,768]{1,0:T(8,128)(2,1)} %add_convert_fusion.3), channel_id=1, source_target_pairs={{0,1},{1,2},{2,3},{3,0},{4,5},{5,6},{6,7},{7,4},{8,9},{9,10},{10,1... | collective-permute-start | bytes 7299080 | tf_op jit(solution)/shard_map/ppermute | solution.py:1160
  432.1 38.1 %copy-start.6 = (bf16[1584,768]{1,0:T(8,128)(2,1)S(1)}, bf16[1584,768]{1,0:T(8,128)(2,1)}, u32[]{:S(2)}) copy-start(bf16[1584,768]{1,0:T(8,128)(2,1)} %get-tuple-element.435) | copy-start | bytes 7299076
  470.2 9.1 %collective-permute-start.12 = (bf16[9,4,96,768]{3,2,1,0:T(8,128)(2,1)}, bf16[9,4,96,768]{3,2,1,0:T(8,128)(2,1)}, u32[]{:S(2)}, u32[]{:S(2)}) collective-permute-start(bf16[9,4,96,768]{3,2,1,0:T(8,128)(2,1)} %get-tuple-element.428), channel_id=1, source_target_pairs={{0,4},{4,0},{1,5},{5,1},{2,6},{6,2},{3,7},{7,3},{8,12},{12,8},{9,1... | collective-permute-start | bytes 15925256 | tf_op jit(solution)/shard_map/ppermute | solution.py:671
  474.0 57.6 %collective-permute-start.13 = (bf16[1584,768]{1,0:T(8,128)(2,1)}, bf16[1584,768]{1,0:T(8,128)(2,1)S(1)}, u32[]{:S(2)}, u32[]{:S(2)}) collective-permute-start(bf16[1584,768]{1,0:T(8,128)(2,1)} %add_convert_fusion.2), channel_id=1, source_target_pairs={{0,1},{1,2},{2,3},{3,0},{4,5},{5,6},{6,7},{7,4},{8,9},{9,10},{10,1... | collective-permute-start | bytes 7299080 | tf_op jit(solution)/shard_map/ppermute | solution.py:1160
  488.9 53.2 %collective-permute-start.14 = (bf16[9,96,768]{2,1,0:T(8,128)(2,1)}, bf16[9,96,768]{2,1,0:T(8,128)(2,1)}, u32[]{:S(2)}, u32[]{:S(2)}) collective-permute-start(bf16[9,96,768]{2,1,0:T(8,128)(2,1)} %get-tuple-element.551), channel_id=1, source_target_pairs={{0,8},{8,0},{16,24},{24,16},{1,9},{9,1},{17,25},{25,17},{2,10},{10... | collective-permute-start | bytes 3981320 | tf_op jit(solution)/shard_map/ppermute | solution.py:662
  488.9 59.3 %collective-permute-start.15 = (bf16[9,96,768]{2,1,0:T(8,128)(2,1)}, bf16[9,96,768]{2,1,0:T(8,128)(2,1)}, u32[]{:S(2)}, u32[]{:S(2)}) collective-permute-start(bf16[9,96,768]{2,1,0:T(8,128)(2,1)} %get-tuple-element.553), channel_id=1, source_target_pairs={{0,16},{8,24},{16,0},{24,8},{1,17},{9,25},{17,1},{25,9},{2,18},{10... | collective-permute-start | bytes 3981320 | tf_op jit(solution)/shard_map/ppermute | solution.py:662
  491.0 58.7 %collective-permute-start.16 = (bf16[9,96,768]{2,1,0:T(8,128)(2,1)}, bf16[9,96,768]{2,1,0:T(8,128)(2,1)}, u32[]{:S(2)}, u32[]{:S(2)}) collective-permute-start(bf16[9,96,768]{2,1,0:T(8,128)(2,1)} %get-tuple-element.552), channel_id=1, source_target_pairs={{0,24},{8,16},{16,8},{24,0},{1,25},{9,17},{17,9},{25,1},{2,26},{10... | collective-permute-start | bytes 3981320 | tf_op jit(solution)/shard_map/ppermute | solution.py:662
  531.6 10.5 %copy-start.5 = (bf16[1584,768]{1,0:T(8,128)(2,1)}, bf16[1584,768]{1,0:T(8,128)(2,1)S(1)}, u32[]{:S(2)}) copy-start(bf16[1584,768]{1,0:T(8,128)(2,1)S(1)} %collective-permute-done.13.moved_ref) | copy-start | bytes 7299076
  542.1 10.9 %copy-start.17 = (s32[1024]{0:T(1024)S(1)}, s32[1024]{0:T(1024)}, u32[]{:S(2)}) copy-start(s32[1024]{0:T(1024)} %copy-done.16) | copy-start | bytes 12292
  559.0 69.4 %all-to-all-start.8 = ((bf16[32,40,768]{2,1,0:T(8,128)(2,1)}), bf16[32,40,768]{2,1,0:T(8,128)(2,1)}, u32[]{:S(2)}, u32[]{:S(2)}) async-start(bf16[32,40,768]{2,1,0:T(8,128)(2,1)} %bitcast.169), calls=%async_computation.8 | async-start | bytes 3932160 | tf_op jit(solution)/shard_map/all_to_all | solution.py:757
  562.4 58.6 %reduce-scatter.4.cloned.1.call-start = ((), (), s32[]{:S(2)}) async-start(), calls=%async_computation.13 | async-start | bytes 1658880
  574.6 6.5 copy-start.7
  576.5 2.1 collective-permute-start.17
  576.6 2.8 collective-permute-start.18
  577.1 3.2 collective-permute-start.19
  577.1 3.9 collective-permute-start.20
  582.9 19.3 %collective-permute-start.21 = (bf16[4,96,768]{2,1,0:T(8,128)(2,1)}, bf16[4,96,768]{2,1,0:T(8,128)(2,1)S(1)}, u32[]{:S(2)}, u32[]{:S(2)}) collective-permute-start(bf16[4,96,768]{2,1,0:T(8,128)(2,1)} %get-tuple-element.556), channel_id=1, source_target_pairs={{0,8},{8,0},{16,24},{24,16},{1,9},{9,1},{17,25},{25,17},{2,10},{10... | collective-permute-start | bytes 1769480 | tf_op jit(solution)/shard_map/ppermute | solution.py:662
  584.5 17.7 %collective-permute-start.22 = (bf16[4,96,768]{2,1,0:T(8,128)(2,1)}, bf16[4,96,768]{2,1,0:T(8,128)(2,1)}, u32[]{:S(2)}, u32[]{:S(2)}) collective-permute-start(bf16[4,96,768]{2,1,0:T(8,128)(2,1)} %get-tuple-element.558), channel_id=1, source_target_pairs={{0,16},{8,24},{16,0},{24,8},{1,17},{9,25},{17,1},{25,9},{2,18},{10... | collective-permute-start | bytes 1769480 | tf_op jit(solution)/shard_map/ppermute | solution.py:662
  586.0 33.5 %collective-permute-start.23 = (bf16[4,96,768]{2,1,0:T(8,128)(2,1)S(1)}, bf16[4,96,768]{2,1,0:T(8,128)(2,1)}, u32[]{:S(2)}, u32[]{:S(2)}) collective-permute-start(bf16[4,96,768]{2,1,0:T(8,128)(2,1)S(1)} %get-tuple-element.557), channel_id=1, source_target_pairs={{0,24},{8,16},{16,8},{24,0},{1,25},{9,17},{17,9},{25,1},{2,26},{10... | collective-permute-start | bytes 1769480 | tf_op jit(solution)/shard_map/ppermute | solution.py:662
  628.4 9.0 %collective-permute-start.24 = (bf16[4,24,768]{2,1,0:T(8,128)(2,1)S(1)}, bf16[4,24,768]{2,1,0:T(8,128)(2,1)S(1)}, u32[]{:S(2)}, u32[]{:S(2)}) collective-permute-start(bf16[4,24,768]{2,1,0:T(8,128)(2,1)S(1)} %get-tuple-element.565), channel_id=1, source_target_pairs={{0,1},{1,0},{2,3},{3,2},{4,5},{5,4},{6,7},{7,6},{8,9},{9,8},{10,11... | collective-permute-start | bytes 442376 | tf_op jit(solution)/shard_map/ppermute | solution.py:662
  631.9 13.4 %collective-permute-start.25 = (bf16[4,24,768]{2,1,0:T(8,128)(2,1)S(1)}, bf16[4,24,768]{2,1,0:T(8,128)(2,1)S(1)}, u32[]{:S(2)}, u32[]{:S(2)}) collective-permute-start(bf16[4,24,768]{2,1,0:T(8,128)(2,1)S(1)} %get-tuple-element.567), channel_id=1, source_target_pairs={{0,2},{1,3},{2,0},{3,1},{4,6},{5,7},{6,4},{7,5},{8,10},{9,11},{10,... | collective-permute-start | bytes 442376 | tf_op jit(solution)/shard_map/ppermute | solution.py:662
  632.0 13.3 %collective-permute-start.26 = (bf16[4,24,768]{2,1,0:T(8,128)(2,1)S(1)}, bf16[4,24,768]{2,1,0:T(8,128)(2,1)S(1)}, u32[]{:S(2)}, u32[]{:S(2)}) collective-permute-start(bf16[4,24,768]{2,1,0:T(8,128)(2,1)S(1)} %get-tuple-element.566), channel_id=1, source_target_pairs={{0,3},{1,2},{2,1},{3,0},{4,7},{5,6},{6,5},{7,4},{8,11},{9,10},{10,... | collective-permute-start | bytes 442376 | tf_op jit(solution)/shard_map/ppermute | solution.py:662
  691.0 11.0 %all-to-all-start.10 = ((f32[32,8,128]{2,1,0:T(8,128)}), f32[32,8,128]{2,1,0:T(8,128)S(1)}, u32[]{:S(2)}, u32[]{:S(2)}) async-start(f32[32,8,128]{2,1,0:T(8,128)} %broadcast_in_dim.168), calls=%async_computation.10 | async-start | bytes 262144 | tf_op jit(solution)/shard_map/all_to_all | solution.py:1342
  (10 other events, 36.7 us)
Sparse Core Ops, SparseCore 0:
  14.4 192.3 all-gather.1
  565.6 53.4 reduce-scatter.3
where the time goes:
time: 732 us; the launch traced here: 721 us
  waiting for transfers between devices  286 us (39%)
  Pallas kernels  225 us (31%)
  starting transfers between devices  81 us (11%)
  other arithmetic  50.5 us (7%)
  local copies, waits for them, and re-layouts  31.5 us (4%)
  between operations  17 us (2%)
  matrix products  16.1 us (2%)
  blocking collectives  12.2 us (2%)
    pallas_call x11, Pallas kernels, row_kernel(): pl.pallas_call(kernel, out_shape=tuple((jax.ShapeDtypeStruct(shape, kind)...  142 us
    all_gather x1, waiting for transfers between devices, on_device(): gathered = lax.all_gather(packed_low, axes, axis=0, tiled=True)  61.2 us
    ppermute x9, waiting for transfers between devices, sum_over_peers(): lax.ppermute(given, axis, [(peer, peer ^ apart) for peer in range(size)])  50.3 us
    ppermute x2, waiting for transfers between devices, pass_sum(): head_sums.append(lax.ppermute(total.astype(bf16), 'fsdp', ring))  46.9 us
    ppermute x2, waiting for transfers between devices, pass_table(): tables.append(lax.ppermute(newest, 'fsdp', ring))  43.4 us
    all_to_all x1, waiting for transfers between devices, ask_rows(): lax.all_to_all(rows.reshape(n_dev, room, -1), axes, split_axis=0, concat_...  42.4 us
    pallas_call x2, Pallas kernels, head_products(): pl.pallas_call(functools.partial(head_kernel, steps), out_shape=(jax.Shap...  39.6 us
    pallas_call x1, Pallas kernels, parcels_of(): pl.pallas_call(functools.partial(parcel_kernel, own_rows, tiles, wide), o...  24.3 us
  transfers between devices with their start and end apart: 35, of which 23 were waited for; matrix products, arithmetic and copies ran while one was open for 10% of the time, Pallas kernels for 26%

commit v1 on v0

--- a/solution.py
+++ b/solution.py
@@ -1036,6 +1036,7 @@
     def weight(width, place):
         return (gathered, (row_width, width), lambda *_: (0, place))
 
+    (gathered,) = pass_table(gathered)
     vectors = weight(gain_width, pack_width // gain_width)
     qkv_weight = weight(3 * row_width, 0)
     out_weight = weight(row_width, 3)
@@ -1059,7 +1060,6 @@
         (n_block, seq_count),
     )
     mixed_output = attend(lengths, packed)
-    (mixed_output,) = pass_table(mixed_output)
     up_bias = hidden_order(
         gathered[:, pack_width + 10 : pack_width + 14].astype(f32).T.reshape(1, -1), row_width
     )
@@ -1104,16 +1104,7 @@
 
     if n_fs > 2:
         (chosen,) = pass_table(chosen)
-    by_distance = jnp.stack(
-        [chosen]
-        + [
-            lax.ppermute(chosen, SPLIT, [(p, p ^ apart) for p in range(n_dp)])
-            for apart in range(1, n_dp)
-        ]
-    )
-    all_chosen = jnp.concatenate(
-        [lax.dynamic_index_in_dim(by_distance, i_dp ^ p, 0, False) for p in range(n_dp)]
-    )
+    all_chosen = lax.all_gather(chosen, SPLIT, axis=0, tiled=True)
     while len(tables) < n_fs:
         (all_chosen,) = pass_table(all_chosen)
     slopes, chosen_part, head_loss = head_products(
@@ -1299,7 +1290,7 @@
         (late_kept, late_given, own_part)
     )
     last = sum_in_plane(sum_in_pair(late_kept, late_given, 4))
-    returned, last = lax.optimization_barrier((returned, last))
+    early, last = lax.optimization_barrier((early, last))
     last = sum_in_line(last)
     early_grads = (
         early[0],

time: 732 us -> 709 us (0.969)
  starting transfers between devices: 81 us -> 59.2 us
  waiting for transfers between devices: 286 us -> 267 us
  Pallas kernels: 225 us -> 241 us
    ppermute x1, waiting for transfers between devices: 0.01 us -> 58.2 us  [on_device(): tables = [first_table, lax.ppermute(first_table, 'fsdp', ring)]]
    all_gather x1, waiting for transfers between devices: 61.2 us -> 3.6 us  [on_device(): gathered = lax.all_gather(packed_low, axes, axis=0, tiled=True)]
    ppermute x2, waiting for transfers between devices: 43.4 us -> 12.2 us  [pass_table(): tables.append(lax.ppermute(newest, 'fsdp', ring))]
    all_to_all x1, waiting for transfers between devices: 0.01 us -> 24 us  [on_device(): lax.all_to_all(targets.reshape(n_dp, n_fs, n_pick, lanes), SPLIT, split_a...]
    ppermute x7 -> x0, starting transfers between devices: 17 us -> none  [on_device(): lax.ppermute(chosen, SPLIT, [(p, p ^ apart) for p in range(n_dp)])]
    pallas_call x11, Pallas kernels: 142 us -> 152 us  [row_kernel(): pl.pallas_call(kernel, out_shape=tuple((jax.ShapeDtypeStruct(shape, kind)...]
    all_gather x0 -> x1, waiting for transfers between devices: none -> 7.98 us  [on_device(): all_chosen = lax.all_gather(chosen, SPLIT, axis=0, tiled=True)]
    ppermute x2, waiting for transfers between devices: 46.9 us -> 38.9 us  [pass_sum(): head_sums.append(lax.ppermute(total.astype(bf16), 'fsdp', ring))]
  transfers between devices with their start and end apart: 35 -> 29, of which waited for: 23 -> 21; matrix products, arithmetic and copies ran while one was open for 10% -> 10% of each run, Pallas kernels for 26% -> 29%
where the time goes in v1:
time: 709 us; the launch traced here: 698 us
  waiting for transfers between devices  267 us (38%)
  Pallas kernels  241 us (34%)
  starting transfers between devices  59.2 us (8%)
  other arithmetic  51 us (7%)
  local copies, waits for them, and re-layouts  32.6 us (5%)
  between operations  16.6 us (2%)
  matrix products  16.1 us (2%)
  blocking collectives  13.2 us (2%)
    pallas_call x11, Pallas kernels, row_kernel(): pl.pallas_call(kernel, out_shape=tuple((jax.ShapeDtypeStruct(shape, kind)...  152 us
    ppermute x1, waiting for transfers between devices, on_device(): tables = [first_table, lax.ppermute(first_table, 'fsdp', ring)]  58.2 us
    ppermute x9, waiting for transfers between devices, sum_over_peers(): lax.ppermute(given, axis, [(peer, peer ^ apart) for peer in range(size)])  47.3 us
    all_to_all x1, waiting for transfers between devices, ask_rows(): lax.all_to_all(rows.reshape(n_dev, room, -1), axes, split_axis=0, concat_...  42.4 us
    pallas_call x2, Pallas kernels, head_products(): pl.pallas_call(functools.partial(head_kernel, steps), out_shape=(jax.Shap...  39.6 us
    ppermute x2, waiting for transfers between devices, pass_sum(): head_sums.append(lax.ppermute(total.astype(bf16), 'fsdp', ring))  38.9 us
    pallas_call x2, Pallas kernels, attend(): pl.pallas_call(mix_kernel if forward else unmix_kernel, out_shape=out if...  25.4 us
    pallas_call x1, Pallas kernels, parcels_of(): pl.pallas_call(functools.partial(parcel_kernel, own_rows, tiles, wide), o...  24.3 us
  transfers between devices with their start and end apart: 29, of which 21 were waited for; matrix products, arithmetic and copies ran while one was open for 10% of the time, Pallas kernels for 29%

profile of v1, /device:TPU:0, one launch (start us, length us, event | category | flops | bytes accessed | tf_op | source)
XLA Modules:
  0.0 698.3 jit_solution(1905652861648429747)
XLA Ops:
  21.2 7.3 %all-to-all-start.4 = ((s32[32,1,128]{2,1,0:T(1,128)}), s32[32,1,128]{2,1,0:T(1,128)S(1)}, u32[]{:S(2)}, u32[]{:S(2)}) async-start(s32[32,1,128]{2,1,0:T(1,128)} %bitcast.8), calls=%async_computation.4 | async-start | bytes 32768 | tf_op jit(solution)/shard_map/all_to_all | solution.py:718
  28.5 7.1 %multiply_reduce_fusion = (f32[]{:T(128)}, bf16[1572,768]{1,0:T(8,128)(2,1)}) fusion(f32[1572,768]{1,0:T(8,128)} %refs_0_.3), kind=kLoop, calls=%fused_computation.35 | loop fusion | flops 3621887 | bytes 7243780 | tf_op jit(solution)/shard_map/reduce_sum | solution.py:999
  35.9 6.9 fusion.17
  42.8 5.6 all-to-all-start.5
  48.5 24.3 %shard_map.450 = bf16[32,128,1664]{2,1,0:T(8,128)(2,1)} custom-call(bf16[128,50304]{1,0:T(8,128)(2,1)} %bitcast.129), custom_call_target="tpu_custom_call" | custom-call | tf_op jit(solution)/shard_map/pallas_call | solution.py:581
  78.7 5.8 select_add_fusion.tile_ref
  85.3 42.4 %all-to-all-done.5 = bf16[32,40,768]{2,1,0:T(8,128)(2,1)S(1)} async-done(((bf16[32,40,768]{2,1,0:T(8,128)(2,1)}), bf16[32,40,768]{2,1,0:T(8,128)(2,1)S(1)}, u32[]{:S(2)}, u32[]{:S(2)}) %all-to-all-start.5) | async-done | bytes 1966112 | tf_op jit(solution)/shard_map/all_to_all | solution.py:726
  127.7 4.1 fusion.13
  132.7 5.6 all-to-all-start.6
  138.3 6.7 collective-permute-start
  145.0 58.2 %collective-permute-done.refs_1_ = bf16[1584,768]{1,0:T(8,128)(2,1)} collective-permute-done((bf16[1584,768]{1,0:T(8,128)(2,1)S(1)}, bf16[1584,768]{1,0:T(8,128)(2,1)}, u32[]{:S(2)}, u32[]{:S(2)}) %collective-permute-start) | collective-permute-done | bytes 2433056 | tf_op jit(solution)/shard_map/ppermute | solution.py:1003
  203.2 3.6 all-gather.3.cloned.1.call-done.place_ref.vector_ref.weight_ref.out_ref.up_ref.down_ref
  208.5 10.3 %shard_map.451 = (f32[1024,768]{1,0:T(8,128)}, f32[1024,768]{1,0:T(8,128)}, bf16[1024,768]{1,0:T(8,128)(2,1)}, bf16[1024,2304]{1,0:T(8,128)(2,1)}) custom-call(s32[2]{0:T(128)} %compare_select_fusion.2.length_ref, f32[1024,768]{1,0:T(8,128)} %get-tuple-element.394.token_ref, ...), custom_call_target="tpu_custom_call" | custom-call | tf_op jit(solution)/shard_map/pallas_call | solution.py:519
  218.8 11.9 %shard_map.452.mixed_ref = bf16[1024,768]{1,0:T(8,128)(2,1)} custom-call(s32[2]{0:T(128)} %compare_select_fusion.2.length_ref, bf16[1024,2304]{1,0:T(8,128)(2,1)} %get-tuple-element.397.query_ref.key_ref.value_ref, bf16[1024,2304]{1,0:T(8,128)(2,1)} %get-tuple-element.397.query_ref.key_ref.value_ref, ...), custom_call_target="tpu_custom_call" | custom-call | tf_op jit(solution)/shard_map/pallas_call | solution.py:170
  233.1 18.8 %shard_map.453 = (f32[1024,768]{1,0:T(8,128)}, bf16[1024,768]{1,0:T(8,128)(2,1)}, bf16[1024,3072]{1,0:T(8,128)(2,1)}, bf16[1024,3072]{1,0:T(8,128)(2,1)}, f32[10...) custom-call(s32[2]{0:T(128)} %compare_select_fusion.2.length_ref, ...), custom_call_target="tpu_custom_call" | custom-call | tf_op jit(solution)/shard_map/pallas_call | solution.py:519
  251.9 12.1 %collective-permute-done.1.refs_2_ = bf16[1584,768]{1,0:T(8,128)(2,1)S(1)} collective-permute-done((bf16[1584,768]{1,0:T(8,128)(2,1)}, bf16[1584,768]{1,0:T(8,128)(2,1)S(1)}, u32[]{:S(2)}, u32[]{:S(2)}) %collective-permute-start.1) | collective-permute-done | bytes 2433056 | tf_op jit(solution)/shard_map/ppermute | solution.py:1012
  266.5 24.0 %all-to-all-done.6.target_ref = bf16[8,4,128,1664]{3,2,1,0:T(8,128)(2,1)} async-done(((bf16[8,4,128,1664]{3,2,1,0:T(8,128)(2,1)}), bf16[8,4,128,1664]{3,2,1,0:T(8,128)(2,1)}, u32[]{:S(2)}, u32[]{:S(2)}) %all-to-all-start.6) | async-done | bytes 13631520 | tf_op jit(solution)/shard_map/all_to_all | solution.py:994
  290.6 8.0 %all-gather.5.cloned.1.call-done.chosen_ref = bf16[1024,768]{1,0:T(8,128)(2,1)} async-done(((bf16[128,768]{1,0:T(8,128)(2,1)}), bf16[1024,768]{1,0:T(8,128)(2,1)}) %all-gather.5.cloned.1.call-update) | async-done | bytes 1572880 | tf_op jit(solution)/shard_map/all_gather | solution.py:1107
  298.6 25.6 %shard_map.454 = (bf16[3,1024,1584]{2,1,0:T(8,128)(2,1)}, f32[1024,768]{1,0:T(8,128)}, f32[8,1584]{1,0:T(8,128)}) custom-call(s32[3]{0:T(128)} %bitcast.164, bf16[1024,768]{1,0:T(8,128)(2,1)} %all-gather.5.cloned.1.call-done.chosen_ref, bf16[8,4,128,1664]{3,2,1,0:T(8,128)(2,1)} %all-to-all-done.6.target_ref, bf16[1584,768]{1,0:T(8,128)(2,1)} %pad.18.refs_0_, ...), custom_call_target="tpu_custom_call" | custom-call | tf_op jit(solution)/shard_map/pallas_call | solution.py:630
  324.2 6.7 shard_map.455
  330.9 4.4 collective-permute-start.2
  337.2 14.0 %shard_map.456 = (bf16[1,1024,1584]{2,1,0:T(8,128)(2,1)}, bf16[1024,768]{1,0:T(8,128)(2,1)}, f32[8,1584]{1,0:T(8,128)}) custom-call(s32[1]{0:T(128)} %slice.67.place_ref, bf16[1024,768]{1,0:T(8,128)(2,1)} %all-gather.5.cloned.1.call-done.chosen_ref, bf16[8,4,128,1664]{3,2,1,0:T(8,128)(2,1)} %all-to-all-done.6.target_ref, bf16[1584,768]{1,0:T(8,128)(2,1)} %copy-done.6, ...), custom_call_target="tpu_custom_call" | custom-call | tf_op jit(solution)/shard_map/pallas_call | solution.py:630
  351.2 3.8 all-to-all-start.7
  355.0 14.8 %shard_map.457 = (bf16[1584,768]{1,0:T(8,128)(2,1)}, bf16[1584,768]{1,0:T(8,128)(2,1)}, bf16[1584,768]{1,0:T(8,128)(2,1)}) custom-call(bf16[3,1024,1584]{2,1,0:T(8,128)(2,1)} %get-tuple-element.404.slope_ref, bf16[1,1024,1584]{2,1,0:T(8,128)(2,1)} %get-tuple-element.410.last_ref, bf16[1024,768]{1,0:T(8,128)(2,1)} %all-gather.5.cloned.1.call-done.chosen_ref), custom_call_target="tpu_custom_call" | custom-call | tf_op jit(solution)/shard_map/pallas_call | solution.py:519
  369.8 6.1 all-to-all-done.7.head_ref
  376.0 12.1 %collective-permute-done.2 = bf16[1584,768]{1,0:T(8,128)(2,1)} collective-permute-done((bf16[1584,768]{1,0:T(8,128)(2,1)}, bf16[1584,768]{1,0:T(8,128)(2,1)}, u32[]{:S(2)}, u32[]{:S(2)}) %collective-permute-start.2) | collective-permute-done | bytes 2433056 | tf_op jit(solution)/shard_map/ppermute | solution.py:1125
  388.1 4.5 add_convert_fusion.3
  395.2 20.2 %shard_map.458 = (f32[1024,768]{1,0:T(8,128)}, f32[1024,768]{1,0:T(8,128)}, bf16[1024,768]{1,0:T(8,128)(2,1)}, bf16[1024,768]{1,0:T(8,128)(2,1)}, bf16[1024,768]...) custom-call(s32[2]{0:T(128)} %compare_select_fusion.2.length_ref, ...), custom_call_target="tpu_custom_call" | custom-call | tf_op jit(solution)/shard_map/pallas_call | solution.py:519
  415.4 20.0 %shard_map.459 = (bf16[9,4,96,768]{3,2,1,0:T(8,128)(2,1)}, bf16[9,4,96,768]{3,2,1,0:T(8,128)(2,1)}) custom-call(s32[1]{0:T(128)} %bitcast.22.member_ref, bf16[1024,768]{1,0:T(8,128)(2,1)} %shard_map.452.mixed_ref, bf16[1024,768]{1,0:T(8,128)(2,1)} %get-tuple-element.420.attention_ref, bf16[1024,768]{1,0:T(8,128)(2,1)} %get-tuple-element.421.normed_ref, ...), custom_call_target="tpu_custom_call" | custom-call | tf_op jit(solution)/shard_map/pallas_call | solution.py:519
  435.4 13.7 %collective-permute-done.4 = bf16[1584,768]{1,0:T(8,128)(2,1)} collective-permute-done((bf16[1584,768]{1,0:T(8,128)(2,1)}, bf16[1584,768]{1,0:T(8,128)(2,1)}, u32[]{:S(2)}, u32[]{:S(2)}) %collective-permute-start.4) | collective-permute-done | bytes 2433056 | tf_op jit(solution)/shard_map/ppermute | solution.py:1151
  449.1 3.8 add_convert_fusion.2
  454.5 3.7 collective-permute-done.5
  458.2 6.1 add_convert_fusion.1
  471.8 13.5 %shard_map.460 = (bf16[1024,768]{1,0:T(8,128)(2,1)}, bf16[1024,768]{1,0:T(8,128)(2,1)}, bf16[1024,768]{1,0:T(8,128)(2,1)}) custom-call(s32[2]{0:T(128)} %compare_select_fusion.2.length_ref, bf16[1024,2304]{1,0:T(8,128)(2,1)} %get-tuple-element.397.query_ref.key_ref.value_ref, bf16[1024,2304]{1,0:T(8,128)(2,1)} %get-tuple-element.397.query_ref.key_ref.value_ref, ...), custom_call_target="tpu_custom_call" | custom-call | tf_op jit(solution)/shard_map/pallas_call | solution.py:170
  485.3 25.2 %collective-permute-done.6.moved_ref = bf16[1584,768]{1,0:T(8,128)(2,1)S(1)} collective-permute-done((bf16[1584,768]{1,0:T(8,128)(2,1)}, bf16[1584,768]{1,0:T(8,128)(2,1)S(1)}, u32[]{:S(2)}, u32[]{:S(2)}) %collective-permute-start.6) | collective-permute-done | bytes 2433056 | tf_op jit(solution)/shard_map/ppermute | solution.py:1151
  510.5 11.4 %shard_map.461 = (bf16[1024,768]{1,0:T(8,128)(2,1)}, bf16[768,512]{1,0:T(8,128)(2,1)}, f32[4,8,768]{2,1,0:T(8,128)}) custom-call(s32[2]{0:T(128)} %compare_select_fusion.2.length_ref, s32[2]{0:T(128)} %compare_convert_fusion.keep_ref, bf16[1024,768]{1,0:T(8,128)(2,1)} %get-tuple-element.448.query_ref, bf16[1024,768]{1,0:T(8,128)(2,1)} %get-tuple-element.449.key_ref, ...), custom_call_target="tpu_custom_call" | custom-call | tf_op jit(solution)/shard_map/pallas_call | solution.py:519
  521.9 6.9 collective-permute-done.8
  532.1 5.1 fusion.18
  544.5 9.1 %shard_map.462 = (bf16[4,4,96,768]{3,2,1,0:T(8,128)(2,1)}, bf16[4,4,96,768]{3,2,1,0:T(8,128)(2,1)}) custom-call(s32[1]{0:T(128)} %bitcast.22.member_ref, bf16[1024,768]{1,0:T(8,128)(2,1)} %get-tuple-element.447.low_ref, bf16[1024,768]{1,0:T(8,128)(2,1)} %get-tuple-element.448.query_ref, bf16[1024,768]{1,0:T(8,128)(2,1)} %get-tuple-element.449.key_ref, ...), custom_call_target="tpu_custom_call" | custom-call | tf_op jit(solution)/shard_map/pallas_call | solution.py:519
  566.2 15.1 %collective-permute-done.14 = bf16[4,96,768]{2,1,0:T(8,128)(2,1)S(1)} collective-permute-done((bf16[4,96,768]{2,1,0:T(8,128)(2,1)}, bf16[4,96,768]{2,1,0:T(8,128)(2,1)S(1)}, u32[]{:S(2)}, u32[]{:S(2)}) %collective-permute-start.14) | collective-permute-done | bytes 589856 | tf_op jit(solution)/shard_map/ppermute | solution.py:662
  581.3 17.2 %collective-permute-done.16 = bf16[4,96,768]{2,1,0:T(8,128)(2,1)} collective-permute-done((bf16[4,96,768]{2,1,0:T(8,128)(2,1)S(1)}, bf16[4,96,768]{2,1,0:T(8,128)(2,1)}, u32[]{:S(2)}, u32[]{:S(2)}) %collective-permute-start.16) | collective-permute-done | bytes 589856 | tf_op jit(solution)/shard_map/ppermute | solution.py:662
  602.2 4.7 collective-permute-start.17
  612.7 8.0 %collective-permute-done.18 = bf16[4,24,768]{2,1,0:T(8,128)(2,1)} collective-permute-done((bf16[4,24,768]{2,1,0:T(8,128)(2,1)}, bf16[4,24,768]{2,1,0:T(8,128)(2,1)}, u32[]{:S(2)}, u32[]{:S(2)}) %collective-permute-start.18) | collective-permute-done | bytes 147488 | tf_op jit(solution)/shard_map/ppermute | solution.py:662
  622.5 10.8 %shard_map.463 = (f32[1572,768]{1,0:T(8,128)}, f32[24,512]{1,0:T(8,128)}, f32[24,2304]{1,0:T(8,128)}, f32[14,24]{1,0:T(8,128)}, f32[8,128]{1,0:T(8,128)}) custom-call(s32[1,1280]{1,0:T(1,128)} %reshape_reshape.7.wanted_ref, bf16[1280,768]{1,0:T(8,128)(2,1)} %bitcast.30.returned_ref, bf16[1584,768]{1,0:T(8,128)(2,1)} %copy-done.4, ...), custom_call_target="tpu_custom_call" | custom-call | tf_op jit(solution)/shard_map/pallas_call | solution.py:519
  634.1 13.2 %all_to_all.71.every_ref = f32[32,8,128]{2,1,0:T(8,128)} all-to-all(f32[32,8,128]{2,1,0:T(8,128)S(1)} %broadcast_in_dim.167), channel_id=1, replica_groups=mesh['plane'=4,'pair'=2,'fsdp'=4] {'plane','pair','fsdp'}, dimensions={0} | all-to-all | bytes 262144 | tf_op jit(solution)/shard_map/all_to_all | solution.py:1333
  647.3 20.0 %shard_map.464 = (f32[1572,768]{1,0:T(8,128)}, f32[24,512]{1,0:T(8,128)}, f32[24,2304]{1,0:T(8,128)}, f32[24,768]{1,0:T(8,128)}, f32[24,3072]{1,0:T(8,128)}, /*i...) custom-call(f32[32,8,128]{2,1,0:T(8,128)} %all_to_all.71.every_ref, ...), custom_call_target="tpu_custom_call" | custom-call | tf_op jit(solution)/shard_map/pallas_call | solution.py:519
  673.3 6.3 all-to-all-done.10.every_ref
  680.2 10.1 %shard_map.465 = (f32[1572,768]{1,0:T(8,128)}, f32[24,512]{1,0:T(8,128)}, f32[24,2304]{1,0:T(8,128)}, f32[24,768]{1,0:T(8,128)}, f32[24,3072]{1,0:T(8,128)}, /*i...) custom-call(f32[32,8,128]{2,1,0:T(8,128)} %copy-done.12, f32[8,128]{1,0:T(8,128)} %get-tuple-element.474.total_ref, ...), custom_call_target="tpu_custom_call" | custom-call | tf_op jit(solution)/shard_map/pallas_call | solution.py:519
  (170 shorter events, 82.9 us)
Async XLA Ops:
  7.2 6.0 copy-start.3
  7.2 6.2 copy-start.9
  7.2 6.2 copy-start.10
  7.2 7.1 %copy-start.19 = (s32[2,512]{1,0:T(2,128)S(1)}, s32[2,512]{1,0:T(2,128)}, u32[]{:S(2)}) copy-start(s32[2,512]{1,0:T(2,128)} %param.31) | copy-start | bytes 12292
  7.2 7.1 %copy-start.16 = (s32[2,512]{1,0:T(2,128)S(1)}, s32[2,512]{1,0:T(2,128)}, u32[]{:S(2)}) copy-start(s32[2,512]{1,0:T(2,128)} %param.32) | copy-start | bytes 12292
  7.3 199.5 %all-gather.3.cloned.1.call-start = ((), (), s32[]{:S(2)}) async-start(), calls=%async_computation.12 | async-start | bytes 15611904 | tf_op jit(solution)/shard_map/all_gather | solution.py:983
  19.8 107.9 %copy-start.17 = (s32[1024]{0:T(1024)}, s32[1024]{0:T(1024)S(1)}, u32[]{:S(2)}) copy-start(s32[1024]{0:T(1024)S(1)} %add_select_fusion.4) | copy-start | bytes 12292
  21.2 14.6 %all-to-all-start.4 = ((s32[32,1,128]{2,1,0:T(1,128)}), s32[32,1,128]{2,1,0:T(1,128)S(1)}, u32[]{:S(2)}, u32[]{:S(2)}) async-start(s32[32,1,128]{2,1,0:T(1,128)} %bitcast.8), calls=%async_computation.4 | async-start | bytes 32768 | tf_op jit(solution)/shard_map/all_to_all | solution.py:718
  35.8 48.8 %copy-start.13 = (s32[32,1,128]{2,1,0:T(1,128)}, s32[32,1,128]{2,1,0:T(1,128)S(1)}, u32[]{:S(2)}) copy-start(s32[32,1,128]{2,1,0:T(1,128)S(1)} %all-to-all-done.4) | copy-start | bytes 49156
  42.8 84.8 %all-to-all-start.5 = ((bf16[32,40,768]{2,1,0:T(8,128)(2,1)}), bf16[32,40,768]{2,1,0:T(8,128)(2,1)S(1)}, u32[]{:S(2)}, u32[]{:S(2)}) async-start(bf16[32,40,768]{2,1,0:T(8,128)(2,1)} %bitcast.139), calls=%async_computation.5 | async-start | bytes 3932160 | tf_op jit(solution)/shard_map/all_to_all | solution.py:726
  132.6 5.7 copy-start.1
  132.6 74.5 %copy-start.21 = (s32[2,64]{1,0:T(2,128)S(1)}, s32[2,64]{1,0:T(2,128)}, u32[]{:S(2)}) copy-start(s32[2,64]{1,0:T(2,128)} %param.34) | copy-start | bytes 1540
  132.6 75.3 %copy-start.23 = (s32[2]{0:T(128)S(1)}, s32[2]{0:T(128)}, u32[]{:S(2)}) copy-start(s32[2]{0:T(128)} %param.33) | copy-start | bytes 28
  132.7 157.9 %all-to-all-start.6 = ((bf16[8,4,128,1664]{3,2,1,0:T(8,128)(2,1)}), bf16[8,4,128,1664]{3,2,1,0:T(8,128)(2,1)}, u32[]{:S(2)}, u32[]{:S(2)}) async-start(bf16[8,4,128,1664]{3,2,1,0:T(8,128)(2,1)} %bitcast.125), calls=%async_computation.6 | async-start | bytes 27262976 | tf_op jit(solution)/shard_map/all_to_all | solution.py:994
  138.2 160.3 %all-gather.5.cloned.1.call-start = ((), (), s32[]{:S(2)}) async-start(), calls=%async_computation.13 | async-start | bytes 1769472 | tf_op jit(solution)/shard_map/all_gather | solution.py:1107
  138.3 64.9 %collective-permute-start = (bf16[1584,768]{1,0:T(8,128)(2,1)S(1)}, bf16[1584,768]{1,0:T(8,128)(2,1)}, u32[]{:S(2)}, u32[]{:S(2)}) collective-permute-start(bf16[1584,768]{1,0:T(8,128)(2,1)S(1)} %copy-done.1), channel_id=1, source_target_pairs={{0,1},{1,2},{2,3},{3,0},{4,5},{5,6},{6,7},{7,4},{8,9},{9,10},{10,1... | collective-permute-start | bytes 7299080 | tf_op jit(solution)/shard_map/ppermute | solution.py:1003
  206.8 57.2 %collective-permute-start.1 = (bf16[1584,768]{1,0:T(8,128)(2,1)}, bf16[1584,768]{1,0:T(8,128)(2,1)S(1)}, u32[]{:S(2)}, u32[]{:S(2)}) collective-permute-start(bf16[1584,768]{1,0:T(8,128)(2,1)} %collective-permute-done.refs_1_), channel_id=1, source_target_pairs={{0,1},{1,2},{2,3},{3,0},{4,5},{5,6},{6,7},{7,4},{8,9},{9,10},{10,1... | collective-permute-start | bytes 7299080 | tf_op jit(solution)/shard_map/ppermute | solution.py:1012
  207.2 11.6 %copy-start.20 = (s32[2]{0:T(128)}, s32[2]{0:T(128)S(1)}, u32[]{:S(2)}) copy-start(s32[2]{0:T(128)S(1)} %reduce_sum.103.true_ref) | copy-start | bytes 28
  265.5 70.3 %collective-permute-start.3 = (bf16[1584,768]{1,0:T(8,128)(2,1)}, bf16[1584,768]{1,0:T(8,128)(2,1)S(1)}, u32[]{:S(2)}, u32[]{:S(2)}) collective-permute-start(bf16[1584,768]{1,0:T(8,128)(2,1)} %copy-done.7), channel_id=1, source_target_pairs={{0,1},{1,2},{2,3},{3,0},{4,5},{5,6},{6,7},{7,4},{8,9},{9,10},{10,1... | collective-permute-start | bytes 7299080 | tf_op jit(solution)/shard_map/ppermute | solution.py:1012
  324.1 11.1 %copy-start.22 = (s32[4]{0:T(128)S(1)}, s32[4]{0:T(128)}, u32[]{:S(2)}) copy-start(s32[4]{0:T(128)} %compare_select_fusion) | copy-start | bytes 52
  330.9 57.2 %collective-permute-start.2 = (bf16[1584,768]{1,0:T(8,128)(2,1)}, bf16[1584,768]{1,0:T(8,128)(2,1)}, u32[]{:S(2)}, u32[]{:S(2)}) collective-permute-start(bf16[1584,768]{1,0:T(8,128)(2,1)} %shard_map.455), channel_id=1, source_target_pairs={{0,1},{1,2},{2,3},{3,0},{4,5},{5,6},{6,7},{7,4},{8,9},{9,10},{10,1... | collective-permute-start | bytes 7299080 | tf_op jit(solution)/shard_map/ppermute | solution.py:1125
  351.2 24.7 %all-to-all-start.7 = ((bf16[8,128,768]{2,1,0:T(8,128)(2,1)}), bf16[8,128,768]{2,1,0:T(8,128)(2,1)S(1)}, u32[]{:S(2)}, u32[]{:S(2)}) async-start(bf16[8,128,768]{2,1,0:T(8,128)(2,1)} %bitcast.143), calls=%async_computation.7 | async-start | bytes 3145728 | tf_op jit(solution)/shard_map/all_to_all | solution.py:1127
  376.0 16.6 %copy-start.2 = (bf16[8,128,768]{2,1,0:T(8,128)(2,1)}, bf16[8,128,768]{2,1,0:T(8,128)(2,1)S(1)}, u32[]{:S(2)}) copy-start(bf16[8,128,768]{2,1,0:T(8,128)(2,1)S(1)} %all-to-all-done.7.head_ref) | copy-start | bytes 4718596
  392.6 56.5 %collective-permute-start.4 = (bf16[1584,768]{1,0:T(8,128)(2,1)}, bf16[1584,768]{1,0:T(8,128)(2,1)}, u32[]{:S(2)}, u32[]{:S(2)}) collective-permute-start(bf16[1584,768]{1,0:T(8,128)(2,1)} %add_convert_fusion.3), channel_id=1, source_target_pairs={{0,1},{1,2},{2,3},{3,0},{4,5},{5,6},{6,7},{7,4},{8,9},{9,10},{10,1... | collective-permute-start | bytes 7299080 | tf_op jit(solution)/shard_map/ppermute | solution.py:1151
  415.4 33.7 %copy-start.5 = (bf16[1584,768]{1,0:T(8,128)(2,1)S(1)}, bf16[1584,768]{1,0:T(8,128)(2,1)}, u32[]{:S(2)}) copy-start(bf16[1584,768]{1,0:T(8,128)(2,1)} %get-tuple-element.435) | copy-start | bytes 7299076
  449.1 4.9 copy-start.15
  449.1 9.1 %collective-permute-start.5 = (bf16[9,4,96,768]{3,2,1,0:T(8,128)(2,1)}, bf16[9,4,96,768]{3,2,1,0:T(8,128)(2,1)}, u32[]{:S(2)}, u32[]{:S(2)}) collective-permute-start(bf16[9,4,96,768]{3,2,1,0:T(8,128)(2,1)} %get-tuple-element.428), channel_id=1, source_target_pairs={{0,4},{4,0},{1,5},{5,1},{2,6},{6,2},{3,7},{7,3},{8,12},{12,8},{9,1... | collective-permute-start | bytes 15925256 | tf_op jit(solution)/shard_map/ppermute | solution.py:671
  452.9 57.7 %collective-permute-start.6 = (bf16[1584,768]{1,0:T(8,128)(2,1)}, bf16[1584,768]{1,0:T(8,128)(2,1)S(1)}, u32[]{:S(2)}, u32[]{:S(2)}) collective-permute-start(bf16[1584,768]{1,0:T(8,128)(2,1)} %add_convert_fusion.2), channel_id=1, source_target_pairs={{0,1},{1,2},{2,3},{3,0},{4,5},{5,6},{6,7},{7,4},{8,9},{9,10},{10,1... | collective-permute-start | bytes 7299080 | tf_op jit(solution)/shard_map/ppermute | solution.py:1151
  467.8 54.1 %collective-permute-start.7 = (bf16[9,96,768]{2,1,0:T(8,128)(2,1)}, bf16[9,96,768]{2,1,0:T(8,128)(2,1)}, u32[]{:S(2)}, u32[]{:S(2)}) collective-permute-start(bf16[9,96,768]{2,1,0:T(8,128)(2,1)} %get-tuple-element.551), channel_id=1, source_target_pairs={{0,8},{8,0},{16,24},{24,16},{1,9},{9,1},{17,25},{25,17},{2,10},{10... | collective-permute-start | bytes 3981320 | tf_op jit(solution)/shard_map/ppermute | solution.py:662
  469.2 59.6 %collective-permute-start.8 = (bf16[9,96,768]{2,1,0:T(8,128)(2,1)}, bf16[9,96,768]{2,1,0:T(8,128)(2,1)}, u32[]{:S(2)}, u32[]{:S(2)}) collective-permute-start(bf16[9,96,768]{2,1,0:T(8,128)(2,1)} %get-tuple-element.553), channel_id=1, source_target_pairs={{0,16},{8,24},{16,0},{24,8},{1,17},{9,25},{17,1},{25,9},{2,18},{10... | collective-permute-start | bytes 3981320 | tf_op jit(solution)/shard_map/ppermute | solution.py:662
  469.7 59.1 %collective-permute-start.9 = (bf16[9,96,768]{2,1,0:T(8,128)(2,1)}, bf16[9,96,768]{2,1,0:T(8,128)(2,1)}, u32[]{:S(2)}, u32[]{:S(2)}) collective-permute-start(bf16[9,96,768]{2,1,0:T(8,128)(2,1)} %get-tuple-element.552), channel_id=1, source_target_pairs={{0,24},{8,16},{16,8},{24,0},{1,25},{9,17},{17,9},{25,1},{2,26},{10... | collective-permute-start | bytes 3981320 | tf_op jit(solution)/shard_map/ppermute | solution.py:662
  510.5 11.4 %copy-start.4 = (bf16[1584,768]{1,0:T(8,128)(2,1)}, bf16[1584,768]{1,0:T(8,128)(2,1)S(1)}, u32[]{:S(2)}) copy-start(bf16[1584,768]{1,0:T(8,128)(2,1)S(1)} %collective-permute-done.6.moved_ref) | copy-start | bytes 7299076
  521.9 10.2 %copy-start.18 = (s32[1024]{0:T(1024)S(1)}, s32[1024]{0:T(1024)}, u32[]{:S(2)}) copy-start(s32[1024]{0:T(1024)} %copy-done.17) | copy-start | bytes 12292
  538.0 84.5 %all-to-all-start.8 = ((bf16[32,40,768]{2,1,0:T(8,128)(2,1)}), bf16[32,40,768]{2,1,0:T(8,128)(2,1)}, u32[]{:S(2)}, u32[]{:S(2)}) async-start(bf16[32,40,768]{2,1,0:T(8,128)(2,1)} %bitcast.137), calls=%async_computation.8 | async-start | bytes 3932160 | tf_op jit(solution)/shard_map/all_to_all | solution.py:757
  541.5 58.6 %reduce-scatter.4.cloned.1.call-start = ((), (), s32[]{:S(2)}) async-start(), calls=%async_computation.14 | async-start | bytes 1658880
  553.6 6.5 copy-start.8
  555.5 2.1 collective-permute-start.10
  555.6 2.8 collective-permute-start.11
  556.1 3.2 collective-permute-start.12
  556.2 3.9 collective-permute-start.13
  560.8 4.6 copy-start.14
  562.0 19.3 %collective-permute-start.14 = (bf16[4,96,768]{2,1,0:T(8,128)(2,1)}, bf16[4,96,768]{2,1,0:T(8,128)(2,1)S(1)}, u32[]{:S(2)}, u32[]{:S(2)}) collective-permute-start(bf16[4,96,768]{2,1,0:T(8,128)(2,1)} %get-tuple-element.556), channel_id=1, source_target_pairs={{0,8},{8,0},{16,24},{24,16},{1,9},{9,1},{17,25},{25,17},{2,10},{10... | collective-permute-start | bytes 1769480 | tf_op jit(solution)/shard_map/ppermute | solution.py:662
  563.6 17.7 %collective-permute-start.15 = (bf16[4,96,768]{2,1,0:T(8,128)(2,1)}, bf16[4,96,768]{2,1,0:T(8,128)(2,1)}, u32[]{:S(2)}, u32[]{:S(2)}) collective-permute-start(bf16[4,96,768]{2,1,0:T(8,128)(2,1)} %get-tuple-element.558), channel_id=1, source_target_pairs={{0,16},{8,24},{16,0},{24,8},{1,17},{9,25},{17,1},{25,9},{2,18},{10... | collective-permute-start | bytes 1769480 | tf_op jit(solution)/shard_map/ppermute | solution.py:662
  565.1 33.5 %collective-permute-start.16 = (bf16[4,96,768]{2,1,0:T(8,128)(2,1)S(1)}, bf16[4,96,768]{2,1,0:T(8,128)(2,1)}, u32[]{:S(2)}, u32[]{:S(2)}) collective-permute-start(bf16[4,96,768]{2,1,0:T(8,128)(2,1)S(1)} %get-tuple-element.557), channel_id=1, source_target_pairs={{0,24},{8,16},{16,8},{24,0},{1,25},{9,17},{17,9},{25,1},{2,26},{10... | collective-permute-start | bytes 1769480 | tf_op jit(solution)/shard_map/ppermute | solution.py:662
  602.2 10.5 %collective-permute-start.17 = (bf16[4,24,768]{2,1,0:T(8,128)(2,1)}, bf16[4,24,768]{2,1,0:T(8,128)(2,1)}, u32[]{:S(2)}, u32[]{:S(2)}) collective-permute-start(bf16[4,24,768]{2,1,0:T(8,128)(2,1)} %get-tuple-element.565), channel_id=1, source_target_pairs={{0,1},{1,0},{2,3},{3,2},{4,5},{5,4},{6,7},{7,6},{8,9},{9,8},{10,11... | collective-permute-start | bytes 442376 | tf_op jit(solution)/shard_map/ppermute | solution.py:662
  606.8 13.9 %collective-permute-start.18 = (bf16[4,24,768]{2,1,0:T(8,128)(2,1)}, bf16[4,24,768]{2,1,0:T(8,128)(2,1)}, u32[]{:S(2)}, u32[]{:S(2)}) collective-permute-start(bf16[4,24,768]{2,1,0:T(8,128)(2,1)} %get-tuple-element.567), channel_id=1, source_target_pairs={{0,2},{1,3},{2,0},{3,1},{4,6},{5,7},{6,4},{7,5},{8,10},{9,11},{10,... | collective-permute-start | bytes 442376 | tf_op jit(solution)/shard_map/ppermute | solution.py:662
  606.8 13.9 %collective-permute-start.19 = (bf16[4,24,768]{2,1,0:T(8,128)(2,1)}, bf16[4,24,768]{2,1,0:T(8,128)(2,1)}, u32[]{:S(2)}, u32[]{:S(2)}) collective-permute-start(bf16[4,24,768]{2,1,0:T(8,128)(2,1)} %get-tuple-element.566), channel_id=1, source_target_pairs={{0,3},{1,2},{2,1},{3,0},{4,7},{5,6},{6,5},{7,4},{8,11},{9,10},{10,... | collective-permute-start | bytes 442376 | tf_op jit(solution)/shard_map/ppermute | solution.py:662
  668.6 11.0 %all-to-all-start.10 = ((f32[32,8,128]{2,1,0:T(8,128)}), f32[32,8,128]{2,1,0:T(8,128)S(1)}, u32[]{:S(2)}, u32[]{:S(2)}) async-start(f32[32,8,128]{2,1,0:T(8,128)} %broadcast_in_dim.168), calls=%async_computation.10 | async-start | bytes 262144 | tf_op jit(solution)/shard_map/all_to_all | solution.py:1333
  (5 other events, 7.8 us)
Sparse Core Ops, SparseCore 0:
  14.4 192.3 all-gather.2
  265.6 32.9 all-gather.4
  544.6 53.4 reduce-scatter.3

commit v2 on v1

--- a/solution.py
+++ b/solution.py
@@ -1297,7 +1297,7 @@
         jnp.transpose(early[1 : 1 + blocks], (1, 2, 0)).reshape(in_rows, ff),
         jnp.swapaxes(early[1 + blocks :], 0, 1).reshape(-1, row_width),
     )
-    rows = 208
+    rows = 400 if own_rows > 400 else 208
     steps = -(-own_rows // rows)
 
     def by_row(array=None, width=row_width):

time: 709 us -> 703 us (level)
  Pallas kernels: 241 us -> 220 us
  waiting for transfers between devices: 267 us -> 280 us
    pallas_call x11, Pallas kernels: 152 us -> 138 us  [row_kernel(): pl.pallas_call(kernel, out_shape=tuple((jax.ShapeDtypeStruct(shape, kind)...]
    ppermute x2, waiting for transfers between devices: 12.2 us -> 20.5 us  [pass_table(): tables.append(lax.ppermute(newest, 'fsdp', ring))]
  transfers between devices with their start and end apart: 29 -> 29, of which waited for: 21 -> 21; matrix products, arithmetic and copies ran while one was open for 10% -> 10% of each run, Pallas kernels for 29% -> 27%
where the time goes in v2:
time: 703 us; the launch traced here: 693 us
  waiting for transfers between devices  280 us (40%)
  Pallas kernels  220 us (31%)
  starting transfers between devices  60.5 us (9%)
  other arithmetic  51 us (7%)
  local copies, waits for them, and re-layouts  32.6 us (5%)
  between operations  16.8 us (2%)
  matrix products  16.1 us (2%)
  blocking collectives  13.4 us (2%)
    pallas_call x11, Pallas kernels, row_kernel(): pl.pallas_call(kernel, out_shape=tuple((jax.ShapeDtypeStruct(shape, kind)...  138 us
    ppermute x1, waiting for transfers between devices, on_device(): tables = [first_table, lax.ppermute(first_table, 'fsdp', ring)]  58.1 us
    ppermute x9, waiting for transfers between devices, sum_over_peers(): lax.ppermute(given, axis, [(peer, peer ^ apart) for peer in range(size)])  47.6 us
    ppermute x2, waiting for transfers between devices, pass_sum(): head_sums.append(lax.ppermute(total.astype(bf16), 'fsdp', ring))  45.9 us
    all_to_all x1, waiting for transfers between devices, ask_rows(): lax.all_to_all(rows.reshape(n_dev, room, -1), axes, split_axis=0, concat_...  42.4 us
    pallas_call x2, Pallas kernels, head_products(): pl.pallas_call(functools.partial(head_kernel, steps), out_shape=(jax.Shap...  39.6 us
    pallas_call x1, Pallas kernels, parcels_of(): pl.pallas_call(functools.partial(parcel_kernel, own_rows, tiles, wide), o...  24.3 us
    all_to_all x1, waiting for transfers between devices, on_device(): lax.all_to_all(targets.reshape(n_dp, n_fs, n_pick, lanes), SPLIT, split_a...  24.2 us
  transfers between devices with their start and end apart: 29, of which 21 were waited for; matrix products, arithmetic and copies ran while one was open for 10% of the time, Pallas kernels for 27%

profile of v2, /device:TPU:0, one launch (start us, length us, event | category | flops | bytes accessed | tf_op | source)
XLA Modules:
  0.0 692.7 jit_solution(8231344632274733510)
XLA Ops:
  21.2 7.3 %all-to-all-start.4 = ((s32[32,1,128]{2,1,0:T(1,128)}), s32[32,1,128]{2,1,0:T(1,128)S(1)}, u32[]{:S(2)}, u32[]{:S(2)}) async-start(s32[32,1,128]{2,1,0:T(1,128)} %bitcast.8), calls=%async_computation.4 | async-start | bytes 32768 | tf_op jit(solution)/shard_map/all_to_all | solution.py:718
  28.5 7.1 %multiply_reduce_fusion = (f32[]{:T(128)}, bf16[1572,768]{1,0:T(8,128)(2,1)}) fusion(f32[1572,768]{1,0:T(8,128)} %refs_0_.3), kind=kLoop, calls=%fused_computation.35 | loop fusion | flops 3621887 | bytes 7243780 | tf_op jit(solution)/shard_map/reduce_sum | solution.py:999
  35.9 6.9 %fusion.17 = bf16[1280,768]{1,0:T(8,128)(2,1)} fusion(bf16[1572,768]{1,0:T(8,128)(2,1)} %get-tuple-element.727, s32[1280]{0:T(1024)S(1)} %eq.297), kind=kOutput, calls=%fused_computation.43 | convolution fusion | flops 3093672960 | bytes 4385792 | tf_op jit(solution)/shard_map/dot_general | solution.py:36
  42.8 5.6 all-to-all-start.5
  48.5 24.3 %shard_map.450 = bf16[32,128,1664]{2,1,0:T(8,128)(2,1)} custom-call(bf16[128,50304]{1,0:T(8,128)(2,1)} %bitcast.129), custom_call_target="tpu_custom_call" | custom-call | tf_op jit(solution)/shard_map/pallas_call | solution.py:581
  78.7 5.8 select_add_fusion.tile_ref
  85.3 42.4 %all-to-all-done.5 = bf16[32,40,768]{2,1,0:T(8,128)(2,1)S(1)} async-done(((bf16[32,40,768]{2,1,0:T(8,128)(2,1)}), bf16[32,40,768]{2,1,0:T(8,128)(2,1)S(1)}, u32[]{:S(2)}, u32[]{:S(2)}) %all-to-all-start.5) | async-done | bytes 1966112 | tf_op jit(solution)/shard_map/all_to_all | solution.py:726
  127.7 4.1 fusion.13
  132.7 5.6 all-to-all-start.6
  138.4 6.7 collective-permute-start
  145.1 58.1 %collective-permute-done.refs_1_ = bf16[1584,768]{1,0:T(8,128)(2,1)} collective-permute-done((bf16[1584,768]{1,0:T(8,128)(2,1)S(1)}, bf16[1584,768]{1,0:T(8,128)(2,1)}, u32[]{:S(2)}, u32[]{:S(2)}) %collective-permute-start) | collective-permute-done | bytes 2433056 | tf_op jit(solution)/shard_map/ppermute | solution.py:1003
  203.2 3.6 all-gather.3.cloned.1.call-done.place_ref.vector_ref.weight_ref.out_ref.up_ref.down_ref
  208.7 9.2 %shard_map.451 = (f32[1024,768]{1,0:T(8,128)}, f32[1024,768]{1,0:T(8,128)}, bf16[1024,768]{1,0:T(8,128)(2,1)}, bf16[1024,2304]{1,0:T(8,128)(2,1)}) custom-call(s32[2]{0:T(128)} %compare_select_fusion.2.length_ref, f32[1024,768]{1,0:T(8,128)} %get-tuple-element.394.token_ref, ...), custom_call_target="tpu_custom_call" | custom-call | tf_op jit(solution)/shard_map/pallas_call | solution.py:519
  217.9 8.8 %shard_map.452.mixed_ref = bf16[1024,768]{1,0:T(8,128)(2,1)} custom-call(s32[2]{0:T(128)} %compare_select_fusion.2.length_ref, bf16[1024,2304]{1,0:T(8,128)(2,1)} %get-tuple-element.397.query_ref.key_ref.value_ref, bf16[1024,2304]{1,0:T(8,128)(2,1)} %get-tuple-element.397.query_ref.key_ref.value_ref, ...), custom_call_target="tpu_custom_call" | custom-call | tf_op jit(solution)/shard_map/pallas_call | solution.py:170
  229.2 14.6 %shard_map.453 = (f32[1024,768]{1,0:T(8,128)}, bf16[1024,768]{1,0:T(8,128)(2,1)}, bf16[1024,3072]{1,0:T(8,128)(2,1)}, bf16[1024,3072]{1,0:T(8,128)(2,1)}, f32[10...) custom-call(s32[2]{0:T(128)} %compare_select_fusion.2.length_ref, ...), custom_call_target="tpu_custom_call" | custom-call | tf_op jit(solution)/shard_map/pallas_call | solution.py:519
  243.7 20.5 %collective-permute-done.1.refs_2_ = bf16[1584,768]{1,0:T(8,128)(2,1)S(1)} collective-permute-done((bf16[1584,768]{1,0:T(8,128)(2,1)}, bf16[1584,768]{1,0:T(8,128)(2,1)S(1)}, u32[]{:S(2)}, u32[]{:S(2)}) %collective-permute-start.1) | collective-permute-done | bytes 2433056 | tf_op jit(solution)/shard_map/ppermute | solution.py:1012
  266.5 24.2 %all-to-all-done.6.target_ref = bf16[8,4,128,1664]{3,2,1,0:T(8,128)(2,1)} async-done(((bf16[8,4,128,1664]{3,2,1,0:T(8,128)(2,1)}), bf16[8,4,128,1664]{3,2,1,0:T(8,128)(2,1)}, u32[]{:S(2)}, u32[]{:S(2)}) %all-to-all-start.6) | async-done | bytes 13631520 | tf_op jit(solution)/shard_map/all_to_all | solution.py:994
  290.7 5.6 all-gather.5.cloned.1.call-done.chosen_ref
  296.3 25.6 %shard_map.454 = (bf16[3,1024,1584]{2,1,0:T(8,128)(2,1)}, f32[1024,768]{1,0:T(8,128)}, f32[8,1584]{1,0:T(8,128)}) custom-call(s32[3]{0:T(128)} %bitcast.164, bf16[1024,768]{1,0:T(8,128)(2,1)} %all-gather.5.cloned.1.call-done.chosen_ref, bf16[8,4,128,1664]{3,2,1,0:T(8,128)(2,1)} %all-to-all-done.6.target_ref, bf16[1584,768]{1,0:T(8,128)(2,1)} %pad.18.refs_0_, ...), custom_call_target="tpu_custom_call" | custom-call | tf_op jit(solution)/shard_map/pallas_call | solution.py:630
  321.9 6.7 shard_map.455
  328.6 5.7 collective-permute-start.2
  336.4 14.0 %shard_map.456 = (bf16[1,1024,1584]{2,1,0:T(8,128)(2,1)}, bf16[1024,768]{1,0:T(8,128)(2,1)}, f32[8,1584]{1,0:T(8,128)}) custom-call(s32[1]{0:T(128)} %slice.67.place_ref, bf16[1024,768]{1,0:T(8,128)(2,1)} %all-gather.5.cloned.1.call-done.chosen_ref, bf16[8,4,128,1664]{3,2,1,0:T(8,128)(2,1)} %all-to-all-done.6.target_ref, bf16[1584,768]{1,0:T(8,128)(2,1)} %copy-done.6, ...), custom_call_target="tpu_custom_call" | custom-call | tf_op jit(solution)/shard_map/pallas_call | solution.py:630
  350.4 3.8 all-to-all-start.7
  354.2 14.8 %shard_map.457 = (bf16[1584,768]{1,0:T(8,128)(2,1)}, bf16[1584,768]{1,0:T(8,128)(2,1)}, bf16[1584,768]{1,0:T(8,128)(2,1)}) custom-call(bf16[3,1024,1584]{2,1,0:T(8,128)(2,1)} %get-tuple-element.404.slope_ref, bf16[1,1024,1584]{2,1,0:T(8,128)(2,1)} %get-tuple-element.410.last_ref, bf16[1024,768]{1,0:T(8,128)(2,1)} %all-gather.5.cloned.1.call-done.chosen_ref), custom_call_target="tpu_custom_call" | custom-call | tf_op jit(solution)/shard_map/pallas_call | solution.py:519
  369.0 6.1 all-to-all-done.7.head_ref
  375.1 12.1 %collective-permute-done.2 = bf16[1584,768]{1,0:T(8,128)(2,1)} collective-permute-done((bf16[1584,768]{1,0:T(8,128)(2,1)}, bf16[1584,768]{1,0:T(8,128)(2,1)}, u32[]{:S(2)}, u32[]{:S(2)}) %collective-permute-start.2) | collective-permute-done | bytes 2433056 | tf_op jit(solution)/shard_map/ppermute | solution.py:1125
  387.2 4.5 add_convert_fusion.3
  394.6 16.5 %shard_map.458 = (f32[1024,768]{1,0:T(8,128)}, f32[1024,768]{1,0:T(8,128)}, bf16[1024,768]{1,0:T(8,128)(2,1)}, bf16[1024,768]{1,0:T(8,128)(2,1)}, bf16[1024,768]...) custom-call(s32[2]{0:T(128)} %compare_select_fusion.2.length_ref, ...), custom_call_target="tpu_custom_call" | custom-call | tf_op jit(solution)/shard_map/pallas_call | solution.py:519
  411.1 20.0 %shard_map.459 = (bf16[9,4,96,768]{3,2,1,0:T(8,128)(2,1)}, bf16[9,4,96,768]{3,2,1,0:T(8,128)(2,1)}) custom-call(s32[1]{0:T(128)} %bitcast.22.member_ref, bf16[1024,768]{1,0:T(8,128)(2,1)} %shard_map.452.mixed_ref, bf16[1024,768]{1,0:T(8,128)(2,1)} %get-tuple-element.420.attention_ref, bf16[1024,768]{1,0:T(8,128)(2,1)} %get-tuple-element.421.normed_ref, ...), custom_call_target="tpu_custom_call" | custom-call | tf_op jit(solution)/shard_map/pallas_call | solution.py:519
  431.0 17.4 %collective-permute-done.4 = bf16[1584,768]{1,0:T(8,128)(2,1)} collective-permute-done((bf16[1584,768]{1,0:T(8,128)(2,1)}, bf16[1584,768]{1,0:T(8,128)(2,1)}, u32[]{:S(2)}, u32[]{:S(2)}) %collective-permute-start.4) | collective-permute-done | bytes 2433056 | tf_op jit(solution)/shard_map/ppermute | solution.py:1151
  448.4 3.8 add_convert_fusion.2
  453.5 4.0 collective-permute-done.5
  457.5 6.1 add_convert_fusion.1
  471.1 9.9 %shard_map.460 = (bf16[1024,768]{1,0:T(8,128)(2,1)}, bf16[1024,768]{1,0:T(8,128)(2,1)}, bf16[1024,768]{1,0:T(8,128)(2,1)}) custom-call(s32[2]{0:T(128)} %compare_select_fusion.2.length_ref, bf16[1024,2304]{1,0:T(8,128)(2,1)} %get-tuple-element.397.query_ref.key_ref.value_ref, bf16[1024,2304]{1,0:T(8,128)(2,1)} %get-tuple-element.397.query_ref.key_ref.value_ref, ...), custom_call_target="tpu_custom_call" | custom-call | tf_op jit(solution)/shard_map/pallas_call | solution.py:170
  481.0 28.5 %collective-permute-done.6.moved_ref = bf16[1584,768]{1,0:T(8,128)(2,1)S(1)} collective-permute-done((bf16[1584,768]{1,0:T(8,128)(2,1)}, bf16[1584,768]{1,0:T(8,128)(2,1)S(1)}, u32[]{:S(2)}, u32[]{:S(2)}) %collective-permute-start.6) | collective-permute-done | bytes 2433056 | tf_op jit(solution)/shard_map/ppermute | solution.py:1151
  509.5 10.5 %shard_map.461 = (bf16[1024,768]{1,0:T(8,128)(2,1)}, bf16[768,512]{1,0:T(8,128)(2,1)}, f32[4,8,768]{2,1,0:T(8,128)}) custom-call(s32[2]{0:T(128)} %compare_select_fusion.2.length_ref, s32[2]{0:T(128)} %compare_convert_fusion.keep_ref, bf16[1024,768]{1,0:T(8,128)(2,1)} %get-tuple-element.448.query_ref, bf16[1024,768]{1,0:T(8,128)(2,1)} %get-tuple-element.449.key_ref, ...), custom_call_target="tpu_custom_call" | custom-call | tf_op jit(solution)/shard_map/pallas_call | solution.py:519
  520.1 7.2 %collective-permute-done.8 = bf16[9,96,768]{2,1,0:T(8,128)(2,1)} collective-permute-done((bf16[9,96,768]{2,1,0:T(8,128)(2,1)}, bf16[9,96,768]{2,1,0:T(8,128)(2,1)}, u32[]{:S(2)}, u32[]{:S(2)}) %collective-permute-start.8) | collective-permute-done | bytes 1327136 | tf_op jit(solution)/shard_map/ppermute | solution.py:662
  530.6 5.1 fusion.18
  543.0 9.1 %shard_map.462 = (bf16[4,4,96,768]{3,2,1,0:T(8,128)(2,1)}, bf16[4,4,96,768]{3,2,1,0:T(8,128)(2,1)}) custom-call(s32[1]{0:T(128)} %bitcast.22.member_ref, bf16[1024,768]{1,0:T(8,128)(2,1)} %get-tuple-element.447.low_ref, bf16[1024,768]{1,0:T(8,128)(2,1)} %get-tuple-element.448.query_ref, bf16[1024,768]{1,0:T(8,128)(2,1)} %get-tuple-element.449.key_ref, ...), custom_call_target="tpu_custom_call" | custom-call | tf_op jit(solution)/shard_map/pallas_call | solution.py:519
  564.7 15.1 %collective-permute-done.14 = bf16[4,96,768]{2,1,0:T(8,128)(2,1)S(1)} collective-permute-done((bf16[4,96,768]{2,1,0:T(8,128)(2,1)}, bf16[4,96,768]{2,1,0:T(8,128)(2,1)S(1)}, u32[]{:S(2)}, u32[]{:S(2)}) %collective-permute-start.14) | collective-permute-done | bytes 589856 | tf_op jit(solution)/shard_map/ppermute | solution.py:662
  579.8 17.2 %collective-permute-done.16 = bf16[4,96,768]{2,1,0:T(8,128)(2,1)} collective-permute-done((bf16[4,96,768]{2,1,0:T(8,128)(2,1)S(1)}, bf16[4,96,768]{2,1,0:T(8,128)(2,1)}, u32[]{:S(2)}, u32[]{:S(2)}) %collective-permute-start.16) | collective-permute-done | bytes 589856 | tf_op jit(solution)/shard_map/ppermute | solution.py:662
  600.7 4.7 collective-permute-start.17
  611.2 8.0 %collective-permute-done.18 = bf16[4,24,768]{2,1,0:T(8,128)(2,1)} collective-permute-done((bf16[4,24,768]{2,1,0:T(8,128)(2,1)}, bf16[4,24,768]{2,1,0:T(8,128)(2,1)}, u32[]{:S(2)}, u32[]{:S(2)}) %collective-permute-start.18) | collective-permute-done | bytes 147488 | tf_op jit(solution)/shard_map/ppermute | solution.py:662
  621.0 9.0 %shard_map.463 = (f32[1572,768]{1,0:T(8,128)}, f32[24,512]{1,0:T(8,128)}, f32[24,2304]{1,0:T(8,128)}, f32[14,24]{1,0:T(8,128)}, f32[8,128]{1,0:T(8,128)}) custom-call(s32[1,1280]{1,0:T(1,128)} %reshape_reshape.7.wanted_ref, bf16[1280,768]{1,0:T(8,128)(2,1)} %bitcast.30.returned_ref, bf16[1584,768]{1,0:T(8,128)(2,1)} %copy-done.4, ...), custom_call_target="tpu_custom_call" | custom-call | tf_op jit(solution)/shard_map/pallas_call | solution.py:519
  630.8 13.4 %all_to_all.71.every_ref = f32[32,8,128]{2,1,0:T(8,128)} all-to-all(f32[32,8,128]{2,1,0:T(8,128)S(1)} %broadcast_in_dim.167), channel_id=1, replica_groups=mesh['plane'=4,'pair'=2,'fsdp'=4] {'plane','pair','fsdp'}, dimensions={0} | all-to-all | bytes 262144 | tf_op jit(solution)/shard_map/all_to_all | solution.py:1333
  644.2 19.0 %shard_map.464 = (f32[1572,768]{1,0:T(8,128)}, f32[24,512]{1,0:T(8,128)}, f32[24,2304]{1,0:T(8,128)}, f32[24,768]{1,0:T(8,128)}, f32[24,3072]{1,0:T(8,128)}, /*i...) custom-call(f32[32,8,128]{2,1,0:T(8,128)} %all_to_all.71.every_ref, ...), custom_call_target="tpu_custom_call" | custom-call | tf_op jit(solution)/shard_map/pallas_call | solution.py:519
  669.2 6.3 all-to-all-done.10.every_ref
  676.2 8.3 %shard_map.465 = (f32[1572,768]{1,0:T(8,128)}, f32[24,512]{1,0:T(8,128)}, f32[24,2304]{1,0:T(8,128)}, f32[24,768]{1,0:T(8,128)}, f32[24,3072]{1,0:T(8,128)}, /*i...) custom-call(f32[32,8,128]{2,1,0:T(8,128)} %copy-done.12, f32[8,128]{1,0:T(8,128)} %get-tuple-element.474.total_ref, ...), custom_call_target="tpu_custom_call" | custom-call | tf_op jit(solution)/shard_map/pallas_call | solution.py:519
  (170 shorter events, 82.9 us)
Async XLA Ops:
  7.2 6.0 copy-start.3
  7.2 6.2 copy-start.9
  7.2 6.2 copy-start.10
  7.2 7.1 %copy-start.19 = (s32[2,512]{1,0:T(2,128)S(1)}, s32[2,512]{1,0:T(2,128)}, u32[]{:S(2)}) copy-start(s32[2,512]{1,0:T(2,128)} %param.31) | copy-start | bytes 12292
  7.2 7.1 %copy-start.16 = (s32[2,512]{1,0:T(2,128)S(1)}, s32[2,512]{1,0:T(2,128)}, u32[]{:S(2)}) copy-start(s32[2,512]{1,0:T(2,128)} %param.32) | copy-start | bytes 12292
  7.3 199.5 %all-gather.3.cloned.1.call-start = ((), (), s32[]{:S(2)}) async-start(), calls=%async_computation.12 | async-start | bytes 15611904 | tf_op jit(solution)/shard_map/all_gather | solution.py:983
  19.8 107.9 %copy-start.17 = (s32[1024]{0:T(1024)}, s32[1024]{0:T(1024)S(1)}, u32[]{:S(2)}) copy-start(s32[1024]{0:T(1024)S(1)} %add_select_fusion.4) | copy-start | bytes 12292
  21.2 14.6 %all-to-all-start.4 = ((s32[32,1,128]{2,1,0:T(1,128)}), s32[32,1,128]{2,1,0:T(1,128)S(1)}, u32[]{:S(2)}, u32[]{:S(2)}) async-start(s32[32,1,128]{2,1,0:T(1,128)} %bitcast.8), calls=%async_computation.4 | async-start | bytes 32768 | tf_op jit(solution)/shard_map/all_to_all | solution.py:718
  35.8 48.8 %copy-start.13 = (s32[32,1,128]{2,1,0:T(1,128)}, s32[32,1,128]{2,1,0:T(1,128)S(1)}, u32[]{:S(2)}) copy-start(s32[32,1,128]{2,1,0:T(1,128)S(1)} %all-to-all-done.4) | copy-start | bytes 49156
  42.8 84.8 %all-to-all-start.5 = ((bf16[32,40,768]{2,1,0:T(8,128)(2,1)}), bf16[32,40,768]{2,1,0:T(8,128)(2,1)S(1)}, u32[]{:S(2)}, u32[]{:S(2)}) async-start(bf16[32,40,768]{2,1,0:T(8,128)(2,1)} %bitcast.139), calls=%async_computation.5 | async-start | bytes 3932160 | tf_op jit(solution)/shard_map/all_to_all | solution.py:726
  132.7 5.7 copy-start.1
  132.7 74.7 %copy-start.21 = (s32[2,64]{1,0:T(2,128)S(1)}, s32[2,64]{1,0:T(2,128)}, u32[]{:S(2)}) copy-start(s32[2,64]{1,0:T(2,128)} %param.34) | copy-start | bytes 1540
  132.7 75.5 %copy-start.23 = (s32[2]{0:T(128)S(1)}, s32[2]{0:T(128)}, u32[]{:S(2)}) copy-start(s32[2]{0:T(128)} %param.33) | copy-start | bytes 28
  132.7 158.0 %all-to-all-start.6 = ((bf16[8,4,128,1664]{3,2,1,0:T(8,128)(2,1)}), bf16[8,4,128,1664]{3,2,1,0:T(8,128)(2,1)}, u32[]{:S(2)}, u32[]{:S(2)}) async-start(bf16[8,4,128,1664]{3,2,1,0:T(8,128)(2,1)} %bitcast.125), calls=%async_computation.6 | async-start | bytes 27262976 | tf_op jit(solution)/shard_map/all_to_all | solution.py:994
  138.3 158.0 %all-gather.5.cloned.1.call-start = ((), (), s32[]{:S(2)}) async-start(), calls=%async_computation.13 | async-start | bytes 1769472 | tf_op jit(solution)/shard_map/all_gather | solution.py:1107
  138.4 64.8 %collective-permute-start = (bf16[1584,768]{1,0:T(8,128)(2,1)S(1)}, bf16[1584,768]{1,0:T(8,128)(2,1)}, u32[]{:S(2)}, u32[]{:S(2)}) collective-permute-start(bf16[1584,768]{1,0:T(8,128)(2,1)S(1)} %copy-done.1), channel_id=1, source_target_pairs={{0,1},{1,2},{2,3},{3,0},{4,5},{5,6},{6,7},{7,4},{8,9},{9,10},{10,1... | collective-permute-start | bytes 7299080 | tf_op jit(solution)/shard_map/ppermute | solution.py:1003
  206.8 57.5 %collective-permute-start.1 = (bf16[1584,768]{1,0:T(8,128)(2,1)}, bf16[1584,768]{1,0:T(8,128)(2,1)S(1)}, u32[]{:S(2)}, u32[]{:S(2)}) collective-permute-start(bf16[1584,768]{1,0:T(8,128)(2,1)} %collective-permute-done.refs_1_), channel_id=1, source_target_pairs={{0,1},{1,2},{2,3},{3,0},{4,5},{5,6},{6,7},{7,4},{8,9},{9,10},{10,1... | collective-permute-start | bytes 7299080 | tf_op jit(solution)/shard_map/ppermute | solution.py:1012
  207.4 10.5 %copy-start.20 = (s32[2]{0:T(128)}, s32[2]{0:T(128)S(1)}, u32[]{:S(2)}) copy-start(s32[2]{0:T(128)S(1)} %reduce_sum.103.true_ref) | copy-start | bytes 28
  265.7 69.2 %collective-permute-start.3 = (bf16[1584,768]{1,0:T(8,128)(2,1)}, bf16[1584,768]{1,0:T(8,128)(2,1)S(1)}, u32[]{:S(2)}, u32[]{:S(2)}) collective-permute-start(bf16[1584,768]{1,0:T(8,128)(2,1)} %copy-done.7), channel_id=1, source_target_pairs={{0,1},{1,2},{2,3},{3,0},{4,5},{5,6},{6,7},{7,4},{8,9},{9,10},{10,1... | collective-permute-start | bytes 7299080 | tf_op jit(solution)/shard_map/ppermute | solution.py:1012
  321.9 12.4 %copy-start.22 = (s32[4]{0:T(128)S(1)}, s32[4]{0:T(128)}, u32[]{:S(2)}) copy-start(s32[4]{0:T(128)} %compare_select_fusion) | copy-start | bytes 52
  328.6 58.6 %collective-permute-start.2 = (bf16[1584,768]{1,0:T(8,128)(2,1)}, bf16[1584,768]{1,0:T(8,128)(2,1)}, u32[]{:S(2)}, u32[]{:S(2)}) collective-permute-start(bf16[1584,768]{1,0:T(8,128)(2,1)} %shard_map.455), channel_id=1, source_target_pairs={{0,1},{1,2},{2,3},{3,0},{4,5},{5,6},{6,7},{7,4},{8,9},{9,10},{10,1... | collective-permute-start | bytes 7299080 | tf_op jit(solution)/shard_map/ppermute | solution.py:1125
  350.4 24.8 %all-to-all-start.7 = ((bf16[8,128,768]{2,1,0:T(8,128)(2,1)}), bf16[8,128,768]{2,1,0:T(8,128)(2,1)S(1)}, u32[]{:S(2)}, u32[]{:S(2)}) async-start(bf16[8,128,768]{2,1,0:T(8,128)(2,1)} %bitcast.143), calls=%async_computation.7 | async-start | bytes 3145728 | tf_op jit(solution)/shard_map/all_to_all | solution.py:1127
  375.1 16.5 %copy-start.2 = (bf16[8,128,768]{2,1,0:T(8,128)(2,1)}, bf16[8,128,768]{2,1,0:T(8,128)(2,1)S(1)}, u32[]{:S(2)}) copy-start(bf16[8,128,768]{2,1,0:T(8,128)(2,1)S(1)} %all-to-all-done.7.head_ref) | copy-start | bytes 4718596
  391.7 56.7 %collective-permute-start.4 = (bf16[1584,768]{1,0:T(8,128)(2,1)}, bf16[1584,768]{1,0:T(8,128)(2,1)}, u32[]{:S(2)}, u32[]{:S(2)}) collective-permute-start(bf16[1584,768]{1,0:T(8,128)(2,1)} %add_convert_fusion.3), channel_id=1, source_target_pairs={{0,1},{1,2},{2,3},{3,0},{4,5},{5,6},{6,7},{7,4},{8,9},{9,10},{10,1... | collective-permute-start | bytes 7299080 | tf_op jit(solution)/shard_map/ppermute | solution.py:1151
  411.1 37.3 %copy-start.5 = (bf16[1584,768]{1,0:T(8,128)(2,1)S(1)}, bf16[1584,768]{1,0:T(8,128)(2,1)}, u32[]{:S(2)}) copy-start(bf16[1584,768]{1,0:T(8,128)(2,1)} %get-tuple-element.435) | copy-start | bytes 7299076
  448.4 4.6 copy-start.15
  448.4 9.1 %collective-permute-start.5 = (bf16[9,4,96,768]{3,2,1,0:T(8,128)(2,1)}, bf16[9,4,96,768]{3,2,1,0:T(8,128)(2,1)}, u32[]{:S(2)}, u32[]{:S(2)}) collective-permute-start(bf16[9,4,96,768]{3,2,1,0:T(8,128)(2,1)} %get-tuple-element.428), channel_id=1, source_target_pairs={{0,4},{4,0},{1,5},{5,1},{2,6},{6,2},{3,7},{7,3},{8,12},{12,8},{9,1... | collective-permute-start | bytes 15925256 | tf_op jit(solution)/shard_map/ppermute | solution.py:671
  452.2 57.4 %collective-permute-start.6 = (bf16[1584,768]{1,0:T(8,128)(2,1)}, bf16[1584,768]{1,0:T(8,128)(2,1)S(1)}, u32[]{:S(2)}, u32[]{:S(2)}) collective-permute-start(bf16[1584,768]{1,0:T(8,128)(2,1)} %add_convert_fusion.2), channel_id=1, source_target_pairs={{0,1},{1,2},{2,3},{3,0},{4,5},{5,6},{6,7},{7,4},{8,9},{9,10},{10,1... | collective-permute-start | bytes 7299080 | tf_op jit(solution)/shard_map/ppermute | solution.py:1151
  467.1 52.9 %collective-permute-start.7 = (bf16[9,96,768]{2,1,0:T(8,128)(2,1)}, bf16[9,96,768]{2,1,0:T(8,128)(2,1)}, u32[]{:S(2)}, u32[]{:S(2)}) collective-permute-start(bf16[9,96,768]{2,1,0:T(8,128)(2,1)} %get-tuple-element.551), channel_id=1, source_target_pairs={{0,8},{8,0},{16,24},{24,16},{1,9},{9,1},{17,25},{25,17},{2,10},{10... | collective-permute-start | bytes 3981320 | tf_op jit(solution)/shard_map/ppermute | solution.py:662
  467.7 59.6 %collective-permute-start.8 = (bf16[9,96,768]{2,1,0:T(8,128)(2,1)}, bf16[9,96,768]{2,1,0:T(8,128)(2,1)}, u32[]{:S(2)}, u32[]{:S(2)}) collective-permute-start(bf16[9,96,768]{2,1,0:T(8,128)(2,1)} %get-tuple-element.553), channel_id=1, source_target_pairs={{0,16},{8,24},{16,0},{24,8},{1,17},{9,25},{17,1},{25,9},{2,18},{10... | collective-permute-start | bytes 3981320 | tf_op jit(solution)/shard_map/ppermute | solution.py:662
  468.2 59.1 %collective-permute-start.9 = (bf16[9,96,768]{2,1,0:T(8,128)(2,1)}, bf16[9,96,768]{2,1,0:T(8,128)(2,1)}, u32[]{:S(2)}, u32[]{:S(2)}) collective-permute-start(bf16[9,96,768]{2,1,0:T(8,128)(2,1)} %get-tuple-element.552), channel_id=1, source_target_pairs={{0,24},{8,16},{16,8},{24,0},{1,25},{9,17},{17,9},{25,1},{2,26},{10... | collective-permute-start | bytes 3981320 | tf_op jit(solution)/shard_map/ppermute | solution.py:662
  509.5 10.5 %copy-start.4 = (bf16[1584,768]{1,0:T(8,128)(2,1)}, bf16[1584,768]{1,0:T(8,128)(2,1)S(1)}, u32[]{:S(2)}) copy-start(bf16[1584,768]{1,0:T(8,128)(2,1)S(1)} %collective-permute-done.6.moved_ref) | copy-start | bytes 7299076
  520.0 10.5 %copy-start.18 = (s32[1024]{0:T(1024)S(1)}, s32[1024]{0:T(1024)}, u32[]{:S(2)}) copy-start(s32[1024]{0:T(1024)} %copy-done.17) | copy-start | bytes 12292
  536.5 84.5 %all-to-all-start.8 = ((bf16[32,40,768]{2,1,0:T(8,128)(2,1)}), bf16[32,40,768]{2,1,0:T(8,128)(2,1)}, u32[]{:S(2)}, u32[]{:S(2)}) async-start(bf16[32,40,768]{2,1,0:T(8,128)(2,1)} %bitcast.137), calls=%async_computation.8 | async-start | bytes 3932160 | tf_op jit(solution)/shard_map/all_to_all | solution.py:757
  540.0 58.6 %reduce-scatter.4.cloned.1.call-start = ((), (), s32[]{:S(2)}) async-start(), calls=%async_computation.14 | async-start | bytes 1658880
  552.1 6.5 copy-start.8
  554.0 2.1 collective-permute-start.10
  554.2 2.8 collective-permute-start.11
  554.6 3.2 collective-permute-start.12
  554.7 3.9 collective-permute-start.13
  559.3 4.6 copy-start.14
  560.5 19.3 %collective-permute-start.14 = (bf16[4,96,768]{2,1,0:T(8,128)(2,1)}, bf16[4,96,768]{2,1,0:T(8,128)(2,1)S(1)}, u32[]{:S(2)}, u32[]{:S(2)}) collective-permute-start(bf16[4,96,768]{2,1,0:T(8,128)(2,1)} %get-tuple-element.556), channel_id=1, source_target_pairs={{0,8},{8,0},{16,24},{24,16},{1,9},{9,1},{17,25},{25,17},{2,10},{10... | collective-permute-start | bytes 1769480 | tf_op jit(solution)/shard_map/ppermute | solution.py:662
  562.1 17.7 %collective-permute-start.15 = (bf16[4,96,768]{2,1,0:T(8,128)(2,1)}, bf16[4,96,768]{2,1,0:T(8,128)(2,1)}, u32[]{:S(2)}, u32[]{:S(2)}) collective-permute-start(bf16[4,96,768]{2,1,0:T(8,128)(2,1)} %get-tuple-element.558), channel_id=1, source_target_pairs={{0,16},{8,24},{16,0},{24,8},{1,17},{9,25},{17,1},{25,9},{2,18},{10... | collective-permute-start | bytes 1769480 | tf_op jit(solution)/shard_map/ppermute | solution.py:662
  563.6 33.5 %collective-permute-start.16 = (bf16[4,96,768]{2,1,0:T(8,128)(2,1)S(1)}, bf16[4,96,768]{2,1,0:T(8,128)(2,1)}, u32[]{:S(2)}, u32[]{:S(2)}) collective-permute-start(bf16[4,96,768]{2,1,0:T(8,128)(2,1)S(1)} %get-tuple-element.557), channel_id=1, source_target_pairs={{0,24},{8,16},{16,8},{24,0},{1,25},{9,17},{17,9},{25,1},{2,26},{10... | collective-permute-start | bytes 1769480 | tf_op jit(solution)/shard_map/ppermute | solution.py:662
  600.7 10.5 %collective-permute-start.17 = (bf16[4,24,768]{2,1,0:T(8,128)(2,1)}, bf16[4,24,768]{2,1,0:T(8,128)(2,1)}, u32[]{:S(2)}, u32[]{:S(2)}) collective-permute-start(bf16[4,24,768]{2,1,0:T(8,128)(2,1)} %get-tuple-element.565), channel_id=1, source_target_pairs={{0,1},{1,0},{2,3},{3,2},{4,5},{5,4},{6,7},{7,6},{8,9},{9,8},{10,11... | collective-permute-start | bytes 442376 | tf_op jit(solution)/shard_map/ppermute | solution.py:662
  605.4 13.9 %collective-permute-start.18 = (bf16[4,24,768]{2,1,0:T(8,128)(2,1)}, bf16[4,24,768]{2,1,0:T(8,128)(2,1)}, u32[]{:S(2)}, u32[]{:S(2)}) collective-permute-start(bf16[4,24,768]{2,1,0:T(8,128)(2,1)} %get-tuple-element.567), channel_id=1, source_target_pairs={{0,2},{1,3},{2,0},{3,1},{4,6},{5,7},{6,4},{7,5},{8,10},{9,11},{10,... | collective-permute-start | bytes 442376 | tf_op jit(solution)/shard_map/ppermute | solution.py:662
  605.4 13.9 %collective-permute-start.19 = (bf16[4,24,768]{2,1,0:T(8,128)(2,1)}, bf16[4,24,768]{2,1,0:T(8,128)(2,1)}, u32[]{:S(2)}, u32[]{:S(2)}) collective-permute-start(bf16[4,24,768]{2,1,0:T(8,128)(2,1)} %get-tuple-element.566), channel_id=1, source_target_pairs={{0,3},{1,2},{2,1},{3,0},{4,7},{5,6},{6,5},{7,4},{8,11},{9,10},{10,... | collective-permute-start | bytes 442376 | tf_op jit(solution)/shard_map/ppermute | solution.py:662
  664.5 11.0 %all-to-all-start.10 = ((f32[32,8,128]{2,1,0:T(8,128)}), f32[32,8,128]{2,1,0:T(8,128)S(1)}, u32[]{:S(2)}, u32[]{:S(2)}) async-start(f32[32,8,128]{2,1,0:T(8,128)} %broadcast_in_dim.168), calls=%async_computation.10 | async-start | bytes 262144 | tf_op jit(solution)/shard_map/all_to_all | solution.py:1333
  (5 other events, 7.8 us)
Sparse Core Ops, SparseCore 0:
  14.4 192.2 all-gather.2
  265.8 30.4 all-gather.4
  543.1 53.4 reduce-scatter.3

commit v3 on v2

--- a/solution.py
+++ b/solution.py
@@ -1237,9 +1237,7 @@
     early = sum_in_pair(early_kept, early_given)
     grad_mixed, early, up_rows = lax.optimization_barrier((grad_mixed, early, up_rows))
     early = sum_in_plane(early)
-    *grad_parts, head_sums[-1] = lax.optimization_barrier(
-        (*attend(lengths, packed, grad_mixed), head_sums[-1])
-    )
+    grad_parts = attend(lengths, packed, grad_mixed)
     flat_grad, place_grad, sums_two = row_kernel(
         leave_kernel,
         (lengths, keeps),
@@ -1259,7 +1257,9 @@
         (n_block, seq_count),
         [pltpu.VMEM((rows, row_width), f32)],
     )
-    flat_grad, early = lax.optimization_barrier((flat_grad, early))
+    flat_grad, early, head_sums[-1] = lax.optimization_barrier(
+        (flat_grad, early, head_sums[-1])
+    )
     early = lax.psum_scatter(
         early.reshape(early.shape[0], -1, row_width), "fsdp", scatter_dimension=1, tiled=True
     ).astype(f32)

time: 703 us -> 702 us (level)
    ppermute x9, waiting for transfers between devices: 47.6 us -> 77 us  [sum_over_peers(): lax.ppermute(given, axis, [(peer, peer ^ apart) for peer in range(size)])]
    ppermute x2, waiting for transfers between devices: 45.9 us -> 17.4 us  [pass_sum(): head_sums.append(lax.ppermute(total.astype(bf16), 'fsdp', ring))]
  transfers between devices with their start and end apart: 29 -> 29, of which waited for: 21 -> 21; matrix products, arithmetic and copies ran while one was open for 10% -> 11% of each run, Pallas kernels for 27% -> 27%
where the time goes in v3:
time: 702 us; the launch traced here: 692 us
  waiting for transfers between devices  284 us (40%)
  Pallas kernels  220 us (31%)
  starting transfers between devices  58.8 us (8%)
  other arithmetic  49.4 us (7%)
  local copies, waits for them, and re-layouts  31.8 us (5%)
  between operations  16.8 us (2%)
  matrix products  16.1 us (2%)
  blocking collectives  13.4 us (2%)
    pallas_call x11, Pallas kernels, row_kernel(): pl.pallas_call(kernel, out_shape=tuple((jax.ShapeDtypeStruct(shape, kind)...  138 us
    ppermute x9, waiting for transfers between devices, sum_over_peers(): lax.ppermute(given, axis, [(peer, peer ^ apart) for peer in range(size)])  77 us
    ppermute x1, waiting for transfers between devices, on_device(): tables = [first_table, lax.ppermute(first_table, 'fsdp', ring)]  58.1 us
    all_to_all x1, waiting for transfers between devices, ask_rows(): lax.all_to_all(rows.reshape(n_dev, room, -1), axes, split_axis=0, concat_...  42.4 us
    pallas_call x2, Pallas kernels, head_products(): pl.pallas_call(functools.partial(head_kernel, steps), out_shape=(jax.Shap...  39.6 us
    pallas_call x1, Pallas kernels, parcels_of(): pl.pallas_call(functools.partial(parcel_kernel, own_rows, tiles, wide), o...  24.3 us
    all_to_all x1, waiting for transfers between devices, on_device(): lax.all_to_all(targets.reshape(n_dp, n_fs, n_pick, lanes), SPLIT, split_a...  24.2 us
    ppermute x2, waiting for transfers between devices, pass_table(): tables.append(lax.ppermute(newest, 'fsdp', ring))  20.5 us
  transfers between devices with their start and end apart: 29, of which 21 were waited for; matrix products, arithmetic and copies ran while one was open for 11% of the time, Pallas kernels for 27%

profile of v3, /device:TPU:0, one launch (start us, length us, event | category | flops | bytes accessed | tf_op | source)
XLA Modules:
  0.0 691.9 jit_solution(12153513074883144926)
XLA Ops:
  21.2 7.3 %all-to-all-start.4 = ((s32[32,1,128]{2,1,0:T(1,128)}), s32[32,1,128]{2,1,0:T(1,128)S(1)}, u32[]{:S(2)}, u32[]{:S(2)}) async-start(s32[32,1,128]{2,1,0:T(1,128)} %bitcast.8), calls=%async_computation.4 | async-start | bytes 32768 | tf_op jit(solution)/shard_map/all_to_all | solution.py:718
  28.5 7.1 %multiply_reduce_fusion = (f32[]{:T(128)}, bf16[1572,768]{1,0:T(8,128)(2,1)}) fusion(f32[1572,768]{1,0:T(8,128)} %refs_0_.3), kind=kLoop, calls=%fused_computation.35 | loop fusion | flops 3621887 | bytes 7243780 | tf_op jit(solution)/shard_map/reduce_sum | solution.py:999
  35.9 6.9 %fusion.17 = bf16[1280,768]{1,0:T(8,128)(2,1)} fusion(bf16[1572,768]{1,0:T(8,128)(2,1)} %get-tuple-element.721, s32[1280]{0:T(1024)S(1)} %eq.297), kind=kOutput, calls=%fused_computation.43 | convolution fusion | flops 3093672960 | bytes 4385792 | tf_op jit(solution)/shard_map/dot_general | solution.py:36
  42.8 5.6 all-to-all-start.5
  48.5 24.3 %shard_map.450 = bf16[32,128,1664]{2,1,0:T(8,128)(2,1)} custom-call(bf16[128,50304]{1,0:T(8,128)(2,1)} %bitcast.129), custom_call_target="tpu_custom_call" | custom-call | tf_op jit(solution)/shard_map/pallas_call | solution.py:581
  78.7 5.8 select_add_fusion.tile_ref
  85.3 42.4 %all-to-all-done.5 = bf16[32,40,768]{2,1,0:T(8,128)(2,1)S(1)} async-done(((bf16[32,40,768]{2,1,0:T(8,128)(2,1)}), bf16[32,40,768]{2,1,0:T(8,128)(2,1)S(1)}, u32[]{:S(2)}, u32[]{:S(2)}) %all-to-all-start.5) | async-done | bytes 1966112 | tf_op jit(solution)/shard_map/all_to_all | solution.py:726
  127.7 4.1 fusion.13
  132.7 5.6 all-to-all-start.6
  138.4 6.7 collective-permute-start
  145.1 58.1 %collective-permute-done.refs_1_ = bf16[1584,768]{1,0:T(8,128)(2,1)} collective-permute-done((bf16[1584,768]{1,0:T(8,128)(2,1)S(1)}, bf16[1584,768]{1,0:T(8,128)(2,1)}, u32[]{:S(2)}, u32[]{:S(2)}) %collective-permute-start) | collective-permute-done | bytes 2433056 | tf_op jit(solution)/shard_map/ppermute | solution.py:1003
  203.2 3.6 all-gather.3.cloned.1.call-done.place_ref.vector_ref.weight_ref.out_ref.up_ref.down_ref
  208.7 9.2 %shard_map.451 = (f32[1024,768]{1,0:T(8,128)}, f32[1024,768]{1,0:T(8,128)}, bf16[1024,768]{1,0:T(8,128)(2,1)}, bf16[1024,2304]{1,0:T(8,128)(2,1)}) custom-call(s32[2]{0:T(128)} %compare_select_fusion.2.length_ref, f32[1024,768]{1,0:T(8,128)} %get-tuple-element.391.token_ref, ...), custom_call_target="tpu_custom_call" | custom-call | tf_op jit(solution)/shard_map/pallas_call | solution.py:519
  217.9 8.8 %shard_map.452.mixed_ref = bf16[1024,768]{1,0:T(8,128)(2,1)} custom-call(s32[2]{0:T(128)} %compare_select_fusion.2.length_ref, bf16[1024,2304]{1,0:T(8,128)(2,1)} %get-tuple-element.394.query_ref.key_ref.value_ref, bf16[1024,2304]{1,0:T(8,128)(2,1)} %get-tuple-element.394.query_ref.key_ref.value_ref, ...), custom_call_target="tpu_custom_call" | custom-call | tf_op jit(solution)/shard_map/pallas_call | solution.py:170
  229.2 14.6 %shard_map.453 = (f32[1024,768]{1,0:T(8,128)}, bf16[1024,768]{1,0:T(8,128)(2,1)}, bf16[1024,3072]{1,0:T(8,128)(2,1)}, bf16[1024,3072]{1,0:T(8,128)(2,1)}, f32[10...) custom-call(s32[2]{0:T(128)} %compare_select_fusion.2.length_ref, ...), custom_call_target="tpu_custom_call" | custom-call | tf_op jit(solution)/shard_map/pallas_call | solution.py:519
  243.7 20.5 %collective-permute-done.1.refs_2_ = bf16[1584,768]{1,0:T(8,128)(2,1)S(1)} collective-permute-done((bf16[1584,768]{1,0:T(8,128)(2,1)}, bf16[1584,768]{1,0:T(8,128)(2,1)S(1)}, u32[]{:S(2)}, u32[]{:S(2)}) %collective-permute-start.1) | collective-permute-done | bytes 2433056 | tf_op jit(solution)/shard_map/ppermute | solution.py:1012
  266.5 24.2 %all-to-all-done.6.target_ref = bf16[8,4,128,1664]{3,2,1,0:T(8,128)(2,1)} async-done(((bf16[8,4,128,1664]{3,2,1,0:T(8,128)(2,1)}), bf16[8,4,128,1664]{3,2,1,0:T(8,128)(2,1)}, u32[]{:S(2)}, u32[]{:S(2)}) %all-to-all-start.6) | async-done | bytes 13631520 | tf_op jit(solution)/shard_map/all_to_all | solution.py:994
  290.7 8.2 %all-gather.5.cloned.1.call-done.chosen_ref = bf16[1024,768]{1,0:T(8,128)(2,1)} async-done(((bf16[128,768]{1,0:T(8,128)(2,1)}), bf16[1024,768]{1,0:T(8,128)(2,1)}) %all-gather.5.cloned.1.call-update) | async-done | bytes 1572880 | tf_op jit(solution)/shard_map/all_gather | solution.py:1107
  298.8 25.6 %shard_map.454 = (bf16[3,1024,1584]{2,1,0:T(8,128)(2,1)}, f32[1024,768]{1,0:T(8,128)}, f32[8,1584]{1,0:T(8,128)}) custom-call(s32[3]{0:T(128)} %bitcast.164, bf16[1024,768]{1,0:T(8,128)(2,1)} %all-gather.5.cloned.1.call-done.chosen_ref, bf16[8,4,128,1664]{3,2,1,0:T(8,128)(2,1)} %all-to-all-done.6.target_ref, bf16[1584,768]{1,0:T(8,128)(2,1)} %pad.18.refs_0_, ...), custom_call_target="tpu_custom_call" | custom-call | tf_op jit(solution)/shard_map/pallas_call | solution.py:630
  324.4 6.7 shard_map.455
  331.1 4.2 collective-permute-start.2
  337.3 14.0 %shard_map.456 = (bf16[1,1024,1584]{2,1,0:T(8,128)(2,1)}, bf16[1024,768]{1,0:T(8,128)(2,1)}, f32[8,1584]{1,0:T(8,128)}) custom-call(s32[1]{0:T(128)} %slice.67.place_ref, bf16[1024,768]{1,0:T(8,128)(2,1)} %all-gather.5.cloned.1.call-done.chosen_ref, bf16[8,4,128,1664]{3,2,1,0:T(8,128)(2,1)} %all-to-all-done.6.target_ref, bf16[1584,768]{1,0:T(8,128)(2,1)} %copy-done.6, ...), custom_call_target="tpu_custom_call" | custom-call | tf_op jit(solution)/shard_map/pallas_call | solution.py:630
  351.3 3.8 all-to-all-start.7
  355.1 14.8 %shard_map.457 = (bf16[1584,768]{1,0:T(8,128)(2,1)}, bf16[1584,768]{1,0:T(8,128)(2,1)}, bf16[1584,768]{1,0:T(8,128)(2,1)}) custom-call(bf16[3,1024,1584]{2,1,0:T(8,128)(2,1)} %get-tuple-element.401.slope_ref, bf16[1,1024,1584]{2,1,0:T(8,128)(2,1)} %get-tuple-element.407.last_ref, bf16[1024,768]{1,0:T(8,128)(2,1)} %all-gather.5.cloned.1.call-done.chosen_ref), custom_call_target="tpu_custom_call" | custom-call | tf_op jit(solution)/shard_map/pallas_call | solution.py:519
  370.0 6.1 all-to-all-done.7.head_ref
  376.1 12.1 %collective-permute-done.2 = bf16[1584,768]{1,0:T(8,128)(2,1)} collective-permute-done((bf16[1584,768]{1,0:T(8,128)(2,1)}, bf16[1584,768]{1,0:T(8,128)(2,1)}, u32[]{:S(2)}, u32[]{:S(2)}) %collective-permute-start.2) | collective-permute-done | bytes 2433056 | tf_op jit(solution)/shard_map/ppermute | solution.py:1125
  388.2 4.5 add_convert_fusion.3
  395.5 16.5 %shard_map.458 = (f32[1024,768]{1,0:T(8,128)}, f32[1024,768]{1,0:T(8,128)}, bf16[1024,768]{1,0:T(8,128)(2,1)}, bf16[1024,768]{1,0:T(8,128)(2,1)}, bf16[1024,768]...) custom-call(s32[2]{0:T(128)} %compare_select_fusion.2.length_ref, ...), custom_call_target="tpu_custom_call" | custom-call | tf_op jit(solution)/shard_map/pallas_call | solution.py:519
  412.0 20.0 %shard_map.459 = (bf16[9,4,96,768]{3,2,1,0:T(8,128)(2,1)}, bf16[9,4,96,768]{3,2,1,0:T(8,128)(2,1)}) custom-call(s32[1]{0:T(128)} %bitcast.22.member_ref, bf16[1024,768]{1,0:T(8,128)(2,1)} %shard_map.452.mixed_ref, bf16[1024,768]{1,0:T(8,128)(2,1)} %get-tuple-element.417.attention_ref, bf16[1024,768]{1,0:T(8,128)(2,1)} %get-tuple-element.418.normed_ref, ...), custom_call_target="tpu_custom_call" | custom-call | tf_op jit(solution)/shard_map/pallas_call | solution.py:519
  432.0 17.4 %collective-permute-done.4 = bf16[1584,768]{1,0:T(8,128)(2,1)} collective-permute-done((bf16[1584,768]{1,0:T(8,128)(2,1)}, bf16[1584,768]{1,0:T(8,128)(2,1)}, u32[]{:S(2)}, u32[]{:S(2)}) %collective-permute-start.4) | collective-permute-done | bytes 2433056 | tf_op jit(solution)/shard_map/ppermute | solution.py:1151
  449.9 3.9 add_convert_fusion.2
  454.6 3.9 collective-permute-done.5
  458.5 4.4 add_convert_fusion.1
  469.6 9.9 %shard_map.460 = (bf16[1024,768]{1,0:T(8,128)(2,1)}, bf16[1024,768]{1,0:T(8,128)(2,1)}, bf16[1024,768]{1,0:T(8,128)(2,1)}) custom-call(s32[2]{0:T(128)} %compare_select_fusion.2.length_ref, bf16[1024,2304]{1,0:T(8,128)(2,1)} %get-tuple-element.394.query_ref.key_ref.value_ref, bf16[1024,2304]{1,0:T(8,128)(2,1)} %get-tuple-element.394.query_ref.key_ref.value_ref, ...), custom_call_target="tpu_custom_call" | custom-call | tf_op jit(solution)/shard_map/pallas_call | solution.py:170
  479.5 10.4 %shard_map.461 = (bf16[1024,768]{1,0:T(8,128)(2,1)}, bf16[768,512]{1,0:T(8,128)(2,1)}, f32[4,8,768]{2,1,0:T(8,128)}) custom-call(s32[2]{0:T(128)} %compare_select_fusion.2.length_ref, s32[2]{0:T(128)} %compare_convert_fusion.keep_ref, bf16[1024,768]{1,0:T(8,128)(2,1)} %get-tuple-element.442.query_ref, bf16[1024,768]{1,0:T(8,128)(2,1)} %get-tuple-element.443.key_ref, ...), custom_call_target="tpu_custom_call" | custom-call | tf_op jit(solution)/shard_map/pallas_call | solution.py:519
  489.9 8.0 %collective-permute-done.6 = bf16[9,96,768]{2,1,0:T(8,128)(2,1)} collective-permute-done((bf16[9,96,768]{2,1,0:T(8,128)(2,1)}, bf16[9,96,768]{2,1,0:T(8,128)(2,1)}, u32[]{:S(2)}, u32[]{:S(2)}) %collective-permute-start.6) | collective-permute-done | bytes 1327136 | tf_op jit(solution)/shard_map/ppermute | solution.py:662
  497.9 28.6 %collective-permute-done.7 = bf16[9,96,768]{2,1,0:T(8,128)(2,1)} collective-permute-done((bf16[9,96,768]{2,1,0:T(8,128)(2,1)S(1)}, bf16[9,96,768]{2,1,0:T(8,128)(2,1)}, u32[]{:S(2)}, u32[]{:S(2)}) %collective-permute-start.7) | collective-permute-done | bytes 1327136 | tf_op jit(solution)/shard_map/ppermute | solution.py:662
  529.8 5.1 fusion.18
  542.2 9.1 %shard_map.462 = (bf16[4,4,96,768]{3,2,1,0:T(8,128)(2,1)}, bf16[4,4,96,768]{3,2,1,0:T(8,128)(2,1)}) custom-call(s32[1]{0:T(128)} %bitcast.22.member_ref, bf16[1024,768]{1,0:T(8,128)(2,1)} %get-tuple-element.441.low_ref, bf16[1024,768]{1,0:T(8,128)(2,1)} %get-tuple-element.442.query_ref, bf16[1024,768]{1,0:T(8,128)(2,1)} %get-tuple-element.443.key_ref, ...), custom_call_target="tpu_custom_call" | custom-call | tf_op jit(solution)/shard_map/pallas_call | solution.py:519
  563.9 15.1 %collective-permute-done.14 = bf16[4,96,768]{2,1,0:T(8,128)(2,1)S(1)} collective-permute-done((bf16[4,96,768]{2,1,0:T(8,128)(2,1)}, bf16[4,96,768]{2,1,0:T(8,128)(2,1)S(1)}, u32[]{:S(2)}, u32[]{:S(2)}) %collective-permute-start.14) | collective-permute-done | bytes 589856 | tf_op jit(solution)/shard_map/ppermute | solution.py:662
  579.0 17.2 %collective-permute-done.16 = bf16[4,96,768]{2,1,0:T(8,128)(2,1)} collective-permute-done((bf16[4,96,768]{2,1,0:T(8,128)(2,1)S(1)}, bf16[4,96,768]{2,1,0:T(8,128)(2,1)}, u32[]{:S(2)}, u32[]{:S(2)}) %collective-permute-start.16) | collective-permute-done | bytes 589856 | tf_op jit(solution)/shard_map/ppermute | solution.py:662
  599.9 4.7 collective-permute-start.17
  610.4 8.0 %collective-permute-done.18 = bf16[4,24,768]{2,1,0:T(8,128)(2,1)} collective-permute-done((bf16[4,24,768]{2,1,0:T(8,128)(2,1)}, bf16[4,24,768]{2,1,0:T(8,128)(2,1)}, u32[]{:S(2)}, u32[]{:S(2)}) %collective-permute-start.18) | collective-permute-done | bytes 147488 | tf_op jit(solution)/shard_map/ppermute | solution.py:662
  620.2 9.0 %shard_map.463 = (f32[1572,768]{1,0:T(8,128)}, f32[24,512]{1,0:T(8,128)}, f32[24,2304]{1,0:T(8,128)}, f32[14,24]{1,0:T(8,128)}, f32[8,128]{1,0:T(8,128)}) custom-call(s32[1,1280]{1,0:T(1,128)} %reshape_reshape.7.wanted_ref, bf16[1280,768]{1,0:T(8,128)(2,1)} %bitcast.30.returned_ref, bf16[1584,768]{1,0:T(8,128)(2,1)} %collective-permute-done.9.moved_ref, ...), custom_call_target="tpu_custom_call" | custom-call | tf_op jit(solution)/shard_map/pallas_call | solution.py:519
  630.0 13.4 %all_to_all.71.every_ref = f32[32,8,128]{2,1,0:T(8,128)} all-to-all(f32[32,8,128]{2,1,0:T(8,128)S(1)} %broadcast_in_dim.167), channel_id=1, replica_groups=mesh['plane'=4,'pair'=2,'fsdp'=4] {'plane','pair','fsdp'}, dimensions={0} | all-to-all | bytes 262144 | tf_op jit(solution)/shard_map/all_to_all | solution.py:1333
  643.4 19.0 %shard_map.464 = (f32[1572,768]{1,0:T(8,128)}, f32[24,512]{1,0:T(8,128)}, f32[24,2304]{1,0:T(8,128)}, f32[24,768]{1,0:T(8,128)}, f32[24,3072]{1,0:T(8,128)}, /*i...) custom-call(f32[32,8,128]{2,1,0:T(8,128)} %all_to_all.71.every_ref, ...), custom_call_target="tpu_custom_call" | custom-call | tf_op jit(solution)/shard_map/pallas_call | solution.py:519
  668.4 6.3 all-to-all-done.10.every_ref
  675.3 8.3 %shard_map.465 = (f32[1572,768]{1,0:T(8,128)}, f32[24,512]{1,0:T(8,128)}, f32[24,2304]{1,0:T(8,128)}, f32[24,768]{1,0:T(8,128)}, f32[24,3072]{1,0:T(8,128)}, /*i...) custom-call(f32[32,8,128]{2,1,0:T(8,128)} %copy-done.12, f32[8,128]{1,0:T(8,128)} %get-tuple-element.468.total_ref, ...), custom_call_target="tpu_custom_call" | custom-call | tf_op jit(solution)/shard_map/pallas_call | solution.py:519
  (170 shorter events, 82.0 us)
Async XLA Ops:
  7.2 6.0 copy-start.4
  7.2 6.2 copy-start.9
  7.2 6.2 copy-start.10
  7.2 7.1 %copy-start.19 = (s32[2,512]{1,0:T(2,128)S(1)}, s32[2,512]{1,0:T(2,128)}, u32[]{:S(2)}) copy-start(s32[2,512]{1,0:T(2,128)} %param.31) | copy-start | bytes 12292
  7.2 7.1 %copy-start.16 = (s32[2,512]{1,0:T(2,128)S(1)}, s32[2,512]{1,0:T(2,128)}, u32[]{:S(2)}) copy-start(s32[2,512]{1,0:T(2,128)} %param.32) | copy-start | bytes 12292
  7.3 199.5 %all-gather.3.cloned.1.call-start = ((), (), s32[]{:S(2)}) async-start(), calls=%async_computation.12 | async-start | bytes 15611904 | tf_op jit(solution)/shard_map/all_gather | solution.py:983
  19.8 107.9 %copy-start.17 = (s32[1024]{0:T(1024)}, s32[1024]{0:T(1024)S(1)}, u32[]{:S(2)}) copy-start(s32[1024]{0:T(1024)S(1)} %add_select_fusion.4) | copy-start | bytes 12292
  21.2 14.6 %all-to-all-start.4 = ((s32[32,1,128]{2,1,0:T(1,128)}), s32[32,1,128]{2,1,0:T(1,128)S(1)}, u32[]{:S(2)}, u32[]{:S(2)}) async-start(s32[32,1,128]{2,1,0:T(1,128)} %bitcast.8), calls=%async_computation.4 | async-start | bytes 32768 | tf_op jit(solution)/shard_map/all_to_all | solution.py:718
  35.8 48.8 %copy-start.13 = (s32[32,1,128]{2,1,0:T(1,128)}, s32[32,1,128]{2,1,0:T(1,128)S(1)}, u32[]{:S(2)}) copy-start(s32[32,1,128]{2,1,0:T(1,128)S(1)} %all-to-all-done.4) | copy-start | bytes 49156
  42.8 84.8 %all-to-all-start.5 = ((bf16[32,40,768]{2,1,0:T(8,128)(2,1)}), bf16[32,40,768]{2,1,0:T(8,128)(2,1)S(1)}, u32[]{:S(2)}, u32[]{:S(2)}) async-start(bf16[32,40,768]{2,1,0:T(8,128)(2,1)} %bitcast.139), calls=%async_computation.5 | async-start | bytes 3932160 | tf_op jit(solution)/shard_map/all_to_all | solution.py:726
  132.7 5.7 copy-start.1
  132.7 74.7 %copy-start.21 = (s32[2,64]{1,0:T(2,128)S(1)}, s32[2,64]{1,0:T(2,128)}, u32[]{:S(2)}) copy-start(s32[2,64]{1,0:T(2,128)} %param.34) | copy-start | bytes 1540
  132.7 75.5 %copy-start.23 = (s32[2]{0:T(128)S(1)}, s32[2]{0:T(128)}, u32[]{:S(2)}) copy-start(s32[2]{0:T(128)} %param.33) | copy-start | bytes 28
  132.7 157.9 %all-to-all-start.6 = ((bf16[8,4,128,1664]{3,2,1,0:T(8,128)(2,1)}), bf16[8,4,128,1664]{3,2,1,0:T(8,128)(2,1)}, u32[]{:S(2)}, u32[]{:S(2)}) async-start(bf16[8,4,128,1664]{3,2,1,0:T(8,128)(2,1)} %bitcast.125), calls=%async_computation.6 | async-start | bytes 27262976 | tf_op jit(solution)/shard_map/all_to_all | solution.py:994
  138.3 160.5 %all-gather.5.cloned.1.call-start = ((), (), s32[]{:S(2)}) async-start(), calls=%async_computation.13 | async-start | bytes 1769472 | tf_op jit(solution)/shard_map/all_gather | solution.py:1107
  138.4 64.8 %collective-permute-start = (bf16[1584,768]{1,0:T(8,128)(2,1)S(1)}, bf16[1584,768]{1,0:T(8,128)(2,1)}, u32[]{:S(2)}, u32[]{:S(2)}) collective-permute-start(bf16[1584,768]{1,0:T(8,128)(2,1)S(1)} %copy-done.1), channel_id=1, source_target_pairs={{0,1},{1,2},{2,3},{3,0},{4,5},{5,6},{6,7},{7,4},{8,9},{9,10},{10,1... | collective-permute-start | bytes 7299080 | tf_op jit(solution)/shard_map/ppermute | solution.py:1003
  206.8 57.5 %collective-permute-start.1 = (bf16[1584,768]{1,0:T(8,128)(2,1)}, bf16[1584,768]{1,0:T(8,128)(2,1)S(1)}, u32[]{:S(2)}, u32[]{:S(2)}) collective-permute-start(bf16[1584,768]{1,0:T(8,128)(2,1)} %collective-permute-done.refs_1_), channel_id=1, source_target_pairs={{0,1},{1,2},{2,3},{3,0},{4,5},{5,6},{6,7},{7,4},{8,9},{9,10},{10,1... | collective-permute-start | bytes 7299080 | tf_op jit(solution)/shard_map/ppermute | solution.py:1012
  207.4 10.5 %copy-start.20 = (s32[2]{0:T(128)}, s32[2]{0:T(128)S(1)}, u32[]{:S(2)}) copy-start(s32[2]{0:T(128)S(1)} %reduce_sum.103.true_ref) | copy-start | bytes 28
  265.7 70.2 %collective-permute-start.3 = (bf16[1584,768]{1,0:T(8,128)(2,1)}, bf16[1584,768]{1,0:T(8,128)(2,1)S(1)}, u32[]{:S(2)}, u32[]{:S(2)}) collective-permute-start(bf16[1584,768]{1,0:T(8,128)(2,1)} %copy-done.7), channel_id=1, source_target_pairs={{0,1},{1,2},{2,3},{3,0},{4,5},{5,6},{6,7},{7,4},{8,9},{9,10},{10,1... | collective-permute-start | bytes 7299080 | tf_op jit(solution)/shard_map/ppermute | solution.py:1012
  324.4 10.9 %copy-start.22 = (s32[4]{0:T(128)S(1)}, s32[4]{0:T(128)}, u32[]{:S(2)}) copy-start(s32[4]{0:T(128)} %compare_select_fusion) | copy-start | bytes 52
  331.1 57.1 %collective-permute-start.2 = (bf16[1584,768]{1,0:T(8,128)(2,1)}, bf16[1584,768]{1,0:T(8,128)(2,1)}, u32[]{:S(2)}, u32[]{:S(2)}) collective-permute-start(bf16[1584,768]{1,0:T(8,128)(2,1)} %shard_map.455), channel_id=1, source_target_pairs={{0,1},{1,2},{2,3},{3,0},{4,5},{5,6},{6,7},{7,4},{8,9},{9,10},{10,1... | collective-permute-start | bytes 7299080 | tf_op jit(solution)/shard_map/ppermute | solution.py:1125
  351.3 24.8 %all-to-all-start.7 = ((bf16[8,128,768]{2,1,0:T(8,128)(2,1)}), bf16[8,128,768]{2,1,0:T(8,128)(2,1)S(1)}, u32[]{:S(2)}, u32[]{:S(2)}) async-start(bf16[8,128,768]{2,1,0:T(8,128)(2,1)} %bitcast.143), calls=%async_computation.7 | async-start | bytes 3145728 | tf_op jit(solution)/shard_map/all_to_all | solution.py:1127
  376.1 16.6 %copy-start.2 = (bf16[8,128,768]{2,1,0:T(8,128)(2,1)}, bf16[8,128,768]{2,1,0:T(8,128)(2,1)S(1)}, u32[]{:S(2)}) copy-start(bf16[8,128,768]{2,1,0:T(8,128)(2,1)S(1)} %all-to-all-done.7.head_ref) | copy-start | bytes 4718596
  392.7 56.7 %collective-permute-start.4 = (bf16[1584,768]{1,0:T(8,128)(2,1)}, bf16[1584,768]{1,0:T(8,128)(2,1)}, u32[]{:S(2)}, u32[]{:S(2)}) collective-permute-start(bf16[1584,768]{1,0:T(8,128)(2,1)} %add_convert_fusion.3), channel_id=1, source_target_pairs={{0,1},{1,2},{2,3},{3,0},{4,5},{5,6},{6,7},{7,4},{8,9},{9,10},{10,1... | collective-permute-start | bytes 7299080 | tf_op jit(solution)/shard_map/ppermute | solution.py:1151
  412.0 37.4 %copy-start.15 = (f32[8,3072]{1,0:T(8,128)S(1)}, f32[8,3072]{1,0:T(8,128)}, u32[]{:S(2)}) copy-start(f32[8,3072]{1,0:T(8,128)} %get-tuple-element.426) | copy-start | bytes 294916
  412.0 37.9 %copy-start.5 = (bf16[1584,768]{1,0:T(8,128)(2,1)S(1)}, bf16[1584,768]{1,0:T(8,128)(2,1)}, u32[]{:S(2)}) copy-start(bf16[1584,768]{1,0:T(8,128)(2,1)} %get-tuple-element.437) | copy-start | bytes 7299076
  449.4 9.1 %collective-permute-start.5 = (bf16[9,4,96,768]{3,2,1,0:T(8,128)(2,1)}, bf16[9,4,96,768]{3,2,1,0:T(8,128)(2,1)}, u32[]{:S(2)}, u32[]{:S(2)}) collective-permute-start(bf16[9,4,96,768]{3,2,1,0:T(8,128)(2,1)} %get-tuple-element.425), channel_id=1, source_target_pairs={{0,4},{4,0},{1,5},{5,1},{2,6},{6,2},{3,7},{7,3},{8,12},{12,8},{9,1... | collective-permute-start | bytes 15925256 | tf_op jit(solution)/shard_map/ppermute | solution.py:671
  449.9 8.6 %copy-start.3 = (bf16[9,4,96,768]{3,2,1,0:T(8,128)(2,1)S(1)}, bf16[9,4,96,768]{3,2,1,0:T(8,128)(2,1)}, u32[]{:S(2)}) copy-start(bf16[9,4,96,768]{3,2,1,0:T(8,128)(2,1)} %get-tuple-element.424) | copy-start | bytes 15925252
  453.8 75.9 %collective-permute-start.9 = (bf16[1584,768]{1,0:T(8,128)(2,1)}, bf16[1584,768]{1,0:T(8,128)(2,1)}, u32[]{:S(2)}, u32[]{:S(2)}) collective-permute-start(bf16[1584,768]{1,0:T(8,128)(2,1)} %add_convert_fusion.2), channel_id=1, source_target_pairs={{0,1},{1,2},{2,3},{3,0},{4,5},{5,6},{6,7},{7,4},{8,9},{9,10},{10,1... | collective-permute-start | bytes 7299080 | tf_op jit(solution)/shard_map/ppermute | solution.py:1151
  465.6 32.3 %collective-permute-start.6 = (bf16[9,96,768]{2,1,0:T(8,128)(2,1)}, bf16[9,96,768]{2,1,0:T(8,128)(2,1)}, u32[]{:S(2)}, u32[]{:S(2)}) collective-permute-start(bf16[9,96,768]{2,1,0:T(8,128)(2,1)} %get-tuple-element.545), channel_id=1, source_target_pairs={{0,8},{8,0},{16,24},{24,16},{1,9},{9,1},{17,25},{25,17},{2,10},{10... | collective-permute-start | bytes 3981320 | tf_op jit(solution)/shard_map/ppermute | solution.py:662
  467.1 59.4 %collective-permute-start.7 = (bf16[9,96,768]{2,1,0:T(8,128)(2,1)S(1)}, bf16[9,96,768]{2,1,0:T(8,128)(2,1)}, u32[]{:S(2)}, u32[]{:S(2)}) collective-permute-start(bf16[9,96,768]{2,1,0:T(8,128)(2,1)S(1)} %get-tuple-element.547), channel_id=1, source_target_pairs={{0,16},{8,24},{16,0},{24,8},{1,17},{9,25},{17,1},{25,9},{2,18},{10... | collective-permute-start | bytes 3981320 | tf_op jit(solution)/shard_map/ppermute | solution.py:662
  467.6 58.9 %collective-permute-start.8 = (bf16[9,96,768]{2,1,0:T(8,128)(2,1)S(1)}, bf16[9,96,768]{2,1,0:T(8,128)(2,1)}, u32[]{:S(2)}, u32[]{:S(2)}) collective-permute-start(bf16[9,96,768]{2,1,0:T(8,128)(2,1)S(1)} %get-tuple-element.546), channel_id=1, source_target_pairs={{0,24},{8,16},{16,8},{24,0},{1,25},{9,17},{17,9},{25,1},{2,26},{10... | collective-permute-start | bytes 3981320 | tf_op jit(solution)/shard_map/ppermute | solution.py:662
  489.9 39.9 %copy-start.18 = (s32[1024]{0:T(1024)S(1)}, s32[1024]{0:T(1024)}, u32[]{:S(2)}) copy-start(s32[1024]{0:T(1024)} %copy-done.17) | copy-start | bytes 12292
  535.7 84.5 %all-to-all-start.8 = ((bf16[32,40,768]{2,1,0:T(8,128)(2,1)}), bf16[32,40,768]{2,1,0:T(8,128)(2,1)}, u32[]{:S(2)}, u32[]{:S(2)}) async-start(bf16[32,40,768]{2,1,0:T(8,128)(2,1)} %bitcast.137), calls=%async_computation.8 | async-start | bytes 3932160 | tf_op jit(solution)/shard_map/all_to_all | solution.py:757
  539.2 58.6 %reduce-scatter.4.cloned.1.call-start = ((), (), s32[]{:S(2)}) async-start(), calls=%async_computation.14 | async-start | bytes 1658880
  551.3 6.5 copy-start.8
  553.2 2.1 collective-permute-start.10
  553.4 2.8 collective-permute-start.11
  553.8 3.2 collective-permute-start.12
  553.9 3.9 collective-permute-start.13
  558.5 4.6 copy-start.14
  559.7 19.3 %collective-permute-start.14 = (bf16[4,96,768]{2,1,0:T(8,128)(2,1)}, bf16[4,96,768]{2,1,0:T(8,128)(2,1)S(1)}, u32[]{:S(2)}, u32[]{:S(2)}) collective-permute-start(bf16[4,96,768]{2,1,0:T(8,128)(2,1)} %get-tuple-element.550), channel_id=1, source_target_pairs={{0,8},{8,0},{16,24},{24,16},{1,9},{9,1},{17,25},{25,17},{2,10},{10... | collective-permute-start | bytes 1769480 | tf_op jit(solution)/shard_map/ppermute | solution.py:662
  561.3 17.7 %collective-permute-start.15 = (bf16[4,96,768]{2,1,0:T(8,128)(2,1)}, bf16[4,96,768]{2,1,0:T(8,128)(2,1)}, u32[]{:S(2)}, u32[]{:S(2)}) collective-permute-start(bf16[4,96,768]{2,1,0:T(8,128)(2,1)} %get-tuple-element.552), channel_id=1, source_target_pairs={{0,16},{8,24},{16,0},{24,8},{1,17},{9,25},{17,1},{25,9},{2,18},{10... | collective-permute-start | bytes 1769480 | tf_op jit(solution)/shard_map/ppermute | solution.py:662
  562.8 33.5 %collective-permute-start.16 = (bf16[4,96,768]{2,1,0:T(8,128)(2,1)S(1)}, bf16[4,96,768]{2,1,0:T(8,128)(2,1)}, u32[]{:S(2)}, u32[]{:S(2)}) collective-permute-start(bf16[4,96,768]{2,1,0:T(8,128)(2,1)S(1)} %get-tuple-element.551), channel_id=1, source_target_pairs={{0,24},{8,16},{16,8},{24,0},{1,25},{9,17},{17,9},{25,1},{2,26},{10... | collective-permute-start | bytes 1769480 | tf_op jit(solution)/shard_map/ppermute | solution.py:662
  599.9 10.5 %collective-permute-start.17 = (bf16[4,24,768]{2,1,0:T(8,128)(2,1)}, bf16[4,24,768]{2,1,0:T(8,128)(2,1)}, u32[]{:S(2)}, u32[]{:S(2)}) collective-permute-start(bf16[4,24,768]{2,1,0:T(8,128)(2,1)} %get-tuple-element.559), channel_id=1, source_target_pairs={{0,1},{1,0},{2,3},{3,2},{4,5},{5,4},{6,7},{7,6},{8,9},{9,8},{10,11... | collective-permute-start | bytes 442376 | tf_op jit(solution)/shard_map/ppermute | solution.py:662
  604.5 13.9 %collective-permute-start.18 = (bf16[4,24,768]{2,1,0:T(8,128)(2,1)}, bf16[4,24,768]{2,1,0:T(8,128)(2,1)}, u32[]{:S(2)}, u32[]{:S(2)}) collective-permute-start(bf16[4,24,768]{2,1,0:T(8,128)(2,1)} %get-tuple-element.561), channel_id=1, source_target_pairs={{0,2},{1,3},{2,0},{3,1},{4,6},{5,7},{6,4},{7,5},{8,10},{9,11},{10,... | collective-permute-start | bytes 442376 | tf_op jit(solution)/shard_map/ppermute | solution.py:662
  604.6 13.9 %collective-permute-start.19 = (bf16[4,24,768]{2,1,0:T(8,128)(2,1)}, bf16[4,24,768]{2,1,0:T(8,128)(2,1)}, u32[]{:S(2)}, u32[]{:S(2)}) collective-permute-start(bf16[4,24,768]{2,1,0:T(8,128)(2,1)} %get-tuple-element.560), channel_id=1, source_target_pairs={{0,3},{1,2},{2,1},{3,0},{4,7},{5,6},{6,5},{7,4},{8,11},{9,10},{10,... | collective-permute-start | bytes 442376 | tf_op jit(solution)/shard_map/ppermute | solution.py:662
  663.7 11.0 %all-to-all-start.10 = ((f32[32,8,128]{2,1,0:T(8,128)}), f32[32,8,128]{2,1,0:T(8,128)S(1)}, u32[]{:S(2)}, u32[]{:S(2)}) async-start(f32[32,8,128]{2,1,0:T(8,128)} %broadcast_in_dim.168), calls=%async_computation.10 | async-start | bytes 262144 | tf_op jit(solution)/shard_map/all_to_all | solution.py:1333
  (5 other events, 7.0 us)
Sparse Core Ops, SparseCore 0:
  14.4 192.2 all-gather.2
  265.8 32.9 all-gather.4
  542.3 53.4 reduce-scatter.3
